TPU v7x, 32 devices: a whole 2x2x4 slice. The times are simulated.
32 devices in a mesh: tm: 16 (over z, x, core), space: 2 (over y).
Axes of the slice: x: 2, y: 2, z: 4, core: 2. Of those that a mesh axis runs over, the one named last changes fastest.
Arguments:
- field: float32 [256, 64, 2048], P('tm', 'space'), may hold values from -3 to 3
- step: float32 [1], replicated, may hold values from 9.9e-05 to 0.001
- mass: float32 [1], replicated, may hold values from 0.02 to 0.05
Outputs:
- field_out: float32 [256, 64, 2048], P('tm', 'space')
All inputs are finite; a program needn't handle non-finite values.
Results may differ from a plain program's by a relative error of at most 0.0001.
Values sent between devices are 32-bit elements; how exact they have to be, the bound alone decides.
No kernel may reach another device: no remote copies, remote signals or barrier semaphores. Data moves between devices by JAX's collectives and lax.ppermute only.
A program may use at most 64 MiB of HBM per device.

v0:
```python
import jax
import jax.numpy as jnp
from jax import lax
from jax.sharding import PartitionSpec as P

NZ = 32
ITERS = 2


HIGH = lax.Precision.HIGHEST


def with_halo(shard, sides, width, wrap):
    for axis, dim in sides:
        devices, length = (lax.axis_size(axis), shard.shape[dim])
        up = [(i, (i + 1) % devices) for i in range(devices if wrap else devices - 1)]
        down = [(j, i) for i, j in up]
        last = lax.slice_in_dim(shard, length - width, length, axis=dim)
        leading = lax.slice_in_dim(shard, 0, width, axis=dim)
        before = lax.ppermute(last, axis, up)
        after = lax.ppermute(leading, axis, down)
        shard = jnp.concatenate([before, shard, after], axis=dim)
    return shard


def local_terms(flat, depth):
    width = flat.shape[-1]
    column = lax.broadcasted_iota(jnp.int32, (width,), 0)
    zplace = column % depth
    padded = jnp.pad(flat, ((0, 0), (0, 0), (depth, depth)))
    total = padded[:, :, 2 * depth :] + padded[:, :, :width]
    upper = padded[:, :, depth + 1 : depth + 1 + width]
    lower = padded[:, :, depth - 1 : depth - 1 + width]
    total = total + jnp.where(zplace == depth - 1, 0.0, upper) + jnp.where(zplace == 0, 0.0, lower)
    return total - 8.0 * flat


def on_device(field, step, mass):
    slices = field.shape[0]
    depth = NZ
    flat = field
    total_t = slices * lax.axis_size("tm")
    wave = lax.broadcasted_iota(jnp.int32, (total_t, total_t), 0)
    times = lax.broadcasted_iota(jnp.int32, (total_t, total_t), 1)
    angle = 2.0 * jnp.pi / total_t * (wave * times % total_t).astype(jnp.float32)
    cosines = jnp.cos(angle)
    sines = jnp.sin(angle)
    freq = jnp.arange(total_t).astype(jnp.float32)
    inverse = 1.0 / (mass[0] * mass[0] + 4.0 * jnp.sin(jnp.pi * freq / total_t) ** 2)
    operator = (
        jnp.dot(cosines * inverse[None, :], cosines, precision=HIGH)
        + jnp.dot(sines * inverse[None, :], sines, precision=HIGH)
    ) / total_t
    for turn in range(ITERS):
        padded_t = with_halo(flat, (("tm", 0),), 1, True)
        padded_x = with_halo(flat, (("space", 1),), 1, False)
        lap = (
            local_terms(flat, depth)
            + padded_t[2:]
            + padded_t[:-2]
            + padded_x[:, 2:]
            + padded_x[:, :-2]
        )
        force = -lap + flat - 0.9 * flat * flat + 0.25 * flat * flat * flat
        lines = jnp.einsum(
            "ts,sab->tab",
            operator,
            lax.all_to_all(force, "tm", split_axis=1, concat_axis=0, tiled=True),
            precision=HIGH,
        )
        update = lax.all_to_all(lines, "tm", split_axis=0, concat_axis=1, tiled=True)
        flat = flat - step[0] * update
    return flat


def solution(mesh):
    return jax.shard_map(
        on_device,
        mesh=mesh,
        in_specs=(P("tm", "space", None), P(), P()),
        out_specs=P("tm", "space", None),
        check_vma=False,
    )
```

profile of v0, /device:TPU:0, one launch (start us, length us, event | category | flops | bytes accessed | tf_op | source)
XLA Modules:
  0.0 472.8 jit_solution(12100418435675768304)
XLA Ops:
  0.0 1.1 fusion.50
  1.1 5.5 %collective-permute-start = (f32[1,32,2048]{2,1,0:T(8,128)S(1)}, f32[1,32,2048]{2,1,0:T(8,128)S(1)}, u32[]{:S(2)}, u32[]{:S(2)}) collective-permute-start(f32[1,32,2048]{2,1,0:T(8,128)S(1)} %get-tuple-element.9), channel_id=1, source_target_pairs={{2,0},{4,2},{6,4},{8,6},{10,8},{12,10},{14,12},{16,14},{18,16},{20... | collective-permute-start | bytes 786440 | tf_op jit(solution)/shard_map/ppermute | solution.py:21
  6.5 0.0 collective-permute-start.1
  6.5 4.6 copy.51
  11.2 1.3 collective-permute-start.2
  12.5 4.6 collective-permute-start.3
  17.1 0.0 collective-permute-done
  17.1 0.3 copy.35
  17.4 0.0 collective-permute-done.1
  17.4 0.3 copy.36
  17.6 0.4 collective-permute-done.2
  18.1 1.5 collective-permute-done.3
  19.6 7.8 %fusion.1 = f32[16,32,2048]{2,0,1:T(8,128)} fusion(f32[16,32,2048]{2,0,1:T(8,128)S(1)} %copy.51, f32[16,1,2048]{2,0,1:T(8,128)S(1)} %collective-permute-done.3, f32[16,1,2048]{2,0,1:T(8,128)S(1)} %collective-permute-done.2, f32[1,32,2048]{2,0,1:T(1,128)S(1)} %copy.36, f32[1,32,2048]{2,0,1:T(1,128)S(1)} %copy.35, pred[2048]{0:T(1024)(128)(4,1)S(1)} %get-tuple-element.13, ...), kind=kLoop, calls=%fused_computation.5 | loop fusion | flops 25165824 | bytes 9179136 | tf_op jit(solution)/shard_map/add | solution.py:64
  27.4 5.3 %all-to-all-start = ((f32[16,32,2048]{2,0,1:T(8,128)}), f32[16,32,2048]{2,0,1:T(8,128)}, u32[]{:S(2)}, u32[]{:S(2)}) async-start(f32[16,32,2048]{2,0,1:T(8,128)} %fusion.1), calls=%async_computation | async-start | bytes 8388608 | tf_op jit(solution)/shard_map/all_to_all | solution.py:68
  33.4 1.4 fusion.21
  34.8 1.4 fusion.19
  36.1 74.2 %all-to-all-done = f32[16,32,2048]{2,0,1:T(8,128)} async-done(((f32[16,32,2048]{2,0,1:T(8,128)}), f32[16,32,2048]{2,0,1:T(8,128)}, u32[]{:S(2)}, u32[]{:S(2)}) %all-to-all-start) | async-done | bytes 4194336 | tf_op jit(solution)/shard_map/all_to_all | solution.py:68
  110.3 2.5 copy.48
  112.8 4.1 fusion.52
  116.9 5.2 %copy.49 = f32[256,2,2048]{2,1,0:T(2,128)} copy(f32[256,2,2048]{2,0,1:T(8,128)S(1)} %fusion.52) | data formatting | bytes 8388608 | tf_op jit(solution)/shard_map/ts,sab->tab/dot_general | solution.py:65
  122.1 19.9 %all-to-all-start.1 = ((f32[256,2,2048]{2,1,0:T(2,128)}), f32[256,2,2048]{2,1,0:T(2,128)}, u32[]{:S(2)}, u32[]{:S(2)}) async-start(f32[256,2,2048]{2,1,0:T(2,128)} %copy.49), calls=%async_computation.1 | async-start | bytes 8388608 | tf_op jit(solution)/shard_map/all_to_all | solution.py:71
  142.6 77.0 %all-to-all-done.1 = f32[256,2,2048]{2,1,0:T(2,128)} async-done(((f32[256,2,2048]{2,1,0:T(2,128)}), f32[256,2,2048]{2,1,0:T(2,128)}, u32[]{:S(2)}, u32[]{:S(2)}) %all-to-all-start.1) | async-done | bytes 4194336 | tf_op jit(solution)/shard_map/all_to_all | solution.py:71
  219.6 2.5 broadcast_multiply_fusion.1
  222.1 0.0 copy-start
  222.1 3.3 copy.50
  225.5 2.7 bitcast_subtract_fusion.1
  228.1 0.4 fusion.48
  228.6 0.1 copy.52
  228.7 0.1 copy.54
  228.8 0.8 collective-permute-start.5
  229.6 17.5 %collective-permute-start.4 = (f32[1,32,2048]{2,1,0:T(8,128)S(1)}, f32[1,32,2048]{2,1,0:T(8,128)S(1)}, u32[]{:S(2)}, u32[]{:S(2)}) collective-permute-start(f32[1,32,2048]{2,1,0:T(8,128)S(1)} %copy.52), channel_id=1, source_target_pairs={{2,0},{4,2},{6,4},{8,6},{10,8},{12,10},{14,12},{16,14},{18,16},{20... | collective-permute-start | bytes 786440 | tf_op jit(solution)/shard_map/ppermute | solution.py:21
  247.1 1.3 collective-permute-start.6
  248.4 4.6 collective-permute-start.7
  253.0 0.3 copy.55
  253.2 0.0 collective-permute-done.4
  253.2 0.3 copy.53
  253.5 0.4 collective-permute-done.6
  253.9 1.5 collective-permute-done.7
  255.4 6.9 %fusion.3 = f32[16,32,2048]{2,0,1:T(8,128)S(1)} fusion(f32[16,32,2048]{2,0,1:T(8,128)S(1)} %bitcast_subtract_fusion.1, f32[16,1,2048]{2,0,1:T(8,128)S(1)} %collective-permute-done.7, f32[16,1,2048]{2,0,1:T(8,128)S(1)} %collective-permute-done.6, f32[1,32,2048]{2,0,1:T(1,128)S(1)} %copy.55, f32[1,32,2048]{2,0,1:T(1,128)S(1)} %copy.53, ...), kind=kLoop, calls=%fused_computation.7 | loop fusion | flops 25165824 | bytes 9179136 | tf_op jit(solution)/shard_map/add | solution.py:64
  262.3 95.9 %all_to_all.54 = f32[16,32,2048]{2,0,1:T(8,128)S(1)} all-to-all(f32[16,32,2048]{2,0,1:T(8,128)S(1)} %fusion.3), channel_id=1, replica_groups=mesh['tm'=16,'space'=2] {'tm'}, dimensions={1} | all-to-all | bytes 8388608 | tf_op jit(solution)/shard_map/all_to_all | solution.py:68
  358.2 0.5 copy.56
  358.7 4.1 fusion.53
  362.8 3.2 copy.57
  366.0 97.6 %all_to_all.55 = f32[256,2,2048]{2,1,0:T(2,128)S(1)} all-to-all(f32[256,2,2048]{2,1,0:T(2,128)S(1)} %copy.57), channel_id=1, replica_groups=mesh['tm'=16,'space'=2] {'tm'}, dimensions={0} | all-to-all | bytes 8388608 | tf_op jit(solution)/shard_map/all_to_all | solution.py:71
  463.6 0.3 broadcast_multiply_fusion
  463.9 3.3 copy.58
  467.2 0.9 bitcast_subtract_fusion
  468.1 4.4 copy.59
  (6 shorter events, 0.1 us)
Async XLA Ops:
  1.1 16.0 %collective-permute-start = (f32[1,32,2048]{2,1,0:T(8,128)S(1)}, f32[1,32,2048]{2,1,0:T(8,128)S(1)}, u32[]{:S(2)}, u32[]{:S(2)}) collective-permute-start(f32[1,32,2048]{2,1,0:T(8,128)S(1)} %get-tuple-element.9), channel_id=1, source_target_pairs={{2,0},{4,2},{6,4},{8,6},{10,8},{12,10},{14,12},{16,14},{18,16},{20... | collective-permute-start | bytes 786440 | tf_op jit(solution)/shard_map/ppermute | solution.py:21
  6.5 10.8 %collective-permute-start.1 = (f32[1,32,2048]{2,1,0:T(8,128)S(1)}, f32[1,32,2048]{2,1,0:T(8,128)S(1)}, u32[]{:S(2)}, u32[]{:S(2)}) collective-permute-start(f32[1,32,2048]{2,1,0:T(8,128)S(1)} %get-tuple-element.10), channel_id=1, source_target_pairs={{0,2},{2,4},{4,6},{6,8},{8,10},{10,12},{12,14},{14,16},{16,18},{18... | collective-permute-start | bytes 786440 | tf_op jit(solution)/shard_map/ppermute | solution.py:20
  11.2 6.9 %collective-permute-start.2 = (f32[16,1,2048]{2,0,1:T(8,128)S(1)}, f32[16,1,2048]{2,0,1:T(8,128)S(1)}, u32[]{:S(2)}, u32[]{:S(2)}) collective-permute-start(f32[16,1,2048]{2,0,1:T(8,128)S(1)} %get-tuple-element.11), channel_id=1, source_target_pairs={{1,0},{3,2},{5,4},{7,6},{9,8},{11,10},{13,12},{15,14},{17,16},{19,... | collective-permute-start | bytes 393224 | tf_op jit(solution)/shard_map/ppermute | solution.py:21
  12.5 7.1 %collective-permute-start.3 = (f32[16,1,2048]{2,0,1:T(8,128)S(1)}, f32[16,1,2048]{2,0,1:T(8,128)S(1)}, u32[]{:S(2)}, u32[]{:S(2)}) collective-permute-start(f32[16,1,2048]{2,0,1:T(8,128)S(1)} %get-tuple-element.12), channel_id=1, source_target_pairs={{0,1},{2,3},{4,5},{6,7},{8,9},{10,11},{12,13},{14,15},{16,17},{18,... | collective-permute-start | bytes 393224 | tf_op jit(solution)/shard_map/ppermute | solution.py:20
  27.4 82.9 %all-to-all-start = ((f32[16,32,2048]{2,0,1:T(8,128)}), f32[16,32,2048]{2,0,1:T(8,128)}, u32[]{:S(2)}, u32[]{:S(2)}) async-start(f32[16,32,2048]{2,0,1:T(8,128)} %fusion.1), calls=%async_computation | async-start | bytes 8388608 | tf_op jit(solution)/shard_map/all_to_all | solution.py:68
  122.1 97.5 %all-to-all-start.1 = ((f32[256,2,2048]{2,1,0:T(2,128)}), f32[256,2,2048]{2,1,0:T(2,128)}, u32[]{:S(2)}, u32[]{:S(2)}) async-start(f32[256,2,2048]{2,1,0:T(2,128)} %copy.49), calls=%async_computation.1 | async-start | bytes 8388608 | tf_op jit(solution)/shard_map/all_to_all | solution.py:71
  222.1 3.3 copy-start
  228.8 24.2 %collective-permute-start.5 = (f32[1,32,2048]{2,1,0:T(8,128)S(1)}, f32[1,32,2048]{2,1,0:T(8,128)S(1)}, u32[]{:S(2)}, u32[]{:S(2)}) collective-permute-start(f32[1,32,2048]{2,1,0:T(8,128)S(1)} %copy.54), channel_id=1, source_target_pairs={{0,2},{2,4},{4,6},{6,8},{8,10},{10,12},{12,14},{14,16},{16,18},{18... | collective-permute-start | bytes 786440 | tf_op jit(solution)/shard_map/ppermute | solution.py:20
  229.6 23.6 %collective-permute-start.4 = (f32[1,32,2048]{2,1,0:T(8,128)S(1)}, f32[1,32,2048]{2,1,0:T(8,128)S(1)}, u32[]{:S(2)}, u32[]{:S(2)}) collective-permute-start(f32[1,32,2048]{2,1,0:T(8,128)S(1)} %copy.52), channel_id=1, source_target_pairs={{2,0},{4,2},{6,4},{8,6},{10,8},{12,10},{14,12},{16,14},{18,16},{20... | collective-permute-start | bytes 786440 | tf_op jit(solution)/shard_map/ppermute | solution.py:21
  247.1 6.9 %collective-permute-start.6 = (f32[16,1,2048]{2,0,1:T(8,128)S(1)}, f32[16,1,2048]{2,0,1:T(8,128)S(1)}, u32[]{:S(2)}, u32[]{:S(2)}) collective-permute-start(f32[16,1,2048]{2,0,1:T(8,128)S(1)} %get-tuple-element.7), channel_id=1, source_target_pairs={{1,0},{3,2},{5,4},{7,6},{9,8},{11,10},{13,12},{15,14},{17,16},{19,... | collective-permute-start | bytes 393224 | tf_op jit(solution)/shard_map/ppermute | solution.py:21
  248.4 7.1 %collective-permute-start.7 = (f32[16,1,2048]{2,0,1:T(8,128)S(1)}, f32[16,1,2048]{2,0,1:T(8,128)S(1)}, u32[]{:S(2)}, u32[]{:S(2)}) collective-permute-start(f32[16,1,2048]{2,0,1:T(8,128)S(1)} %get-tuple-element.8), channel_id=1, source_target_pairs={{0,1},{2,3},{4,5},{6,7},{8,9},{10,11},{12,13},{14,15},{16,17},{18,... | collective-permute-start | bytes 393224 | tf_op jit(solution)/shard_map/ppermute | solution.py:20
where the time goes:
time: 478 us; the launch traced here: 473 us
  blocking collectives  193 us (40%)
  waiting for transfers between devices  155 us (32%)
  starting transfers between devices  60.6 us (13%)
  local copies, waits for them, and re-layouts  29.8 us (6%)
  other arithmetic  21.2 us (4%)
  matrix products  10.9 us (2%)
    all_to_all x1, blocking collectives, on_device(): lax.all_to_all(lines, 'tm', split_axis=0, concat_axis=1, tiled=True)  97.6 us
    all_to_all x1, blocking collectives, on_device(): lax.all_to_all(force, 'tm', split_axis=1, concat_axis=0, tiled=True)  95.9 us
    all_to_all x1, waiting for transfers between devices, on_device(): lax.all_to_all(lines, 'tm', split_axis=0, concat_axis=1, tiled=True)  77 us
    all_to_all x1, waiting for transfers between devices, on_device(): lax.all_to_all(force, 'tm', split_axis=1, concat_axis=0, tiled=True)  74.2 us
    ppermute x4, starting transfers between devices, with_halo(): after = lax.ppermute(leading, axis, down)  25.5 us
    all_to_all x1, starting transfers between devices, on_device(): lax.all_to_all(lines, 'tm', split_axis=0, concat_axis=1, tiled=True)  19.9 us
    add x2, other arithmetic, on_device(): force = -lap + flat - 0.9 * flat * flat + 0.25 * flat * flat * flat  14.7 us
    ppermute x4, starting transfers between devices, with_halo(): before = lax.ppermute(last, axis, up)  9.94 us
  transfers between devices with their start and end apart: 10, of which 6 were waited for; matrix products, arithmetic and copies ran while one was open for 2% of the time, Pallas kernels for 0%

commit v1 on v0

v1 whole, which is shorter than its diff:
```python
import jax
import jax.numpy as jnp
from jax import lax
from jax.experimental import pallas as pl
from jax.experimental.pallas import tpu as pltpu
from jax.sharding import PartitionSpec as P

NZ = 32
ITERS = 2

LANES = 128
ROWS = 8


def decay(mass):
    root = jnp.sqrt(1.0 + 0.25 * mass * mass)
    return 1.0 + 0.5 * mass * mass - mass * root, 0.5 / (mass * root)


def relax(phi, step_ref, mass_ref, psi_ref, ends_ref, tiles):
    slices, planes, _ = psi_ref.shape
    blocks = planes // ROWS
    lane = lax.broadcasted_iota(jnp.int32, (ROWS, LANES), 1)
    row = lax.broadcasted_iota(jnp.int32, (ROWS, LANES), 0)
    mass = jnp.full((ROWS, LANES), mass_ref[0], jnp.float32)
    step = jnp.full((ROWS, LANES), step_ref[0], jnp.float32)
    r, amplitude = decay(mass)
    scale = step * amplitude
    c1, c2, c3 = scale * (7.0 - mass * mass), -0.9 * scale, 0.25 * scale
    keep = 1.0 - step
    first_z, last_z = lane % NZ == 0, lane % NZ == NZ - 1
    first_row, last_row = row == 0, row == ROWS - 1
    head, tail = lane < NZ, lane >= LANES - NZ
    zero = jnp.zeros((ROWS, LANES), jnp.float32)

    def at(t, i, start):
        return phi[t, ROWS * i : ROWS * (i + 1), pl.ds(start, LANES)]

    def tile(j, carry):
        start = pl.multiple_of((j + 1) * LANES, LANES)
        out = pl.ds(pl.multiple_of(j * LANES, LANES), LANES)
        for i in range(blocks):
            force = [None] * slices
            for k in range(slices):
                t = k // 2 if k % 2 == 0 else slices - 1 - k // 2
                v = at(t, i, start)
                before = zero if i == 0 else at(t, i - 1, start)
                after = zero if i == blocks - 1 else at(t, i + 1, start)
                total = pltpu.roll(jnp.where(last_row, before, v), 1, 0)
                total = total + pltpu.roll(jnp.where(first_row, after, v), ROWS - 1, 0)
                total = total + jnp.where(first_z, 0.0, pltpu.roll(v, 1, 1))
                total = total + jnp.where(last_z, 0.0, pltpu.roll(v, LANES - 1, 1))
                total = total + pltpu.roll(jnp.where(tail, at(t, i, start - LANES), v), NZ, 1)
                total = total + pltpu.roll(jnp.where(head, at(t, i, start + LANES), v), LANES - NZ, 1)
                force[t] = v * (c1 + v * (c2 + c3 * v)) - scale * total
            forward, backward = [None] * slices, [None] * slices
            a, b = force[0], force[-1]
            forward[0], backward[-1] = None, b
            for t in range(1, slices):
                forward[t] = r * a
                a = force[t] + forward[t]
                s = slices - 1 - t
                b = force[s] + r * b
                backward[s] = b
            rows = slice(ROWS * i, ROWS * (i + 1))
            ends_ref[0, rows, out] = a
            ends_ref[1, rows, out] = b
            for t in range(slices):
                local = backward[t] if t == 0 else forward[t] + backward[t]
                psi_ref[t, rows, out] = keep * at(t, i, start) - local
        return carry

    lax.fori_loop(tiles[0], tiles[1], tile, 0)


def clear_guards(phi):
    slices, planes, width = phi.shape
    guard = jnp.zeros((slices, planes, LANES), jnp.float32)
    phi[:, :, :LANES] = guard
    phi[:, :, width - LANES :] = guard


def first_kernel(step_ref, mass_ref, field_ref, psi_ref, ends_ref, phi, sems):
    width = psi_ref.shape[-1]
    parts = sems.shape[0]
    part = width // parts
    copies = []
    for n in range(parts):
        copies.append(
            pltpu.make_async_copy(
                field_ref.at[:, :, n * part : (n + 1) * part],
                phi.at[:, :, LANES + n * part : LANES + (n + 1) * part],
                sems.at[n],
            )
        )
        copies[-1].start()
    clear_guards(phi)
    copies[0].wait()
    for n in range(parts):
        if n + 1 < parts:
            copies[n + 1].wait()
        relax(phi, step_ref, mass_ref, psi_ref, ends_ref, (n * part // LANES, (n + 1) * part // LANES))


def next_kernel(core_ref, step_ref, mass_ref, own_ref, other_ref, low_ref, high_ref, old_ref, psi_ref, ends_ref, phi):
    slices, planes, width = psi_ref.shape
    blocks = planes // ROWS
    mass = jnp.full((ROWS, LANES), mass_ref[0], jnp.float32)
    r, _ = decay(mass)
    inverse = 1.0 / r
    last = r
    for _ in range(slices - 1):
        last = last * r
    row = lax.broadcasted_iota(jnp.int32, (ROWS, LANES), 0)
    core = core_ref[0]
    clear_guards(phi)

    def tile(j, carry):
        lanes = pl.ds(pl.multiple_of(j * LANES, LANES), LANES)
        inner = pl.ds(pl.multiple_of((j + 1) * LANES, LANES), LANES)
        for i in range(blocks):
            rows = slice(ROWS * i, ROWS * (i + 1))
            half = 2 * i // blocks
            place = slice(ROWS * i - half * planes // 2, ROWS * (i + 1) - half * planes // 2)
            mine = core == half
            p = jnp.where(mine, own_ref[0, place, lanes], other_ref[0, place, lanes]) * r
            q = jnp.where(mine, own_ref[1, place, lanes], other_ref[1, place, lanes]) * last
            for t in range(slices):
                value = old_ref[t, rows, lanes] - p - q
                if i == 0:
                    value = value + jnp.where(row == 0, low_ref[t : t + 1, lanes], 0.0)
                if i == blocks - 1:
                    value = value + jnp.where(row == ROWS - 1, high_ref[t : t + 1, lanes], 0.0)
                phi[t, rows, inner] = value
                p, q = p * r, q * inverse
        return carry

    lax.fori_loop(0, width // LANES, tile, 0)
    relax(phi, step_ref, mass_ref, psi_ref, ends_ref, (0, width // LANES))


VMEM = pl.BlockSpec(memory_space=pltpu.VMEM)
SMEM = pl.BlockSpec(memory_space=pltpu.SMEM)


def outputs_of(shape):
    slices, planes, width = shape
    return dict(
        out_shape=(
            jax.ShapeDtypeStruct(shape, jnp.float32),
            jax.ShapeDtypeStruct((2, planes, width), jnp.float32),
        ),
        out_specs=(VMEM, VMEM),
        compiler_params=pltpu.CompilerParams(vmem_limit_bytes=24 * 2**20),
        cost_estimate=pl.CostEstimate(flops=30 * slices * planes * width, bytes_accessed=8 * slices * planes * width, transcendentals=0),
    )


def first_relax(field, step, mass):
    slices, planes, width = field.shape
    parts = 4 if width % (4 * LANES) == 0 else 1
    return pl.pallas_call(
        first_kernel,
        in_specs=[SMEM, SMEM, pl.BlockSpec(memory_space=pl.ANY)],
        scratch_shapes=[
            pltpu.VMEM((slices, planes, width + 2 * LANES), jnp.float32),
            pltpu.SemaphoreType.DMA((parts,)),
        ],
        **outputs_of(field.shape),
    )(step, mass, field)


def next_relax(core, step, mass, own, other, low, high, psi):
    slices, planes, width = psi.shape
    return pl.pallas_call(
        next_kernel,
        in_specs=[SMEM] * 3 + [VMEM] * 5,
        scratch_shapes=[pltpu.VMEM((slices, planes, width + 2 * LANES), jnp.float32)],
        **outputs_of(psi.shape),
    )(core, step, mass, own, other, low, high, psi)


class Loop:
    def __init__(self, mass, slices):
        self.devices = lax.axis_size("tm")
        self.me = lax.axis_index("tm")
        self.rate = 2.0 * jnp.arcsinh(0.5 * mass) * slices
        self.levels = self.devices.bit_length() - 1
        assert self.devices == 1 << self.levels

    def swap(self, array, offset):
        return lax.ppermute(array, "tm", [(i, i ^ offset) for i in range(self.devices)])

    def rho(self, level):
        return jnp.exp(-self.rate * (1 << level))

    def is_left(self, level):
        return (self.me >> level) & 1 == 0

    def merge(self, mine, theirs, level):
        left, rho = self.is_left(level), self.rho(level)
        ours, others = jnp.where(left, rho, 1.0), jnp.where(left, 1.0, rho)
        return jnp.stack([ours * mine[0] + others * theirs[0], others * mine[1] + ours * theirs[1]])

    def down(self, mine, theirs, both, level):
        left, rho = self.is_left(level), self.rho(level)
        before = jnp.where(left, both[0], theirs[0] + rho * both[0])
        after = jnp.where(left, theirs[1] + rho * both[1], both[1])
        return jnp.stack([before, after])

    def down_other(self, mine, theirs, both, level):
        left, rho = self.is_left(level), self.rho(level)
        before = jnp.where(left, mine[0] + rho * both[0], both[0])
        after = jnp.where(left, both[1], mine[1] + rho * both[1])
        return jnp.stack([before, after])

    def solve(self, ends):
        half = ends.shape[1] // 2
        bit = self.me & 1
        mine0 = lax.dynamic_slice_in_dim(ends, bit * half, half, 1)
        theirs0 = self.swap(lax.dynamic_slice_in_dim(ends, (1 - bit) * half, half, 1), 1)
        chip = self.merge(mine0, theirs0, 0)

        group = (self.me >> 1) & 3
        quarter = half // 4

        def part(k):
            return lax.dynamic_slice_in_dim(chip, (group ^ k) * quarter, quarter, 1)

        a0 = part(0)
        a1, a2, a3 = (self.swap(part(k), 2 * k) for k in (1, 2, 3))
        near, far = self.merge(a0, a1, 1), self.merge(a2, a3, 1)
        arc = self.merge(near, far, 2)
        stack = []
        for level in range(3, self.levels):
            theirs = self.swap(arc, 1 << level)
            stack.append((arc, theirs, level))
            arc = self.merge(arc, theirs, level)
        enters = arc / (1.0 - self.rho(self.levels))
        for mine, theirs, level in reversed(stack):
            enters = self.down(mine, theirs, enters, level)
        enters_near = self.down(near, far, enters, 2)
        enters_far = self.down_other(near, far, enters, 2)
        p0 = self.down(a0, a1, enters_near, 1)
        p1 = self.down_other(a0, a1, enters_near, 1)
        p2 = self.down(a2, a3, enters_far, 1)
        p3 = self.down_other(a2, a3, enters_far, 1)
        back = jnp.stack([p0] + [self.swap(p, 2 * k) for k, p in ((1, p1), (2, p2), (3, p3))])
        chip_enters = jnp.concatenate(
            [lax.dynamic_index_in_dim(back, group ^ k, 0, keepdims=False) for k in range(4)], axis=1
        )
        own = self.down(mine0, theirs0, chip_enters, 0)
        other = self.swap(self.down_other(mine0, theirs0, chip_enters, 0), 1)
        return own, other


class Planes:
    def __init__(self, planes):
        self.planes = planes
        self.devices = lax.axis_size("space")
        self.me = lax.axis_index("space")
        self.rounds = [p for p in (0, 1) if p + 1 < self.devices]

    def row(self, parity):
        return jnp.where(self.me % 2 == parity, self.planes - 1, 0)

    def exchange(self, rows):
        got = []
        for parity, given in zip(self.rounds, rows):
            low = range(parity, self.devices - 1, 2)
            got.append(lax.ppermute(given, "space", [(i, i + 1) for i in low] + [(i + 1, i) for i in low]))
        return got


def on_device(field, step, mass):
    slices, planes, width = field.shape
    loop = Loop(mass[0], slices)
    sides = Planes(planes)
    r, amplitude = decay(mass[0])
    rate = 2.0 * jnp.arcsinh(0.5 * mass[0])
    times = jnp.arange(slices).astype(jnp.float32)
    from_start = jnp.exp(-rate * times)
    from_end = from_start[::-1]
    green = step[0] * amplitude * jnp.exp(-rate * jnp.abs(times[:, None] - times[None, :]))
    weights = step[0] * amplitude * jnp.stack([from_end, from_start])
    core = (loop.me & 1).astype(jnp.int32).reshape(1)
    half = planes // 2

    def edge_terms(ends, halos):
        row = lax.broadcasted_iota(jnp.int32, (1, planes, 1), 1)
        low = high = jnp.zeros((slices, width), jnp.float32)
        for parity, halo in zip(sides.rounds, halos):
            touching = sides.row(parity)
            sums = jnp.sum(weights[:, :, None] * halo[None], axis=1)
            ends = ends - jnp.where(row == touching, sums[:, None, :], 0.0)
            term = jnp.dot(green, halo, precision=lax.Precision.HIGHEST)
            low = low + jnp.where(touching == 0, term, 0.0)
            high = high + jnp.where(touching == 0, 0.0, term)
        return ends, low, high

    def entering(own, other):
        mine = core[0] == 0
        return jnp.concatenate([jnp.where(mine, own, other), jnp.where(mine, other, own)], axis=1)

    given = [lax.dynamic_index_in_dim(field, sides.row(p), 1, keepdims=False) for p in sides.rounds]
    halos = sides.exchange(given)
    psi, ends = first_relax(field, step, mass)
    for turn in range(ITERS):
        ends, low, high = edge_terms(ends, halos)
        own, other = loop.solve(ends)
        both = entering(own, other)
        if turn < ITERS - 1:
            given = []
            for parity in sides.rounds:
                at = sides.row(parity)
                flux = lax.dynamic_index_in_dim(both, at, 1, keepdims=False)
                edge = lax.dynamic_index_in_dim(psi, at, 1, keepdims=False) + jnp.where(at == 0, low, high)
                edge = edge - (r * from_start)[:, None] * flux[0] - (r * from_end)[:, None] * flux[1]
                given.append(edge)
            halos = sides.exchange(given)
            psi, ends = next_relax(core, step, mass, own, other, low, high, psi)
    row = lax.broadcasted_iota(jnp.int32, (1, planes, 1), 1)
    field = psi - (r * from_start)[:, None, None] * both[0] - (r * from_end)[:, None, None] * both[1]
    field = field + jnp.where(row == 0, low[:, None, :], 0.0) + jnp.where(row == planes - 1, high[:, None, :], 0.0)
    return field


def solution(mesh):
    return jax.shard_map(
        on_device,
        mesh=mesh,
        in_specs=(P("tm", "space", None), P(), P()),
        out_specs=P("tm", "space", None),
        check_vma=False,
    )
```

time: 478 us -> 80.1 us (0.17); the launches traced: 473 us -> 79.8 us
  blocking collectives: 193 us -> 0 us
  waiting for transfers between devices: 155 us -> 25.8 us
  starting transfers between devices: 60.6 us -> 23.1 us
  local copies, waits for them, and re-layouts: 29.8 us -> 9.28 us
  other arithmetic: 21.2 us -> 5.15 us
  Pallas kernels: 0 us -> 13.5 us
  matrix products: 10.9 us -> 0.68 us
    all_to_all x2 -> x0, blocking collectives: 193 us -> none  [the longest x1 97.6 us: on_device(): lax.all_to_all(lines, 'tm', split_axis=0, concat_axis=1, tiled=True)]
    all_to_all x2 -> x0, waiting for transfers between devices: 151 us -> none  [the longest x1 77 us: on_device(): lax.all_to_all(lines, 'tm', split_axis=0, concat_axis=1, tiled=True)]
    all_to_all x2 -> x0, starting transfers between devices: 25.1 us -> none  [the longest x1 19.9 us: on_device(): lax.all_to_all(lines, 'tm', split_axis=0, concat_axis=1, tiled=True)]
    ppermute x8 -> x20, waiting for transfers between devices: 3.83 us -> 25.8 us  [the longest x18 25.8 us: swap(): lax.ppermute(array, 'tm', [(i, i ^ offset) for i in range(self.devices)])]
    pallas_call x0 -> x2, Pallas kernels: none -> 13.5 us  [the longest x1 6.82 us: next_relax(): pl.pallas_call(next_kernel, in_specs=[SMEM] * 3 + [VMEM] * 5, scratch_sha...]
    ppermute x8 -> x20, starting transfers between devices: 35.4 us -> 23.1 us  [the longest x18 19.5 us: swap(): lax.ppermute(array, 'tm', [(i, i ^ offset) for i in range(self.devices)])]
    add x2 -> x7, other arithmetic: 14.7 us -> 3.47 us  [the longest x1 3.27 us: on_device(): field + jnp.where(row == 0, low[:, None, :], 0.0)]
    dot_general x4 -> x2, matrix products: 10.9 us -> 0.68 us  [edge_terms(): term = jnp.dot(green, halo, precision=lax.Precision.HIGHEST)]
  transfers between devices with their start and end apart: 10 -> 20, of which waited for: 6 -> 18; matrix products, arithmetic and copies ran while one was open for 2% -> 2% of each run, Pallas kernels for 0% -> 17%
where the time goes in v1:
time: 80.1 us; the launch traced here: 79.8 us
  waiting for transfers between devices  25.8 us (32%)
  starting transfers between devices  23.1 us (29%)
  Pallas kernels  13.5 us (17%)
  local copies, waits for them, and re-layouts  9.28 us (12%)
  other arithmetic  5.15 us (6%)
  between operations  2.34 us (3%)
    ppermute x18, waiting for transfers between devices, swap(): lax.ppermute(array, 'tm', [(i, i ^ offset) for i in range(self.devices)])  25.8 us
    ppermute x18, starting transfers between devices, swap(): lax.ppermute(array, 'tm', [(i, i ^ offset) for i in range(self.devices)])  19.5 us
    pallas_call x1, Pallas kernels, next_relax(): pl.pallas_call(next_kernel, in_specs=[SMEM] * 3 + [VMEM] * 5, scratch_sha...  6.82 us
    pallas_call x1, Pallas kernels, first_relax(): pl.pallas_call(first_kernel, in_specs=[SMEM, SMEM, pl.BlockSpec(memory_sp...  6.65 us
    unnamed x7, local copies, waits for them, and re-layouts  6.42 us
    ppermute x2, starting transfers between devices, exchange(): lax.ppermute(given, 'space', [(i, i + 1) for i in low] + [(i + 1, i) for...  3.6 us
    add x1, other arithmetic, on_device(): field + jnp.where(row == 0, low[:, None, :], 0.0)  3.27 us
  transfers between devices with their start and end apart: 20, of which 18 were waited for; matrix products, arithmetic and copies ran while one was open for 2% of the time, Pallas kernels for 17%

profile of v1, /device:TPU:0, one launch (start us, length us, event | category | flops | bytes accessed | tf_op | source)
XLA Modules:
  0.0 79.8 jit_solution(17443815183800757851)
XLA Ops:
  0.0 1.3 %constant_dynamic-slice_fusion.3 = f32[16,1,2048]{2,1,0:T(1,128)S(1)} fusion(f32[16,32,2048]{2,1,0:T(8,128)} %field_ref.1, s32[]{:T(128)S(6)} %select_n.387), kind=kLoop, calls=%fused_computation.137 | loop fusion | bytes 262148 | tf_op jit(solution)/shard_map/jit(dynamic_index_in_dim)/dynamic_slice | solution.py:305
  1.4 3.0 %collective-permute-start = (f32[16,2048]{1,0:T(8,128)S(1)}, f32[16,2048]{1,0:T(8,128)S(1)}, u32[]{:S(2)}, u32[]{:S(2)}) collective-permute-start(f32[16,2048]{1,0:T(8,128)S(1)} %bitcast.55), channel_id=1, source_target_pairs={{0,1},{1,0},{2,3},{3,2},{4,5},{5,4},{6,7},{7,6},{8,9},{9,8},{10,11... | collective-permute-start | bytes 393224 | tf_op jit(solution)/shard_map/ppermute | solution.py:271
  6.1 2.2 %copy-done = f32[16,32,2048]{2,1,0:T(8,128)S(1)} copy-done((f32[16,32,2048]{2,1,0:T(8,128)S(1)}, f32[16,32,2048]{2,1,0:T(8,128)}, u32[]{:S(2)}) %copy-start) | copy-done | bytes 4194328
  8.3 6.6 %shard_map.37 = (f32[16,32,2048]{2,1,0:T(8,128)S(1)}, f32[2,32,2048]{2,1,0:T(8,128)S(1)}) custom-call(f32[1]{0:T(128)} %copy.11.step_ref, f32[1]{0:T(128)} %copy.12.mass_ref, f32[16,32,2048]{2,1,0:T(8,128)S(1)} %copy-done), custom_call_target="tpu_custom_call" | custom-call | flops 31457280 | bytes 8388608 | tf_op jit(solution)/shard_map/pallas_call | solution.py:162
  15.0 2.0 %copy-done.1 = f32[16,32,2048]{2,1,0:T(8,128)} copy-done((f32[16,32,2048]{2,1,0:T(8,128)}, f32[16,32,2048]{2,1,0:T(8,128)S(1)}, u32[]{:S(2)}) %copy-start.1) | copy-done | bytes 4194328
  17.0 0.1 multiply_reduce_fusion.1
  17.1 0.1 select_subtract_fusion.1
  17.4 1.4 %collective-permute-done.1 = f32[2,16,2048]{2,1,0:T(8,128)S(1)} collective-permute-done((f32[2,16,2048]{2,1,0:T(8,128)S(1)}, f32[2,16,2048]{2,1,0:T(8,128)S(1)}, u32[]{:S(2)}, u32[]{:S(2)}) %collective-permute-start.1) | collective-permute-done | bytes 262176 | tf_op jit(solution)/shard_map/ppermute | solution.py:192
  19.0 1.6 %collective-permute-start.2 = (f32[2,4,2048]{2,1,0:T(4,128)S(1)}, f32[2,4,2048]{2,1,0:T(4,128)S(1)}, u32[]{:S(2)}, u32[]{:S(2)}) collective-permute-start(f32[2,4,2048]{2,1,0:T(4,128)S(1)} %get-tuple-element.76), channel_id=1, source_target_pairs={{0,4},{2,6},{4,0},{6,2},{8,12},{10,14},{12,8},{14,10},{16,20},{18,... | collective-permute-start | bytes 196616 | tf_op jit(solution)/shard_map/ppermute | solution.py:192
  20.5 1.6 %collective-permute-start.3 = (f32[2,4,2048]{2,1,0:T(4,128)S(1)}, f32[2,4,2048]{2,1,0:T(4,128)S(1)}, u32[]{:S(2)}, u32[]{:S(2)}) collective-permute-start(f32[2,4,2048]{2,1,0:T(4,128)S(1)} %get-tuple-element.77), channel_id=1, source_target_pairs={{0,8},{2,10},{4,12},{6,14},{8,0},{10,2},{12,4},{14,6},{16,24},{18,... | collective-permute-start | bytes 196616 | tf_op jit(solution)/shard_map/ppermute | solution.py:192
  22.1 0.4 collective-permute-start.4
  22.7 0.7 collective-permute-done.2
  23.3 2.0 %collective-permute-done.3 = f32[2,4,2048]{2,1,0:T(4,128)S(1)} collective-permute-done((f32[2,4,2048]{2,1,0:T(4,128)S(1)}, f32[2,4,2048]{2,1,0:T(4,128)S(1)}, u32[]{:S(2)}, u32[]{:S(2)}) %collective-permute-start.3) | collective-permute-done | bytes 65568 | tf_op jit(solution)/shard_map/ppermute | solution.py:192
  25.4 1.9 %collective-permute-done.4 = f32[2,4,2048]{2,1,0:T(4,128)S(1)} collective-permute-done((f32[2,4,2048]{2,1,0:T(4,128)S(1)}, f32[2,4,2048]{2,1,0:T(4,128)S(1)}, u32[]{:S(2)}, u32[]{:S(2)}) %collective-permute-start.4) | collective-permute-done | bytes 65568 | tf_op jit(solution)/shard_map/ppermute | solution.py:192
  27.4 2.7 %collective-permute-start.5 = (f32[2,4,2048]{2,1,0:T(4,128)S(1)}, f32[2,4,2048]{2,1,0:T(4,128)S(1)}, u32[]{:S(2)}, u32[]{:S(2)}) collective-permute-start(f32[2,4,2048]{2,1,0:T(4,128)S(1)} %pad_maximum_fusion.9), channel_id=1, source_target_pairs={{0,16},{2,18},{4,20},{6,22},{8,24},{10,26},{12,28},{14,30},{16,0},... | collective-permute-start | bytes 196616 | tf_op jit(solution)/shard_map/ppermute | solution.py:192
  30.1 3.0 %collective-permute-done.5 = f32[2,4,2048]{2,1,0:T(4,128)S(1)} collective-permute-done((f32[2,4,2048]{2,1,0:T(4,128)S(1)}, f32[2,4,2048]{2,1,0:T(4,128)S(1)}, u32[]{:S(2)}, u32[]{:S(2)}) %collective-permute-start.5) | collective-permute-done | bytes 65568 | tf_op jit(solution)/shard_map/ppermute | solution.py:192
  33.4 0.7 collective-permute-start.6
  34.1 0.5 collective-permute-start.7
  34.6 2.5 %collective-permute-start.8 = (f32[2,4,2048]{2,1,0:T(4,128)S(1)}, f32[2,4,2048]{2,1,0:T(4,128)S(1)}, u32[]{:S(2)}, u32[]{:S(2)}) collective-permute-start(f32[2,4,2048]{2,1,0:T(4,128)S(1)} %pad_maximum_fusion.12), channel_id=1, source_target_pairs={{0,12},{2,14},{4,8},{6,10},{8,4},{10,6},{12,0},{14,2},{16,28},{18,... | collective-permute-start | bytes 196616 | tf_op jit(solution)/shard_map/ppermute | solution.py:192
  37.1 0.6 collective-permute-done.6
  37.7 0.7 collective-permute-done.7
  38.5 1.5 %collective-permute-done.8 = f32[2,4,2048]{2,1,0:T(4,128)S(1)} collective-permute-done((f32[2,4,2048]{2,1,0:T(4,128)S(1)}, f32[2,4,2048]{2,1,0:T(4,128)S(1)}, u32[]{:S(2)}, u32[]{:S(2)}) %collective-permute-start.8) | collective-permute-done | bytes 65568 | tf_op jit(solution)/shard_map/ppermute | solution.py:192
  40.4 1.3 %constant_dynamic-slice_fusion.1 = f32[16,1,2048]{2,1,0:T(1,128)S(1)} fusion(f32[16,32,2048]{2,1,0:T(8,128)} %copy-done.1, s32[]{:T(128)S(6)} %select_n.387), kind=kLoop, calls=%fused_computation.135 | loop fusion | bytes 262148 | tf_op jit(solution)/shard_map/jit(dynamic_index_in_dim)/dynamic_slice | solution.py:317
  41.7 0.2 collective-permute-done.9.other_ref
  42.0 0.4 fusion.6
  42.3 0.6 collective-permute-start.10
  42.9 2.2 %copy-done.2 = f32[16,32,2048]{2,1,0:T(8,128)S(1)} copy-done((f32[16,32,2048]{2,1,0:T(8,128)S(1)}, f32[16,32,2048]{2,1,0:T(8,128)}, u32[]{:S(2)}) %copy-start.2) | copy-done | bytes 4194328
  45.1 6.8 %shard_map.38 = (f32[16,32,2048]{2,1,0:T(8,128)S(1)}, f32[2,32,2048]{2,1,0:T(8,128)S(1)}) custom-call(s32[1]{0:T(128)} %bitcast.core_ref, f32[1]{0:T(128)} %copy.11.step_ref, f32[1]{0:T(128)} %copy.12.mass_ref, f32[2,16,2048]{2,1,0:T(8,128)S(1)} %get-tuple-element.64.own_ref, f32[2,16,2048]{2,1,0:T(8,128)S(1)} %collective-permute-done.9.other_ref, ...), custom_call_target="tpu_custom_call" | custom-call | flops 31457280 | bytes 8388608 | tf_op jit(solution)/shard_map/pallas_call | solution.py:175
  51.9 0.1 multiply_reduce_fusion
  52.1 0.1 select_subtract_fusion
  52.3 1.5 %collective-permute-done.11 = f32[2,16,2048]{2,1,0:T(8,128)S(1)} collective-permute-done((f32[2,16,2048]{2,1,0:T(8,128)S(1)}, f32[2,16,2048]{2,1,0:T(8,128)S(1)}, u32[]{:S(2)}, u32[]{:S(2)}) %collective-permute-start.11) | collective-permute-done | bytes 262176 | tf_op jit(solution)/shard_map/ppermute | solution.py:192
  53.9 0.9 %collective-permute-start.12 = (f32[2,4,2048]{2,1,0:T(4,128)S(1)}, f32[2,4,2048]{2,1,0:T(4,128)S(1)}, u32[]{:S(2)}, u32[]{:S(2)}) collective-permute-start(f32[2,4,2048]{2,1,0:T(4,128)S(1)} %get-tuple-element.62), channel_id=1, source_target_pairs={{0,4},{2,6},{4,0},{6,2},{8,12},{10,14},{12,8},{14,10},{16,20},{18,... | collective-permute-start | bytes 196616 | tf_op jit(solution)/shard_map/ppermute | solution.py:192
  54.9 2.0 %collective-permute-start.13 = (f32[2,4,2048]{2,1,0:T(4,128)S(1)}, f32[2,4,2048]{2,1,0:T(4,128)S(1)}, u32[]{:S(2)}, u32[]{:S(2)}) collective-permute-start(f32[2,4,2048]{2,1,0:T(4,128)S(1)} %get-tuple-element.63), channel_id=1, source_target_pairs={{0,8},{2,10},{4,12},{6,14},{8,0},{10,2},{12,4},{14,6},{16,24},{18,... | collective-permute-start | bytes 196616 | tf_op jit(solution)/shard_map/ppermute | solution.py:192
  56.9 0.6 collective-permute-start.14
  57.5 0.8 collective-permute-done.12
  58.3 0.9 %collective-permute-done.13 = f32[2,4,2048]{2,1,0:T(4,128)S(1)} collective-permute-done((f32[2,4,2048]{2,1,0:T(4,128)S(1)}, f32[2,4,2048]{2,1,0:T(4,128)S(1)}, u32[]{:S(2)}, u32[]{:S(2)}) %collective-permute-start.13) | collective-permute-done | bytes 65568 | tf_op jit(solution)/shard_map/ppermute | solution.py:192
  59.2 2.9 %collective-permute-done.14 = f32[2,4,2048]{2,1,0:T(4,128)S(1)} collective-permute-done((f32[2,4,2048]{2,1,0:T(4,128)S(1)}, f32[2,4,2048]{2,1,0:T(4,128)S(1)}, u32[]{:S(2)}, u32[]{:S(2)}) %collective-permute-start.14) | collective-permute-done | bytes 65568 | tf_op jit(solution)/shard_map/ppermute | solution.py:192
  62.1 2.1 %collective-permute-start.15 = (f32[2,4,2048]{2,1,0:T(4,128)S(1)}, f32[2,4,2048]{2,1,0:T(4,128)S(1)}, u32[]{:S(2)}, u32[]{:S(2)}) collective-permute-start(f32[2,4,2048]{2,1,0:T(4,128)S(1)} %pad_maximum_fusion.13), channel_id=1, source_target_pairs={{0,16},{2,18},{4,20},{6,22},{8,24},{10,26},{12,28},{14,30},{16,0},... | collective-permute-start | bytes 196616 | tf_op jit(solution)/shard_map/ppermute | solution.py:192
  64.2 3.6 %collective-permute-done.15 = f32[2,4,2048]{2,1,0:T(4,128)S(1)} collective-permute-done((f32[2,4,2048]{2,1,0:T(4,128)S(1)}, f32[2,4,2048]{2,1,0:T(4,128)S(1)}, u32[]{:S(2)}, u32[]{:S(2)}) %collective-permute-start.15) | collective-permute-done | bytes 65568 | tf_op jit(solution)/shard_map/ppermute | solution.py:192
  68.0 1.0 %collective-permute-start.16 = (f32[2,4,2048]{2,1,0:T(4,128)S(1)}, f32[2,4,2048]{2,1,0:T(4,128)S(1)}, u32[]{:S(2)}, u32[]{:S(2)}) collective-permute-start(f32[2,4,2048]{2,1,0:T(4,128)S(1)} %pad_maximum_fusion.14), channel_id=1, source_target_pairs={{0,4},{2,6},{4,0},{6,2},{8,12},{10,14},{12,8},{14,10},{16,20},{18,... | collective-permute-start | bytes 196616 | tf_op jit(solution)/shard_map/ppermute | solution.py:192
  69.0 0.4 collective-permute-start.17
  69.4 2.3 %collective-permute-start.18 = (f32[2,4,2048]{2,1,0:T(4,128)S(1)}, f32[2,4,2048]{2,1,0:T(4,128)S(1)}, u32[]{:S(2)}, u32[]{:S(2)}) collective-permute-start(f32[2,4,2048]{2,1,0:T(4,128)S(1)} %pad_maximum_fusion.16), channel_id=1, source_target_pairs={{0,12},{2,14},{4,8},{6,10},{8,4},{10,6},{12,0},{14,2},{16,28},{18,... | collective-permute-start | bytes 196616 | tf_op jit(solution)/shard_map/ppermute | solution.py:192
  71.7 0.6 collective-permute-done.16
  72.3 1.0 %collective-permute-done.17 = f32[2,4,2048]{2,1,0:T(4,128)S(1)} collective-permute-done((f32[2,4,2048]{2,1,0:T(4,128)S(1)}, f32[2,4,2048]{2,1,0:T(4,128)S(1)}, u32[]{:S(2)}, u32[]{:S(2)}) %collective-permute-start.17) | collective-permute-done | bytes 65568 | tf_op jit(solution)/shard_map/ppermute | solution.py:192
  73.3 1.3 %collective-permute-done.18 = f32[2,4,2048]{2,1,0:T(4,128)S(1)} collective-permute-done((f32[2,4,2048]{2,1,0:T(4,128)S(1)}, f32[2,4,2048]{2,1,0:T(4,128)S(1)}, u32[]{:S(2)}, u32[]{:S(2)}) %collective-permute-start.18) | collective-permute-done | bytes 65568 | tf_op jit(solution)/shard_map/ppermute | solution.py:192
  75.0 0.3 broadcast_select_fusion.3
  75.3 1.2 %collective-permute-done.19 = f32[2,16,2048]{2,1,0:T(8,128)S(1)} collective-permute-done((f32[2,16,2048]{2,1,0:T(8,128)S(1)}, f32[2,16,2048]{2,1,0:T(8,128)S(1)}, u32[]{:S(2)}, u32[]{:S(2)}) %collective-permute-start.19) | collective-permute-done | bytes 262176 | tf_op jit(solution)/shard_map/ppermute | solution.py:192
  76.6 3.3 %select_add_fusion = f32[16,32,2048]{2,1,0:T(8,128)} fusion(f32[16,32,2048]{2,1,0:T(8,128)S(1)} %get-tuple-element.11, f32[16,2048]{1,0:T(8,128)S(1)} %get-tuple-element.83, f32[16,2048]{1,0:T(8,128)S(1)} %get-tuple-element.82, f32[32,2048]{1,0:T(8,128)S(1)} %get-tuple-element.42, f32[16]{0:T(128)S(1)} %get-tuple-element.109, ...), kind=kLoop, calls=%fused_computation | loop fusion | flops 8388608 | bytes 9175232 | tf_op jit(solution)/shard_map/add | solution.py:324
  (59 shorter events, 2.0 us)
Async XLA Ops:
  1.4 15.6 %collective-permute-start = (f32[16,2048]{1,0:T(8,128)S(1)}, f32[16,2048]{1,0:T(8,128)S(1)}, u32[]{:S(2)}, u32[]{:S(2)}) collective-permute-start(f32[16,2048]{1,0:T(8,128)S(1)} %bitcast.55), channel_id=1, source_target_pairs={{0,1},{1,0},{2,3},{3,2},{4,5},{5,4},{6,7},{7,6},{8,9},{9,8},{10,11... | collective-permute-start | bytes 393224 | tf_op jit(solution)/shard_map/ppermute | solution.py:271
  6.1 2.2 %copy-start = (f32[16,32,2048]{2,1,0:T(8,128)S(1)}, f32[16,32,2048]{2,1,0:T(8,128)}, u32[]{:S(2)}) copy-start(f32[16,32,2048]{2,1,0:T(8,128)} %field_ref.1) | copy-start | bytes 12582916
  15.0 2.0 %copy-start.1 = (f32[16,32,2048]{2,1,0:T(8,128)}, f32[16,32,2048]{2,1,0:T(8,128)S(1)}, u32[]{:S(2)}) copy-start(f32[16,32,2048]{2,1,0:T(8,128)S(1)} %get-tuple-element.10.old_ref) | copy-start | bytes 12582916
  17.3 1.6 %collective-permute-start.1 = (f32[2,16,2048]{2,1,0:T(8,128)S(1)}, f32[2,16,2048]{2,1,0:T(8,128)S(1)}, u32[]{:S(2)}, u32[]{:S(2)}) collective-permute-start(f32[2,16,2048]{2,1,0:T(8,128)S(1)} %constant_dynamic-slice_fusion.2), channel_id=1, source_target_pairs={{0,2},{2,0},{4,6},{6,4},{8,10},{10,8},{12,14},{14,12},{16,18},{18,... | collective-permute-start | bytes 786440 | tf_op jit(solution)/shard_map/ppermute | solution.py:192
  19.0 4.3 %collective-permute-start.2 = (f32[2,4,2048]{2,1,0:T(4,128)S(1)}, f32[2,4,2048]{2,1,0:T(4,128)S(1)}, u32[]{:S(2)}, u32[]{:S(2)}) collective-permute-start(f32[2,4,2048]{2,1,0:T(4,128)S(1)} %get-tuple-element.76), channel_id=1, source_target_pairs={{0,4},{2,6},{4,0},{6,2},{8,12},{10,14},{12,8},{14,10},{16,20},{18,... | collective-permute-start | bytes 196616 | tf_op jit(solution)/shard_map/ppermute | solution.py:192
  20.5 4.8 %collective-permute-start.3 = (f32[2,4,2048]{2,1,0:T(4,128)S(1)}, f32[2,4,2048]{2,1,0:T(4,128)S(1)}, u32[]{:S(2)}, u32[]{:S(2)}) collective-permute-start(f32[2,4,2048]{2,1,0:T(4,128)S(1)} %get-tuple-element.77), channel_id=1, source_target_pairs={{0,8},{2,10},{4,12},{6,14},{8,0},{10,2},{12,4},{14,6},{16,24},{18,... | collective-permute-start | bytes 196616 | tf_op jit(solution)/shard_map/ppermute | solution.py:192
  22.1 5.2 %collective-permute-start.4 = (f32[2,4,2048]{2,1,0:T(4,128)S(1)}, f32[2,4,2048]{2,1,0:T(4,128)S(1)}, u32[]{:S(2)}, u32[]{:S(2)}) collective-permute-start(f32[2,4,2048]{2,1,0:T(4,128)S(1)} %get-tuple-element.74), channel_id=1, source_target_pairs={{0,12},{2,14},{4,8},{6,10},{8,4},{10,6},{12,0},{14,2},{16,28},{18,... | collective-permute-start | bytes 196616 | tf_op jit(solution)/shard_map/ppermute | solution.py:192
  27.4 5.8 %collective-permute-start.5 = (f32[2,4,2048]{2,1,0:T(4,128)S(1)}, f32[2,4,2048]{2,1,0:T(4,128)S(1)}, u32[]{:S(2)}, u32[]{:S(2)}) collective-permute-start(f32[2,4,2048]{2,1,0:T(4,128)S(1)} %pad_maximum_fusion.9), channel_id=1, source_target_pairs={{0,16},{2,18},{4,20},{6,22},{8,24},{10,26},{12,28},{14,30},{16,0},... | collective-permute-start | bytes 196616 | tf_op jit(solution)/shard_map/ppermute | solution.py:192
  33.4 4.3 %collective-permute-start.6 = (f32[2,4,2048]{2,1,0:T(4,128)S(1)}, f32[2,4,2048]{2,1,0:T(4,128)S(1)}, u32[]{:S(2)}, u32[]{:S(2)}) collective-permute-start(f32[2,4,2048]{2,1,0:T(4,128)S(1)} %pad_maximum_fusion.10), channel_id=1, source_target_pairs={{0,4},{2,6},{4,0},{6,2},{8,12},{10,14},{12,8},{14,10},{16,20},{18,... | collective-permute-start | bytes 196616 | tf_op jit(solution)/shard_map/ppermute | solution.py:192
  34.1 4.3 %collective-permute-start.7 = (f32[2,4,2048]{2,1,0:T(4,128)S(1)}, f32[2,4,2048]{2,1,0:T(4,128)S(1)}, u32[]{:S(2)}, u32[]{:S(2)}) collective-permute-start(f32[2,4,2048]{2,1,0:T(4,128)S(1)} %pad_maximum_fusion.11), channel_id=1, source_target_pairs={{0,8},{2,10},{4,12},{6,14},{8,0},{10,2},{12,4},{14,6},{16,24},{18,... | collective-permute-start | bytes 196616 | tf_op jit(solution)/shard_map/ppermute | solution.py:192
  34.6 5.4 %collective-permute-start.8 = (f32[2,4,2048]{2,1,0:T(4,128)S(1)}, f32[2,4,2048]{2,1,0:T(4,128)S(1)}, u32[]{:S(2)}, u32[]{:S(2)}) collective-permute-start(f32[2,4,2048]{2,1,0:T(4,128)S(1)} %pad_maximum_fusion.12), channel_id=1, source_target_pairs={{0,12},{2,14},{4,8},{6,10},{8,4},{10,6},{12,0},{14,2},{16,28},{18,... | collective-permute-start | bytes 196616 | tf_op jit(solution)/shard_map/ppermute | solution.py:192
  40.3 1.6 %collective-permute-start.9 = (f32[2,16,2048]{2,1,0:T(8,128)S(1)}, f32[2,16,2048]{2,1,0:T(8,128)S(1)}, u32[]{:S(2)}, u32[]{:S(2)}) collective-permute-start(f32[2,16,2048]{2,1,0:T(8,128)S(1)} %pad_maximum_fusion.4), channel_id=1, source_target_pairs={{0,2},{2,0},{4,6},{6,4},{8,10},{10,8},{12,14},{14,12},{16,18},{18,... | collective-permute-start | bytes 786440 | tf_op jit(solution)/shard_map/ppermute | solution.py:192
  42.3 9.6 %collective-permute-start.10 = (f32[16,2048]{1,0:T(8,128)S(1)}, f32[16,2048]{1,0:T(8,128)S(1)}, u32[]{:S(2)}, u32[]{:S(2)}) collective-permute-start(f32[16,2048]{1,0:T(8,128)S(1)} %get-tuple-element.84), channel_id=1, source_target_pairs={{0,1},{1,0},{2,3},{3,2},{4,5},{5,4},{6,7},{7,6},{8,9},{9,8},{10,11... | collective-permute-start | bytes 393224 | tf_op jit(solution)/shard_map/ppermute | solution.py:271
  42.9 2.2 %copy-start.2 = (f32[16,32,2048]{2,1,0:T(8,128)S(1)}, f32[16,32,2048]{2,1,0:T(8,128)}, u32[]{:S(2)}) copy-start(f32[16,32,2048]{2,1,0:T(8,128)} %copy-done.1) | copy-start | bytes 12582916
  52.2 1.6 %collective-permute-start.11 = (f32[2,16,2048]{2,1,0:T(8,128)S(1)}, f32[2,16,2048]{2,1,0:T(8,128)S(1)}, u32[]{:S(2)}, u32[]{:S(2)}) collective-permute-start(f32[2,16,2048]{2,1,0:T(8,128)S(1)} %constant_dynamic-slice_fusion), channel_id=1, source_target_pairs={{0,2},{2,0},{4,6},{6,4},{8,10},{10,8},{12,14},{14,12},{16,18},{18,... | collective-permute-start | bytes 786440 | tf_op jit(solution)/shard_map/ppermute | solution.py:192
  53.9 4.3 %collective-permute-start.12 = (f32[2,4,2048]{2,1,0:T(4,128)S(1)}, f32[2,4,2048]{2,1,0:T(4,128)S(1)}, u32[]{:S(2)}, u32[]{:S(2)}) collective-permute-start(f32[2,4,2048]{2,1,0:T(4,128)S(1)} %get-tuple-element.62), channel_id=1, source_target_pairs={{0,4},{2,6},{4,0},{6,2},{8,12},{10,14},{12,8},{14,10},{16,20},{18,... | collective-permute-start | bytes 196616 | tf_op jit(solution)/shard_map/ppermute | solution.py:192
  54.9 4.3 %collective-permute-start.13 = (f32[2,4,2048]{2,1,0:T(4,128)S(1)}, f32[2,4,2048]{2,1,0:T(4,128)S(1)}, u32[]{:S(2)}, u32[]{:S(2)}) collective-permute-start(f32[2,4,2048]{2,1,0:T(4,128)S(1)} %get-tuple-element.63), channel_id=1, source_target_pairs={{0,8},{2,10},{4,12},{6,14},{8,0},{10,2},{12,4},{14,6},{16,24},{18,... | collective-permute-start | bytes 196616 | tf_op jit(solution)/shard_map/ppermute | solution.py:192
  56.9 5.2 %collective-permute-start.14 = (f32[2,4,2048]{2,1,0:T(4,128)S(1)}, f32[2,4,2048]{2,1,0:T(4,128)S(1)}, u32[]{:S(2)}, u32[]{:S(2)}) collective-permute-start(f32[2,4,2048]{2,1,0:T(4,128)S(1)} %get-tuple-element.60), channel_id=1, source_target_pairs={{0,12},{2,14},{4,8},{6,10},{8,4},{10,6},{12,0},{14,2},{16,28},{18,... | collective-permute-start | bytes 196616 | tf_op jit(solution)/shard_map/ppermute | solution.py:192
  62.1 5.7 %collective-permute-start.15 = (f32[2,4,2048]{2,1,0:T(4,128)S(1)}, f32[2,4,2048]{2,1,0:T(4,128)S(1)}, u32[]{:S(2)}, u32[]{:S(2)}) collective-permute-start(f32[2,4,2048]{2,1,0:T(4,128)S(1)} %pad_maximum_fusion.13), channel_id=1, source_target_pairs={{0,16},{2,18},{4,20},{6,22},{8,24},{10,26},{12,28},{14,30},{16,0},... | collective-permute-start | bytes 196616 | tf_op jit(solution)/shard_map/ppermute | solution.py:192
  68.0 4.3 %collective-permute-start.16 = (f32[2,4,2048]{2,1,0:T(4,128)S(1)}, f32[2,4,2048]{2,1,0:T(4,128)S(1)}, u32[]{:S(2)}, u32[]{:S(2)}) collective-permute-start(f32[2,4,2048]{2,1,0:T(4,128)S(1)} %pad_maximum_fusion.14), channel_id=1, source_target_pairs={{0,4},{2,6},{4,0},{6,2},{8,12},{10,14},{12,8},{14,10},{16,20},{18,... | collective-permute-start | bytes 196616 | tf_op jit(solution)/shard_map/ppermute | solution.py:192
  69.0 4.3 %collective-permute-start.17 = (f32[2,4,2048]{2,1,0:T(4,128)S(1)}, f32[2,4,2048]{2,1,0:T(4,128)S(1)}, u32[]{:S(2)}, u32[]{:S(2)}) collective-permute-start(f32[2,4,2048]{2,1,0:T(4,128)S(1)} %pad_maximum_fusion.15), channel_id=1, source_target_pairs={{0,8},{2,10},{4,12},{6,14},{8,0},{10,2},{12,4},{14,6},{16,24},{18,... | collective-permute-start | bytes 196616 | tf_op jit(solution)/shard_map/ppermute | solution.py:192
  69.4 5.2 %collective-permute-start.18 = (f32[2,4,2048]{2,1,0:T(4,128)S(1)}, f32[2,4,2048]{2,1,0:T(4,128)S(1)}, u32[]{:S(2)}, u32[]{:S(2)}) collective-permute-start(f32[2,4,2048]{2,1,0:T(4,128)S(1)} %pad_maximum_fusion.16), channel_id=1, source_target_pairs={{0,12},{2,14},{4,8},{6,10},{8,4},{10,6},{12,0},{14,2},{16,28},{18,... | collective-permute-start | bytes 196616 | tf_op jit(solution)/shard_map/ppermute | solution.py:192
  74.9 1.6 %collective-permute-start.19 = (f32[2,16,2048]{2,1,0:T(8,128)S(1)}, f32[2,16,2048]{2,1,0:T(8,128)S(1)}, u32[]{:S(2)}, u32[]{:S(2)}) collective-permute-start(f32[2,16,2048]{2,1,0:T(8,128)S(1)} %pad_maximum_fusion.8), channel_id=1, source_target_pairs={{0,2},{2,0},{4,6},{6,4},{8,10},{10,8},{12,14},{14,12},{16,18},{18,... | collective-permute-start | bytes 786440 | tf_op jit(solution)/shard_map/ppermute | solution.py:192

commit v2 on v1

--- a/solution.py
+++ b/solution.py
@@ -1,3 +1,5 @@
+import functools
+
 import jax
 import jax.numpy as jnp
 from jax import lax
@@ -17,8 +19,8 @@
     return 1.0 + 0.5 * mass * mass - mass * root, 0.5 / (mass * root)
 
 
-def relax(phi, step_ref, mass_ref, psi_ref, ends_ref, tiles):
-    slices, planes, _ = psi_ref.shape
+def relax(phi, step_ref, mass_ref, psi_ref, ends_ref, edges_ref):
+    slices, planes, width = psi_ref.shape
     blocks = planes // ROWS
     lane = lax.broadcasted_iota(jnp.int32, (ROWS, LANES), 1)
     row = lax.broadcasted_iota(jnp.int32, (ROWS, LANES), 0)
@@ -67,10 +69,15 @@
             ends_ref[1, rows, out] = b
             for t in range(slices):
                 local = backward[t] if t == 0 else forward[t] + backward[t]
-                psi_ref[t, rows, out] = keep * at(t, i, start) - local
+                value = keep * at(t, i, start) - local
+                psi_ref[t, rows, out] = value
+                if i == 0:
+                    edges_ref[0, t : t + 1, out] = value[:1]
+                if i == blocks - 1:
+                    edges_ref[1, t : t + 1, out] = value[ROWS - 1 :]
         return carry
 
-    lax.fori_loop(tiles[0], tiles[1], tile, 0)
+    lax.fori_loop(0, width // LANES, tile, 0)
 
 
 def clear_guards(phi):
@@ -80,30 +87,35 @@
     phi[:, :, width - LANES :] = guard
 
 
-def first_kernel(step_ref, mass_ref, field_ref, psi_ref, ends_ref, phi, sems):
-    width = psi_ref.shape[-1]
+def load_kernel(field_ref, phi_ref, edges_ref, sems):
+    slices, planes, padded = phi_ref.shape
+    width = padded - 2 * LANES
     parts = sems.shape[0]
-    part = width // parts
+    part = planes // parts
     copies = []
     for n in range(parts):
         copies.append(
             pltpu.make_async_copy(
-                field_ref.at[:, :, n * part : (n + 1) * part],
-                phi.at[:, :, LANES + n * part : LANES + (n + 1) * part],
+                field_ref.at[:, n * part : (n + 1) * part, :],
+                phi_ref.at[:, n * part : (n + 1) * part, LANES : LANES + width],
                 sems.at[n],
             )
         )
         copies[-1].start()
-    clear_guards(phi)
-    copies[0].wait()
-    for n in range(parts):
-        if n + 1 < parts:
-            copies[n + 1].wait()
-        relax(phi, step_ref, mass_ref, psi_ref, ends_ref, (n * part // LANES, (n + 1) * part // LANES))
-
-
-def next_kernel(core_ref, step_ref, mass_ref, own_ref, other_ref, low_ref, high_ref, old_ref, psi_ref, ends_ref, phi):
-    slices, planes, width = psi_ref.shape
+    clear_guards(phi_ref)
+    for copy in copies:
+        copy.wait()
+    for t in range(slices):
+        edges_ref[0, t : t + 1, :] = phi_ref[t, 0:1, LANES : LANES + width]
+        edges_ref[1, t : t + 1, :] = phi_ref[t, planes - 1 : planes, LANES : LANES + width]
+
+
+def first_kernel(step_ref, mass_ref, phi_ref, psi_ref, ends_ref, edges_ref):
+    relax(phi_ref, step_ref, mass_ref, psi_ref, ends_ref, edges_ref)
+
+
+def entered(half_ref, mass_ref, own_ref, other_ref, low_ref, high_ref, old_ref, new_ref, offset, done):
+    slices, planes, width = old_ref.shape
     blocks = planes // ROWS
     mass = jnp.full((ROWS, LANES), mass_ref[0], jnp.float32)
     r, _ = decay(mass)
@@ -112,17 +124,15 @@
     for _ in range(slices - 1):
         last = last * r
     row = lax.broadcasted_iota(jnp.int32, (ROWS, LANES), 0)
-    core = core_ref[0]
-    clear_guards(phi)
-
-    def tile(j, carry):
-        lanes = pl.ds(pl.multiple_of(j * LANES, LANES), LANES)
-        inner = pl.ds(pl.multiple_of((j + 1) * LANES, LANES), LANES)
-        for i in range(blocks):
-            rows = slice(ROWS * i, ROWS * (i + 1))
-            half = 2 * i // blocks
-            place = slice(ROWS * i - half * planes // 2, ROWS * (i + 1) - half * planes // 2)
-            mine = core == half
+    for i in range(blocks):
+        rows = slice(ROWS * i, ROWS * (i + 1))
+        half = 2 * i // blocks
+        place = slice(ROWS * i - half * planes // 2, ROWS * (i + 1) - half * planes // 2)
+        mine = half_ref[0] == half
+
+        def tile(j, carry):
+            lanes = pl.ds(pl.multiple_of(j * LANES, LANES), LANES)
+            inner = pl.ds(pl.multiple_of(j * LANES + offset, LANES), LANES)
             p = jnp.where(mine, own_ref[0, place, lanes], other_ref[0, place, lanes]) * r
             q = jnp.where(mine, own_ref[1, place, lanes], other_ref[1, place, lanes]) * last
             for t in range(slices):
@@ -131,53 +141,117 @@
                     value = value + jnp.where(row == 0, low_ref[t : t + 1, lanes], 0.0)
                 if i == blocks - 1:
                     value = value + jnp.where(row == ROWS - 1, high_ref[t : t + 1, lanes], 0.0)
-                phi[t, rows, inner] = value
+                new_ref[t, rows, inner] = value
                 p, q = p * r, q * inverse
-        return carry
-
-    lax.fori_loop(0, width // LANES, tile, 0)
-    relax(phi, step_ref, mass_ref, psi_ref, ends_ref, (0, width // LANES))
+            return carry
+
+        lax.fori_loop(0, width // LANES, tile, 0)
+        done(i)
+
+
+def next_kernel(
+    half_ref, step_ref, mass_ref, own_ref, other_ref, low_ref, high_ref, old_ref, psi_ref, ends_ref, edges_ref, phi
+):
+    clear_guards(phi)
+    entered(half_ref, mass_ref, own_ref, other_ref, low_ref, high_ref, old_ref, phi, LANES, lambda i: None)
+    relax(phi, step_ref, mass_ref, psi_ref, ends_ref, edges_ref)
+
+
+def last_kernel(half_ref, mass_ref, own_ref, other_ref, low_ref, high_ref, old_ref, out_ref, stage, sems):
+    copies = []
+
+    def send(i):
+        rows = slice(ROWS * i, ROWS * (i + 1))
+        copies.append(pltpu.make_async_copy(stage.at[:, rows, :], out_ref.at[:, rows, :], sems.at[i]))
+        copies[-1].start()
+
+    entered(half_ref, mass_ref, own_ref, other_ref, low_ref, high_ref, old_ref, stage, 0, send)
+    for copy in copies:
+        copy.wait()
 
 
 VMEM = pl.BlockSpec(memory_space=pltpu.VMEM)
 SMEM = pl.BlockSpec(memory_space=pltpu.SMEM)
-
-
-def outputs_of(shape):
+PARAMS = pltpu.CompilerParams(vmem_limit_bytes=24 * 2**20)
+
+
+def in_vmem(array):
+    return pltpu.with_memory_space_constraint(array, pltpu.VMEM)
+
+
+def in_hbm(array):
+    return pltpu.with_memory_space_constraint(array, pltpu.HBM)
+
+
+def vmem(shape):
+    return pltpu.VMEM(shape, jnp.float32)
+
+
+def hbm(shape):
+    return pltpu.HBM(shape, jnp.float32)
+
+
+def cost(shape, flops):
+    size = shape[0] * shape[1] * shape[2]
+    return pl.CostEstimate(flops=flops * size, bytes_accessed=8 * size, transcendentals=0)
+
+
+def relaxed(shape):
     slices, planes, width = shape
     return dict(
         out_shape=(
-            jax.ShapeDtypeStruct(shape, jnp.float32),
-            jax.ShapeDtypeStruct((2, planes, width), jnp.float32),
+            vmem(shape),
+            vmem((2, planes, width)),
+            vmem((2, slices, width)),
+        ),
+        out_specs=(VMEM, VMEM, VMEM),
+        compiler_params=PARAMS,
+        cost_estimate=cost(shape, 30),
+    )
+
+
+def load(field):
+    slices, planes, width = field.shape
+    parts = planes // ROWS
+    return pl.pallas_call(
+        load_kernel,
+        in_specs=[pl.BlockSpec(memory_space=pltpu.HBM)],
+        out_shape=(
+            vmem((slices, planes, width + 2 * LANES)),
+            vmem((2, slices, width)),
         ),
         out_specs=(VMEM, VMEM),
-        compiler_params=pltpu.CompilerParams(vmem_limit_bytes=24 * 2**20),
-        cost_estimate=pl.CostEstimate(flops=30 * slices * planes * width, bytes_accessed=8 * slices * planes * width, transcendentals=0),
-    )
-
-
-def first_relax(field, step, mass):
-    slices, planes, width = field.shape
-    parts = 4 if width % (4 * LANES) == 0 else 1
-    return pl.pallas_call(
-        first_kernel,
-        in_specs=[SMEM, SMEM, pl.BlockSpec(memory_space=pl.ANY)],
-        scratch_shapes=[
-            pltpu.VMEM((slices, planes, width + 2 * LANES), jnp.float32),
-            pltpu.SemaphoreType.DMA((parts,)),
-        ],
-        **outputs_of(field.shape),
-    )(step, mass, field)
-
-
-def next_relax(core, step, mass, own, other, low, high, psi):
+        scratch_shapes=[pltpu.SemaphoreType.DMA((parts,))],
+        compiler_params=PARAMS,
+        cost_estimate=cost(field.shape, 1),
+    )(in_hbm(field))
+
+
+def first_relax(shape, phi, step, mass):
+    return pl.pallas_call(first_kernel, in_specs=[SMEM, SMEM, VMEM], **relaxed(shape))(step, mass, in_vmem(phi))
+
+
+def next_relax(half, step, mass, own, other, low, high, psi):
     slices, planes, width = psi.shape
     return pl.pallas_call(
         next_kernel,
         in_specs=[SMEM] * 3 + [VMEM] * 5,
         scratch_shapes=[pltpu.VMEM((slices, planes, width + 2 * LANES), jnp.float32)],
-        **outputs_of(psi.shape),
-    )(core, step, mass, own, other, low, high, psi)
+        **relaxed(psi.shape),
+    )(half, step, mass, own, other, low, high, in_vmem(psi))
+
+
+def last_step(half, mass, own, other, low, high, psi):
+    slices, planes, width = psi.shape
+    return pl.pallas_call(
+        last_kernel,
+        in_specs=[SMEM] * 2 + [VMEM] * 5,
+        out_shape=hbm(psi.shape),
+        out_specs=pl.BlockSpec(memory_space=pltpu.HBM),
+        scratch_shapes=[pltpu.VMEM(psi.shape, jnp.float32), pltpu.SemaphoreType.DMA((planes // ROWS,))],
+        compiler_params=PARAMS,
+        cost_estimate=cost(psi.shape, 6),
+    )(half, mass, own, other, low, high, in_vmem(psi))
 
 
 class Loop:
@@ -186,9 +260,14 @@
         self.me = lax.axis_index("tm")
         self.rate = 2.0 * jnp.arcsinh(0.5 * mass) * slices
         self.levels = self.devices.bit_length() - 1
+        self.half = functools.reduce(jnp.bitwise_xor, [self.me >> k for k in range(self.levels)]) & 1
         assert self.devices == 1 << self.levels
 
     def swap(self, array, offset):
+        offset = 2 * offset | offset.bit_count() & 1
+        return self.exchange(array, offset)
+
+    def exchange(self, array, offset):
         return lax.ppermute(array, "tm", [(i, i ^ offset) for i in range(self.devices)])
 
     def rho(self, level):
@@ -216,9 +295,9 @@
 
     def solve(self, ends):
         half = ends.shape[1] // 2
-        bit = self.me & 1
+        bit = self.half
         mine0 = lax.dynamic_slice_in_dim(ends, bit * half, half, 1)
-        theirs0 = self.swap(lax.dynamic_slice_in_dim(ends, (1 - bit) * half, half, 1), 1)
+        theirs0 = self.exchange(lax.dynamic_slice_in_dim(ends, (1 - bit) * half, half, 1), 1)
         chip = self.merge(mine0, theirs0, 0)
 
         group = (self.me >> 1) & 3
@@ -228,12 +307,12 @@
             return lax.dynamic_slice_in_dim(chip, (group ^ k) * quarter, quarter, 1)
 
         a0 = part(0)
-        a1, a2, a3 = (self.swap(part(k), 2 * k) for k in (1, 2, 3))
+        a1, a2, a3 = (self.swap(part(k), k) for k in (1, 2, 3))
         near, far = self.merge(a0, a1, 1), self.merge(a2, a3, 1)
         arc = self.merge(near, far, 2)
         stack = []
         for level in range(3, self.levels):
-            theirs = self.swap(arc, 1 << level)
+            theirs = self.swap(arc, 1 << level - 1)
             stack.append((arc, theirs, level))
             arc = self.merge(arc, theirs, level)
         enters = arc / (1.0 - self.rho(self.levels))
@@ -245,12 +324,12 @@
         p1 = self.down_other(a0, a1, enters_near, 1)
         p2 = self.down(a2, a3, enters_far, 1)
         p3 = self.down_other(a2, a3, enters_far, 1)
-        back = jnp.stack([p0] + [self.swap(p, 2 * k) for k, p in ((1, p1), (2, p2), (3, p3))])
+        back = jnp.stack([p0] + [self.swap(p, k) for k, p in ((1, p1), (2, p2), (3, p3))])
         chip_enters = jnp.concatenate(
             [lax.dynamic_index_in_dim(back, group ^ k, 0, keepdims=False) for k in range(4)], axis=1
         )
         own = self.down(mine0, theirs0, chip_enters, 0)
-        other = self.swap(self.down_other(mine0, theirs0, chip_enters, 0), 1)
+        other = self.exchange(self.down_other(mine0, theirs0, chip_enters, 0), 1)
         return own, other
 
 
@@ -283,8 +362,7 @@
     from_end = from_start[::-1]
     green = step[0] * amplitude * jnp.exp(-rate * jnp.abs(times[:, None] - times[None, :]))
     weights = step[0] * amplitude * jnp.stack([from_end, from_start])
-    core = (loop.me & 1).astype(jnp.int32).reshape(1)
-    half = planes // 2
+    half = loop.half.astype(jnp.int32).reshape(1)
 
     def edge_terms(ends, halos):
         row = lax.broadcasted_iota(jnp.int32, (1, planes, 1), 1)
@@ -298,31 +376,24 @@
             high = high + jnp.where(touching == 0, 0.0, term)
         return ends, low, high
 
-    def entering(own, other):
-        mine = core[0] == 0
-        return jnp.concatenate([jnp.where(mine, own, other), jnp.where(mine, other, own)], axis=1)
-
-    given = [lax.dynamic_index_in_dim(field, sides.row(p), 1, keepdims=False) for p in sides.rounds]
-    halos = sides.exchange(given)
-    psi, ends = first_relax(field, step, mass)
+    def give(edges):
+        return sides.exchange([jnp.where(sides.row(p) == 0, edges[0], edges[1]) for p in sides.rounds])
+
+    phi, edges = load(field)
+    halos = give(edges)
+    psi, ends, edges = first_relax(field.shape, phi, step, mass)
     for turn in range(ITERS):
         ends, low, high = edge_terms(ends, halos)
         own, other = loop.solve(ends)
-        both = entering(own, other)
         if turn < ITERS - 1:
-            given = []
-            for parity in sides.rounds:
-                at = sides.row(parity)
-                flux = lax.dynamic_index_in_dim(both, at, 1, keepdims=False)
-                edge = lax.dynamic_index_in_dim(psi, at, 1, keepdims=False) + jnp.where(at == 0, low, high)
-                edge = edge - (r * from_start)[:, None] * flux[0] - (r * from_end)[:, None] * flux[1]
-                given.append(edge)
-            halos = sides.exchange(given)
-            psi, ends = next_relax(core, step, mass, own, other, low, high, psi)
-    row = lax.broadcasted_iota(jnp.int32, (1, planes, 1), 1)
-    field = psi - (r * from_start)[:, None, None] * both[0] - (r * from_end)[:, None, None] * both[1]
-    field = field + jnp.where(row == 0, low[:, None, :], 0.0) + jnp.where(row == planes - 1, high[:, None, :], 0.0)
-    return field
+            first = jnp.where(loop.half == 0, own[:, 0], other[:, 0])
+            last = jnp.where(loop.half == 1, own[:, -1], other[:, -1])
+            entering = [
+                (r * from_start)[:, None] * flux[0] + (r * from_end)[:, None] * flux[1] for flux in (first, last)
+            ]
+            halos = give((edges[0] + low - entering[0], edges[1] + high - entering[1]))
+            psi, ends, edges = next_relax(half, step, mass, own, other, low, high, psi)
+    return last_step(half, mass, own, other, low, high, psi)
 
 
 def solution(mesh):

time: 80.1 us -> 84.7 us (1.057)
  waiting for transfers between devices: 25.8 us -> 31.5 us
  Pallas kernels: 13.5 us -> 19 us
  other arithmetic: 5.15 us -> 1.78 us
  starting transfers between devices: 23.1 us -> 20.2 us
    ppermute x18, waiting for transfers between devices: 25.8 us -> 31.5 us  [exchange(): lax.ppermute(array, 'tm', [(i, i ^ offset) for i in range(self.devices)])]
    pallas_call x1 -> x3, Pallas kernels: 6.65 us -> 10.8 us  [the longest x1 5.99 us: first_relax(): pl.pallas_call(first_kernel, in_specs=[SMEM, SMEM, VMEM], **relaxed(shape))]
    add x1 -> x0, other arithmetic: 3.27 us -> none  [on_device(): field + jnp.where(row == 0, low[:, None, :], 0.0)]
    ppermute x18, starting transfers between devices: 19.5 us -> 16.6 us  [exchange(): lax.ppermute(array, 'tm', [(i, i ^ offset) for i in range(self.devices)])]
    dynamic_slice x2 -> x0, local copies, waits for them, and re-layouts: 2.64 us -> none  [the longest x1 1.32 us: on_device(): lax.dynamic_index_in_dim(psi, at, 1, keepdims=False)]
    unnamed x7 -> x8, local copies, waits for them, and re-layouts: 6.42 us -> 8.65 us
    pallas_call x1, Pallas kernels: 6.82 us -> 8.22 us  [next_relax(): pl.pallas_call(next_kernel, in_specs=[SMEM] * 3 + [VMEM] * 5, scratch_sha...]
  transfers between devices with their start and end apart: 20 -> 20, of which waited for: 18 -> 17; matrix products, arithmetic and copies ran while one was open for 2% -> 1% of each run, Pallas kernels for 17% -> 17%
where the time goes in v2:
time: 84.7 us; the launch traced here: 84.5 us
  waiting for transfers between devices  31.5 us (37%)
  starting transfers between devices  20.2 us (24%)
  Pallas kernels  19 us (22%)
  local copies, waits for them, and re-layouts  8.87 us (10%)
  between operations  2.35 us (3%)
  other arithmetic  1.78 us (2%)
    ppermute x18, waiting for transfers between devices, exchange(): lax.ppermute(array, 'tm', [(i, i ^ offset) for i in range(self.devices)])  31.5 us
    ppermute x18, starting transfers between devices, exchange(): lax.ppermute(array, 'tm', [(i, i ^ offset) for i in range(self.devices)])  16.6 us
    unnamed x8, local copies, waits for them, and re-layouts  8.65 us
    pallas_call x1, Pallas kernels, next_relax(): pl.pallas_call(next_kernel, in_specs=[SMEM] * 3 + [VMEM] * 5, scratch_sha...  8.22 us
    pallas_call x1, Pallas kernels, first_relax(): pl.pallas_call(first_kernel, in_specs=[SMEM, SMEM, VMEM], **relaxed(shape))  5.99 us
    ppermute x2, starting transfers between devices, exchange(): lax.ppermute(given, 'space', [(i, i + 1) for i in low] + [(i + 1, i) for...  3.6 us
    pallas_call x1, Pallas kernels, last_step(): pl.pallas_call(last_kernel, in_specs=[SMEM] * 2 + [VMEM] * 5, out_shape=h...  2.56 us
    pallas_call x1, Pallas kernels, load(): pl.pallas_call(load_kernel, in_specs=[pl.BlockSpec(memory_space=pltpu.HBM...  2.27 us
  transfers between devices with their start and end apart: 20, of which 17 were waited for; matrix products, arithmetic and copies ran while one was open for 1% of the time, Pallas kernels for 17%

profile of v2, /device:TPU:0, one launch (start us, length us, event | category | flops | bytes accessed | tf_op | source)
XLA Modules:
  0.0 84.5 jit_solution(14371949403027976307)
XLA Ops:
  0.0 2.3 %shard_map.37 = (f32[16,32,2304]{2,1,0:T(8,128)S(1)}, f32[2,16,2048]{2,1,0:T(8,128)S(1)}) custom-call(f32[16,32,2048]{2,1,0:T(8,128)} %field_ref.1), custom_call_target="tpu_custom_call" | custom-call | flops 1048576 | bytes 8388608 | tf_op jit(solution)/shard_map/pallas_call | solution.py:216
  2.3 2.1 %copy-done = f32[16,32,2304]{2,1,0:T(8,128)} copy-done((f32[16,32,2304]{2,1,0:T(8,128)}, f32[16,32,2304]{2,1,0:T(8,128)S(1)}, u32[]{:S(2)}) %copy-start) | copy-done | bytes 4718616
  4.4 3.0 %collective-permute-start = (f32[16,2048]{1,0:T(8,128)S(1)}, f32[16,2048]{1,0:T(8,128)S(1)}, u32[]{:S(2)}, u32[]{:S(2)}) collective-permute-start(f32[16,2048]{1,0:T(8,128)S(1)} %select_bitcast_fusion), channel_id=1, source_target_pairs={{0,1},{1,0},{2,3},{3,2},{4,5},{5,4},{6,7},{7,6},{8,9},{9,8},{10,11... | collective-permute-start | bytes 393224 | tf_op jit(solution)/shard_map/ppermute | solution.py:350
  8.4 0.1 rev.3
  9.2 2.3 %copy-done.1 = f32[16,32,2304]{2,1,0:T(8,128)S(1)} copy-done((f32[16,32,2304]{2,1,0:T(8,128)S(1)}, f32[16,32,2304]{2,1,0:T(8,128)}, u32[]{:S(2)}) %copy-start.1) | copy-done | bytes 4718616
  11.5 6.0 %shard_map.38 = (f32[16,32,2048]{2,1,0:T(8,128)S(1)}, f32[2,32,2048]{2,1,0:T(8,128)S(1)}, f32[2,16,2048]{2,1,0:T(8,128)S(1)}) custom-call(f32[1]{0:T(128)} %copy.4.step_ref, f32[1]{0:T(128)} %copy.5.mass_ref, f32[16,32,2304]{2,1,0:T(8,128)S(1)} %copy-done.1), custom_call_target="tpu_custom_call" | custom-call | flops 31457280 | bytes 8388608 | tf_op jit(solution)/shard_map/pallas_call | solution.py:231
  17.5 2.0 %copy-done.2 = f32[16,32,2048]{2,1,0:T(8,128)} copy-done((f32[16,32,2048]{2,1,0:T(8,128)}, f32[16,32,2048]{2,1,0:T(8,128)S(1)}, u32[]{:S(2)}) %copy-start.2) | copy-done | bytes 4194328
  19.6 0.1 multiply_reduce_fusion.1
  19.7 0.1 select_subtract_fusion.1
  20.0 1.4 %collective-permute-done.1 = f32[2,16,2048]{2,1,0:T(8,128)S(1)} collective-permute-done((f32[2,16,2048]{2,1,0:T(8,128)S(1)}, f32[2,16,2048]{2,1,0:T(8,128)S(1)}, u32[]{:S(2)}, u32[]{:S(2)}) %collective-permute-start.1) | collective-permute-done | bytes 262176 | tf_op jit(solution)/shard_map/ppermute | solution.py:271
  21.5 1.3 %collective-permute-start.2 = (f32[2,4,2048]{2,1,0:T(4,128)S(1)}, f32[2,4,2048]{2,1,0:T(4,128)S(1)}, u32[]{:S(2)}, u32[]{:S(2)}) collective-permute-start(f32[2,4,2048]{2,1,0:T(4,128)S(1)} %get-tuple-element.77), channel_id=1, source_target_pairs={{0,6},{2,4},{4,2},{6,0},{8,14},{10,12},{12,10},{14,8},{16,22},{18,... | collective-permute-start | bytes 196616 | tf_op jit(solution)/shard_map/ppermute | solution.py:271
  22.8 1.6 %collective-permute-start.3 = (f32[2,4,2048]{2,1,0:T(4,128)S(1)}, f32[2,4,2048]{2,1,0:T(4,128)S(1)}, u32[]{:S(2)}, u32[]{:S(2)}) collective-permute-start(f32[2,4,2048]{2,1,0:T(4,128)S(1)} %get-tuple-element.78), channel_id=1, source_target_pairs={{0,10},{2,8},{4,14},{6,12},{8,2},{10,0},{12,6},{14,4},{16,26},{18,... | collective-permute-start | bytes 196616 | tf_op jit(solution)/shard_map/ppermute | solution.py:271
  24.4 0.4 collective-permute-start.4
  24.9 0.8 collective-permute-done.2
  25.7 1.1 %collective-permute-done.3 = f32[2,4,2048]{2,1,0:T(4,128)S(1)} collective-permute-done((f32[2,4,2048]{2,1,0:T(4,128)S(1)}, f32[2,4,2048]{2,1,0:T(4,128)S(1)}, u32[]{:S(2)}, u32[]{:S(2)}) %collective-permute-start.3) | collective-permute-done | bytes 65568 | tf_op jit(solution)/shard_map/ppermute | solution.py:271
  26.8 2.7 %collective-permute-done.4 = f32[2,4,2048]{2,1,0:T(4,128)S(1)} collective-permute-done((f32[2,4,2048]{2,1,0:T(4,128)S(1)}, f32[2,4,2048]{2,1,0:T(4,128)S(1)}, u32[]{:S(2)}, u32[]{:S(2)}) %collective-permute-start.4) | collective-permute-done | bytes 65568 | tf_op jit(solution)/shard_map/ppermute | solution.py:271
  29.6 1.3 %collective-permute-start.5 = (f32[2,4,2048]{2,1,0:T(4,128)S(1)}, f32[2,4,2048]{2,1,0:T(4,128)S(1)}, u32[]{:S(2)}, u32[]{:S(2)}) collective-permute-start(f32[2,4,2048]{2,1,0:T(4,128)S(1)} %pad_maximum_fusion.8), channel_id=1, source_target_pairs={{0,18},{2,16},{4,22},{6,20},{8,26},{10,24},{12,30},{14,28},{16,2},... | collective-permute-start | bytes 196616 | tf_op jit(solution)/shard_map/ppermute | solution.py:271
  31.0 5.2 %collective-permute-done.5 = f32[2,4,2048]{2,1,0:T(4,128)S(1)} collective-permute-done((f32[2,4,2048]{2,1,0:T(4,128)S(1)}, f32[2,4,2048]{2,1,0:T(4,128)S(1)}, u32[]{:S(2)}, u32[]{:S(2)}) %collective-permute-start.5) | collective-permute-done | bytes 65568 | tf_op jit(solution)/shard_map/ppermute | solution.py:271
  36.4 0.3 collective-permute-start.6
  36.7 0.6 collective-permute-start.7
  37.3 2.6 %collective-permute-start.8 = (f32[2,4,2048]{2,1,0:T(4,128)S(1)}, f32[2,4,2048]{2,1,0:T(4,128)S(1)}, u32[]{:S(2)}, u32[]{:S(2)}) collective-permute-start(f32[2,4,2048]{2,1,0:T(4,128)S(1)} %pad_maximum_fusion.11), channel_id=1, source_target_pairs={{0,12},{2,14},{4,8},{6,10},{8,4},{10,6},{12,0},{14,2},{16,28},{18,... | collective-permute-start | bytes 196616 | tf_op jit(solution)/shard_map/ppermute | solution.py:271
  39.9 0.7 collective-permute-done.6
  40.6 2.9 %collective-permute-done.8 = f32[2,4,2048]{2,1,0:T(4,128)S(1)} collective-permute-done((f32[2,4,2048]{2,1,0:T(4,128)S(1)}, f32[2,4,2048]{2,1,0:T(4,128)S(1)}, u32[]{:S(2)}, u32[]{:S(2)}) %collective-permute-start.8) | collective-permute-done | bytes 65568 | tf_op jit(solution)/shard_map/ppermute | solution.py:271
  43.8 0.1 collective-permute-start.9
  44.0 1.5 %collective-permute-done.9.other_ref = f32[2,16,2048]{2,1,0:T(8,128)S(1)} collective-permute-done((f32[2,16,2048]{2,1,0:T(8,128)S(1)}, f32[2,16,2048]{2,1,0:T(8,128)S(1)}, u32[]{:S(2)}, u32[]{:S(2)}) %collective-permute-start.9) | collective-permute-done | bytes 262176 | tf_op jit(solution)/shard_map/ppermute | solution.py:271
  45.5 0.4 fusion.1
  45.9 0.6 collective-permute-start.10
  46.5 2.2 %copy-done.3 = f32[16,32,2048]{2,1,0:T(8,128)S(1)} copy-done((f32[16,32,2048]{2,1,0:T(8,128)S(1)}, f32[16,32,2048]{2,1,0:T(8,128)}, u32[]{:S(2)}) %copy-start.3) | copy-done | bytes 4194328
  48.6 8.2 %shard_map.39 = (f32[16,32,2048]{2,1,0:T(8,128)S(1)}, f32[2,32,2048]{2,1,0:T(8,128)S(1)}, f32[2,16,2048]{2,1,0:T(8,128)}) custom-call(s32[1]{0:T(128)} %bitcast.half_ref, f32[1]{0:T(128)} %copy.4.step_ref, f32[1]{0:T(128)} %copy.5.mass_ref, f32[2,16,2048]{2,1,0:T(8,128)S(1)} %pad_maximum_fusion.own_ref, f32[2,16,2048]{2,1,0:T(8,128)S(1)} %collective-permute-done.9.other_ref, ...), custom_call_target="tpu_custom_call" | custom-call | flops 31457280 | bytes 8388608 | tf_op jit(solution)/shard_map/pallas_call | solution.py:236
  56.9 0.1 multiply_reduce_fusion
  57.0 0.1 select_subtract_fusion
  57.2 1.5 %collective-permute-done.11 = f32[2,16,2048]{2,1,0:T(8,128)S(1)} collective-permute-done((f32[2,16,2048]{2,1,0:T(8,128)S(1)}, f32[2,16,2048]{2,1,0:T(8,128)S(1)}, u32[]{:S(2)}, u32[]{:S(2)}) %collective-permute-start.11) | collective-permute-done | bytes 262176 | tf_op jit(solution)/shard_map/ppermute | solution.py:271
  58.8 0.3 collective-permute-start.12
  59.1 1.6 %collective-permute-start.13 = (f32[2,4,2048]{2,1,0:T(4,128)S(1)}, f32[2,4,2048]{2,1,0:T(4,128)S(1)}, u32[]{:S(2)}, u32[]{:S(2)}) collective-permute-start(f32[2,4,2048]{2,1,0:T(4,128)S(1)} %get-tuple-element.65), channel_id=1, source_target_pairs={{0,10},{2,8},{4,14},{6,12},{8,2},{10,0},{12,6},{14,4},{16,26},{18,... | collective-permute-start | bytes 196616 | tf_op jit(solution)/shard_map/ppermute | solution.py:271
  60.7 1.4 %collective-permute-start.14 = (f32[2,4,2048]{2,1,0:T(4,128)S(1)}, f32[2,4,2048]{2,1,0:T(4,128)S(1)}, u32[]{:S(2)}, u32[]{:S(2)}) collective-permute-start(f32[2,4,2048]{2,1,0:T(4,128)S(1)} %get-tuple-element.62), channel_id=1, source_target_pairs={{0,12},{2,14},{4,8},{6,10},{8,4},{10,6},{12,0},{14,2},{16,28},{18,... | collective-permute-start | bytes 196616 | tf_op jit(solution)/shard_map/ppermute | solution.py:271
  62.1 0.9 %collective-permute-done.12 = f32[2,4,2048]{2,1,0:T(4,128)S(1)} collective-permute-done((f32[2,4,2048]{2,1,0:T(4,128)S(1)}, f32[2,4,2048]{2,1,0:T(4,128)S(1)}, u32[]{:S(2)}, u32[]{:S(2)}) %collective-permute-start.12) | collective-permute-done | bytes 65568 | tf_op jit(solution)/shard_map/ppermute | solution.py:271
  63.0 0.1 collective-permute-done.13
  63.1 2.9 %collective-permute-done.14 = f32[2,4,2048]{2,1,0:T(4,128)S(1)} collective-permute-done((f32[2,4,2048]{2,1,0:T(4,128)S(1)}, f32[2,4,2048]{2,1,0:T(4,128)S(1)}, u32[]{:S(2)}, u32[]{:S(2)}) %collective-permute-start.14) | collective-permute-done | bytes 65568 | tf_op jit(solution)/shard_map/ppermute | solution.py:271
  66.0 1.7 %collective-permute-start.15 = (f32[2,4,2048]{2,1,0:T(4,128)S(1)}, f32[2,4,2048]{2,1,0:T(4,128)S(1)}, u32[]{:S(2)}, u32[]{:S(2)}) collective-permute-start(f32[2,4,2048]{2,1,0:T(4,128)S(1)} %pad_maximum_fusion.12), channel_id=1, source_target_pairs={{0,18},{2,16},{4,22},{6,20},{8,26},{10,24},{12,30},{14,28},{16,2},... | collective-permute-start | bytes 196616 | tf_op jit(solution)/shard_map/ppermute | solution.py:271
  67.7 5.0 %collective-permute-done.15 = f32[2,4,2048]{2,1,0:T(4,128)S(1)} collective-permute-done((f32[2,4,2048]{2,1,0:T(4,128)S(1)}, f32[2,4,2048]{2,1,0:T(4,128)S(1)}, u32[]{:S(2)}, u32[]{:S(2)}) %collective-permute-start.15) | collective-permute-done | bytes 65568 | tf_op jit(solution)/shard_map/ppermute | solution.py:271
  73.0 0.6 collective-permute-start.17
  73.6 2.8 %collective-permute-start.18 = (f32[2,4,2048]{2,1,0:T(4,128)S(1)}, f32[2,4,2048]{2,1,0:T(4,128)S(1)}, u32[]{:S(2)}, u32[]{:S(2)}) collective-permute-start(f32[2,4,2048]{2,1,0:T(4,128)S(1)} %pad_maximum_fusion.15), channel_id=1, source_target_pairs={{0,12},{2,14},{4,8},{6,10},{8,4},{10,6},{12,0},{14,2},{16,28},{18,... | collective-permute-start | bytes 196616 | tf_op jit(solution)/shard_map/ppermute | solution.py:271
  76.4 0.7 collective-permute-done.16
  77.1 0.1 collective-permute-done.17
  77.2 2.9 %collective-permute-done.18 = f32[2,4,2048]{2,1,0:T(4,128)S(1)} collective-permute-done((f32[2,4,2048]{2,1,0:T(4,128)S(1)}, f32[2,4,2048]{2,1,0:T(4,128)S(1)}, u32[]{:S(2)}, u32[]{:S(2)}) %collective-permute-start.18) | collective-permute-done | bytes 65568 | tf_op jit(solution)/shard_map/ppermute | solution.py:271
  80.4 0.3 broadcast_select_fusion
  80.8 1.2 %collective-permute-done.19.other_ref = f32[2,16,2048]{2,1,0:T(8,128)S(1)} collective-permute-done((f32[2,16,2048]{2,1,0:T(8,128)S(1)}, f32[2,16,2048]{2,1,0:T(8,128)S(1)}, u32[]{:S(2)}, u32[]{:S(2)}) %collective-permute-start.19) | collective-permute-done | bytes 262176 | tf_op jit(solution)/shard_map/ppermute | solution.py:271
  81.9 2.6 %shard_map.40 = f32[16,32,2048]{2,1,0:T(8,128)} custom-call(s32[1]{0:T(128)} %bitcast.half_ref, f32[1]{0:T(128)} %copy.5.mass_ref, f32[2,16,2048]{2,1,0:T(8,128)S(1)} %pad_maximum_fusion.6.own_ref, f32[2,16,2048]{2,1,0:T(8,128)S(1)} %collective-permute-done.19.other_ref, f32[16,2048]{1,0:T(8,128)S(1)} %get-tuple-element.84.low_ref, ...), custom_call_target="tpu_custom_call" | custom-call | flops 6291456 | bytes 8388608 | tf_op jit(solution)/shard_map/pallas_call | solution.py:246
  (58 shorter events, 1.8 us)
Async XLA Ops:
  2.3 2.1 %copy-start = (f32[16,32,2304]{2,1,0:T(8,128)}, f32[16,32,2304]{2,1,0:T(8,128)S(1)}, u32[]{:S(2)}) copy-start(f32[16,32,2304]{2,1,0:T(8,128)S(1)} %get-tuple-element.12.phi_ref) | copy-start | bytes 14155780
  4.4 15.1 %collective-permute-start = (f32[16,2048]{1,0:T(8,128)S(1)}, f32[16,2048]{1,0:T(8,128)S(1)}, u32[]{:S(2)}, u32[]{:S(2)}) collective-permute-start(f32[16,2048]{1,0:T(8,128)S(1)} %select_bitcast_fusion), channel_id=1, source_target_pairs={{0,1},{1,0},{2,3},{3,2},{4,5},{5,4},{6,7},{7,6},{8,9},{9,8},{10,11... | collective-permute-start | bytes 393224 | tf_op jit(solution)/shard_map/ppermute | solution.py:350
  9.2 2.3 %copy-start.1 = (f32[16,32,2304]{2,1,0:T(8,128)S(1)}, f32[16,32,2304]{2,1,0:T(8,128)}, u32[]{:S(2)}) copy-start(f32[16,32,2304]{2,1,0:T(8,128)} %copy-done) | copy-start | bytes 14155780
  17.5 2.0 %copy-start.2 = (f32[16,32,2048]{2,1,0:T(8,128)}, f32[16,32,2048]{2,1,0:T(8,128)S(1)}, u32[]{:S(2)}) copy-start(f32[16,32,2048]{2,1,0:T(8,128)S(1)} %get-tuple-element.15.old_ref) | copy-start | bytes 12582916
  19.8 1.6 %collective-permute-start.1 = (f32[2,16,2048]{2,1,0:T(8,128)S(1)}, f32[2,16,2048]{2,1,0:T(8,128)S(1)}, u32[]{:S(2)}, u32[]{:S(2)}) collective-permute-start(f32[2,16,2048]{2,1,0:T(8,128)S(1)} %constant_dynamic-slice_fusion.1), channel_id=1, source_target_pairs={{0,2},{2,0},{4,6},{6,4},{8,10},{10,8},{12,14},{14,12},{16,18},{18,... | collective-permute-start | bytes 786440 | tf_op jit(solution)/shard_map/ppermute | solution.py:271
  21.5 4.1 %collective-permute-start.2 = (f32[2,4,2048]{2,1,0:T(4,128)S(1)}, f32[2,4,2048]{2,1,0:T(4,128)S(1)}, u32[]{:S(2)}, u32[]{:S(2)}) collective-permute-start(f32[2,4,2048]{2,1,0:T(4,128)S(1)} %get-tuple-element.77), channel_id=1, source_target_pairs={{0,6},{2,4},{4,2},{6,0},{8,14},{10,12},{12,10},{14,8},{16,22},{18,... | collective-permute-start | bytes 196616 | tf_op jit(solution)/shard_map/ppermute | solution.py:271
  22.8 4.0 %collective-permute-start.3 = (f32[2,4,2048]{2,1,0:T(4,128)S(1)}, f32[2,4,2048]{2,1,0:T(4,128)S(1)}, u32[]{:S(2)}, u32[]{:S(2)}) collective-permute-start(f32[2,4,2048]{2,1,0:T(4,128)S(1)} %get-tuple-element.78), channel_id=1, source_target_pairs={{0,10},{2,8},{4,14},{6,12},{8,2},{10,0},{12,6},{14,4},{16,26},{18,... | collective-permute-start | bytes 196616 | tf_op jit(solution)/shard_map/ppermute | solution.py:271
  24.4 5.2 %collective-permute-start.4 = (f32[2,4,2048]{2,1,0:T(4,128)S(1)}, f32[2,4,2048]{2,1,0:T(4,128)S(1)}, u32[]{:S(2)}, u32[]{:S(2)}) collective-permute-start(f32[2,4,2048]{2,1,0:T(4,128)S(1)} %get-tuple-element.75), channel_id=1, source_target_pairs={{0,12},{2,14},{4,8},{6,10},{8,4},{10,6},{12,0},{14,2},{16,28},{18,... | collective-permute-start | bytes 196616 | tf_op jit(solution)/shard_map/ppermute | solution.py:271
  29.6 6.6 %collective-permute-start.5 = (f32[2,4,2048]{2,1,0:T(4,128)S(1)}, f32[2,4,2048]{2,1,0:T(4,128)S(1)}, u32[]{:S(2)}, u32[]{:S(2)}) collective-permute-start(f32[2,4,2048]{2,1,0:T(4,128)S(1)} %pad_maximum_fusion.8), channel_id=1, source_target_pairs={{0,18},{2,16},{4,22},{6,20},{8,26},{10,24},{12,30},{14,28},{16,2},... | collective-permute-start | bytes 196616 | tf_op jit(solution)/shard_map/ppermute | solution.py:271
  36.4 4.2 %collective-permute-start.6 = (f32[2,4,2048]{2,1,0:T(4,128)S(1)}, f32[2,4,2048]{2,1,0:T(4,128)S(1)}, u32[]{:S(2)}, u32[]{:S(2)}) collective-permute-start(f32[2,4,2048]{2,1,0:T(4,128)S(1)} %pad_maximum_fusion.9), channel_id=1, source_target_pairs={{0,6},{2,4},{4,2},{6,0},{8,14},{10,12},{12,10},{14,8},{16,22},{18,... | collective-permute-start | bytes 196616 | tf_op jit(solution)/shard_map/ppermute | solution.py:271
  36.7 3.9 %collective-permute-start.7 = (f32[2,4,2048]{2,1,0:T(4,128)S(1)}, f32[2,4,2048]{2,1,0:T(4,128)S(1)}, u32[]{:S(2)}, u32[]{:S(2)}) collective-permute-start(f32[2,4,2048]{2,1,0:T(4,128)S(1)} %pad_maximum_fusion.10), channel_id=1, source_target_pairs={{0,10},{2,8},{4,14},{6,12},{8,2},{10,0},{12,6},{14,4},{16,26},{18,... | collective-permute-start | bytes 196616 | tf_op jit(solution)/shard_map/ppermute | solution.py:271
  37.3 6.2 %collective-permute-start.8 = (f32[2,4,2048]{2,1,0:T(4,128)S(1)}, f32[2,4,2048]{2,1,0:T(4,128)S(1)}, u32[]{:S(2)}, u32[]{:S(2)}) collective-permute-start(f32[2,4,2048]{2,1,0:T(4,128)S(1)} %pad_maximum_fusion.11), channel_id=1, source_target_pairs={{0,12},{2,14},{4,8},{6,10},{8,4},{10,6},{12,0},{14,2},{16,28},{18,... | collective-permute-start | bytes 196616 | tf_op jit(solution)/shard_map/ppermute | solution.py:271
  43.8 1.6 %collective-permute-start.9 = (f32[2,16,2048]{2,1,0:T(8,128)S(1)}, f32[2,16,2048]{2,1,0:T(8,128)S(1)}, u32[]{:S(2)}, u32[]{:S(2)}) collective-permute-start(f32[2,16,2048]{2,1,0:T(8,128)S(1)} %pad_maximum_fusion.3), channel_id=1, source_target_pairs={{0,2},{2,0},{4,6},{6,4},{8,10},{10,8},{12,14},{14,12},{16,18},{18,... | collective-permute-start | bytes 786440 | tf_op jit(solution)/shard_map/ppermute | solution.py:271
  45.9 11.0 %collective-permute-start.10 = (f32[16,2048]{1,0:T(8,128)S(1)}, f32[16,2048]{1,0:T(8,128)S(1)}, u32[]{:S(2)}, u32[]{:S(2)}) collective-permute-start(f32[16,2048]{1,0:T(8,128)S(1)} %get-tuple-element.85), channel_id=1, source_target_pairs={{0,1},{1,0},{2,3},{3,2},{4,5},{5,4},{6,7},{7,6},{8,9},{9,8},{10,11... | collective-permute-start | bytes 393224 | tf_op jit(solution)/shard_map/ppermute | solution.py:350
  46.5 2.2 %copy-start.3 = (f32[16,32,2048]{2,1,0:T(8,128)S(1)}, f32[16,32,2048]{2,1,0:T(8,128)}, u32[]{:S(2)}) copy-start(f32[16,32,2048]{2,1,0:T(8,128)} %copy-done.2) | copy-start | bytes 12582916
  57.1 1.6 %collective-permute-start.11 = (f32[2,16,2048]{2,1,0:T(8,128)S(1)}, f32[2,16,2048]{2,1,0:T(8,128)S(1)}, u32[]{:S(2)}, u32[]{:S(2)}) collective-permute-start(f32[2,16,2048]{2,1,0:T(8,128)S(1)} %constant_dynamic-slice_fusion), channel_id=1, source_target_pairs={{0,2},{2,0},{4,6},{6,4},{8,10},{10,8},{12,14},{14,12},{16,18},{18,... | collective-permute-start | bytes 786440 | tf_op jit(solution)/shard_map/ppermute | solution.py:271
  58.8 4.1 %collective-permute-start.12 = (f32[2,4,2048]{2,1,0:T(4,128)S(1)}, f32[2,4,2048]{2,1,0:T(4,128)S(1)}, u32[]{:S(2)}, u32[]{:S(2)}) collective-permute-start(f32[2,4,2048]{2,1,0:T(4,128)S(1)} %get-tuple-element.64), channel_id=1, source_target_pairs={{0,6},{2,4},{4,2},{6,0},{8,14},{10,12},{12,10},{14,8},{16,22},{18,... | collective-permute-start | bytes 196616 | tf_op jit(solution)/shard_map/ppermute | solution.py:271
  59.1 3.9 %collective-permute-start.13 = (f32[2,4,2048]{2,1,0:T(4,128)S(1)}, f32[2,4,2048]{2,1,0:T(4,128)S(1)}, u32[]{:S(2)}, u32[]{:S(2)}) collective-permute-start(f32[2,4,2048]{2,1,0:T(4,128)S(1)} %get-tuple-element.65), channel_id=1, source_target_pairs={{0,10},{2,8},{4,14},{6,12},{8,2},{10,0},{12,6},{14,4},{16,26},{18,... | collective-permute-start | bytes 196616 | tf_op jit(solution)/shard_map/ppermute | solution.py:271
  60.7 5.2 %collective-permute-start.14 = (f32[2,4,2048]{2,1,0:T(4,128)S(1)}, f32[2,4,2048]{2,1,0:T(4,128)S(1)}, u32[]{:S(2)}, u32[]{:S(2)}) collective-permute-start(f32[2,4,2048]{2,1,0:T(4,128)S(1)} %get-tuple-element.62), channel_id=1, source_target_pairs={{0,12},{2,14},{4,8},{6,10},{8,4},{10,6},{12,0},{14,2},{16,28},{18,... | collective-permute-start | bytes 196616 | tf_op jit(solution)/shard_map/ppermute | solution.py:271
  66.0 6.7 %collective-permute-start.15 = (f32[2,4,2048]{2,1,0:T(4,128)S(1)}, f32[2,4,2048]{2,1,0:T(4,128)S(1)}, u32[]{:S(2)}, u32[]{:S(2)}) collective-permute-start(f32[2,4,2048]{2,1,0:T(4,128)S(1)} %pad_maximum_fusion.12), channel_id=1, source_target_pairs={{0,18},{2,16},{4,22},{6,20},{8,26},{10,24},{12,30},{14,28},{16,2},... | collective-permute-start | bytes 196616 | tf_op jit(solution)/shard_map/ppermute | solution.py:271
  72.9 4.2 %collective-permute-start.16 = (f32[2,4,2048]{2,1,0:T(4,128)S(1)}, f32[2,4,2048]{2,1,0:T(4,128)S(1)}, u32[]{:S(2)}, u32[]{:S(2)}) collective-permute-start(f32[2,4,2048]{2,1,0:T(4,128)S(1)} %pad_maximum_fusion.13), channel_id=1, source_target_pairs={{0,6},{2,4},{4,2},{6,0},{8,14},{10,12},{12,10},{14,8},{16,22},{18,... | collective-permute-start | bytes 196616 | tf_op jit(solution)/shard_map/ppermute | solution.py:271
  73.0 4.2 %collective-permute-start.17 = (f32[2,4,2048]{2,1,0:T(4,128)S(1)}, f32[2,4,2048]{2,1,0:T(4,128)S(1)}, u32[]{:S(2)}, u32[]{:S(2)}) collective-permute-start(f32[2,4,2048]{2,1,0:T(4,128)S(1)} %pad_maximum_fusion.14), channel_id=1, source_target_pairs={{0,10},{2,8},{4,14},{6,12},{8,2},{10,0},{12,6},{14,4},{16,26},{18,... | collective-permute-start | bytes 196616 | tf_op jit(solution)/shard_map/ppermute | solution.py:271
  73.6 6.4 %collective-permute-start.18 = (f32[2,4,2048]{2,1,0:T(4,128)S(1)}, f32[2,4,2048]{2,1,0:T(4,128)S(1)}, u32[]{:S(2)}, u32[]{:S(2)}) collective-permute-start(f32[2,4,2048]{2,1,0:T(4,128)S(1)} %pad_maximum_fusion.15), channel_id=1, source_target_pairs={{0,12},{2,14},{4,8},{6,10},{8,4},{10,6},{12,0},{14,2},{16,28},{18,... | collective-permute-start | bytes 196616 | tf_op jit(solution)/shard_map/ppermute | solution.py:271
  80.3 1.6 %collective-permute-start.19 = (f32[2,16,2048]{2,1,0:T(8,128)S(1)}, f32[2,16,2048]{2,1,0:T(8,128)S(1)}, u32[]{:S(2)}, u32[]{:S(2)}) collective-permute-start(f32[2,16,2048]{2,1,0:T(8,128)S(1)} %pad_maximum_fusion.7), channel_id=1, source_target_pairs={{0,2},{2,0},{4,6},{6,4},{8,10},{10,8},{12,14},{14,12},{16,18},{18,... | collective-permute-start | bytes 786440 | tf_op jit(solution)/shard_map/ppermute | solution.py:271

commit v3 on v0

v3 whole, which is shorter than its diff:
```python
import functools

import jax
import jax.numpy as jnp
from jax import lax
from jax.experimental import pallas as pl
from jax.experimental.pallas import tpu as pltpu
from jax.sharding import PartitionSpec as P

NZ = 32
ITERS = 2

LANES = 128
ROWS = 8
TILE = (ROWS, LANES)
UNROLL = 4

DECAY, SCALE, LINEAR, SQUARE, CUBE, KEEP, WEIGHTS = range(7)


def decay(mass):
    root = jnp.sqrt(1.0 + 0.25 * mass * mass)
    return 1.0 + 0.5 * mass * mass - mass * root, 0.5 / (mass * root)


def fill_table(scalars, table, slices):
    step, mass = jnp.full(TILE, scalars[0], jnp.float32), jnp.full(TILE, scalars[1], jnp.float32)
    r, amplitude = decay(mass)
    scale = step * amplitude
    table[DECAY], table[SCALE], table[KEEP] = r, scale, 1.0 - step
    table[LINEAR], table[SQUARE], table[CUBE] = scale * (7.0 - mass * mass), -0.9 * scale, 0.25 * scale
    powers = [jnp.ones(TILE, jnp.float32)]
    for _ in range(slices - 1):
        powers.append(powers[-1] * r)
    for k in range(slices // 2):
        table[WEIGHTS + 2 * k] = 0.5 * (powers[k] + powers[slices - 1 - k])
        table[WEIGHTS + 2 * k + 1] = 0.5 * (powers[k] - powers[slices - 1 - k])


def fill_wide(scalars, planes_ref, arcs_ref, levels):
    _, slices, width = planes_ref.shape

    def rate_of(shape):
        half = 0.5 * jnp.full(shape, scalars[1], jnp.float32)
        return 2.0 * jnp.log1p(half + half * half / (1.0 + jnp.sqrt(1.0 + half * half)))

    shape = (slices, LANES)
    rate = rate_of(shape)
    t = lax.broadcasted_iota(jnp.int32, shape, 0).astype(jnp.float32)
    mass = jnp.full(shape, scalars[1], jnp.float32)
    scale = jnp.full(shape, scalars[0], jnp.float32) * decay(mass)[1]
    start, end = jnp.exp(-rate * t), jnp.exp(-rate * (slices - 1 - t))
    r = jnp.exp(-rate)
    values = (r * start, r * end, scale * end, scale * start)
    row = lax.broadcasted_iota(jnp.int32, TILE, 0)
    rate = rate_of(TILE)
    arcs = jnp.zeros(TILE, jnp.float32)
    for level in range(levels):
        arcs = jnp.where(row == level, jnp.exp(-rate * (slices << level)), arcs)
    arcs = jnp.where(row == levels, 1.0 / (1.0 - jnp.exp(-rate * (slices << levels))), arcs)

    def tile(j, carry):
        for n, value in enumerate(values):
            planes_ref[n, :, tile_at(j)] = value
        arcs_ref[:, tile_at(j)] = arcs
        return carry

    lax.fori_loop(0, width // LANES, tile, 0)


def rows_of(i):
    return slice(ROWS * i, ROWS * (i + 1))


def tile_at(j, offset=0):
    return pl.ds(pl.multiple_of(j * LANES + offset, LANES), LANES)


class Masks:
    def __init__(self):
        lane = lax.broadcasted_iota(jnp.int32, TILE, 1)
        row = lax.broadcasted_iota(jnp.int32, TILE, 0)
        self.first_z, self.last_z = lane % NZ == 0, lane % NZ == NZ - 1
        self.first_row, self.last_row = row == 0, row == ROWS - 1
        self.head, self.tail = lane < NZ, lane >= LANES - NZ


def neighbours(masks, v, before, after, left, right):
    total = pltpu.roll(jnp.where(masks.last_row, before, v), 1, 0)
    total = total + pltpu.roll(jnp.where(masks.first_row, after, v), ROWS - 1, 0)
    total = total + jnp.where(masks.first_z, 0.0, pltpu.roll(v, 1, 1))
    total = total + jnp.where(masks.last_z, 0.0, pltpu.roll(v, LANES - 1, 1))
    total = total + pltpu.roll(jnp.where(masks.tail, left, v), NZ, 1)
    return total + pltpu.roll(jnp.where(masks.head, right, v), LANES - NZ, 1)


def entering_tile(table, half_ref, own_ref, other_ref, i, blocks, lanes):
    half = 2 * i // blocks
    place = rows_of(i - half * blocks // 2)
    mine = half_ref[0] == half
    p = jnp.where(mine, own_ref[0, place, lanes], other_ref[0, place, lanes])
    q = jnp.where(mine, own_ref[1, place, lanes], other_ref[1, place, lanes])
    r = table[DECAY]
    return r * (p + q), r * (p - q)


def entered_pair(table, both, old, k, i, lanes):
    v, w = old[k, rows_of(i), lanes], old[old.shape[0] - 1 - k, rows_of(i), lanes]
    if both is None:
        return v, w
    even, odd = table[WEIGHTS + 2 * k] * both[0], table[WEIGHTS + 2 * k + 1] * both[1]
    return v - (even + odd), w - (even - odd)


def sum_tiles(table, enter, old, ends_ref, sums, tiles):
    slices, planes, _ = old.shape
    blocks = planes // ROWS

    def tile(j, carry):
        lanes = tile_at(j)
        for i in range(blocks):
            both = enter(i, lanes) if enter else None
            for k in range(slices // 2):
                v, w = entered_pair(table, both, old, k, i, lanes)
                f = v * v * (table[SQUARE] + table[CUBE] * v)
                g = w * w * (table[SQUARE] + table[CUBE] * w)
                a, b = table[WEIGHTS + 2 * k], table[WEIGHTS + 2 * k + 1]
                terms = (a * (v + w), b * (v - w), a * (f + g), b * (f - g))
                total = terms if k == 0 else tuple(x + y for x, y in zip(total, terms))
            for n, (field, force) in enumerate(
                ((total[0] - total[1], total[2] - total[3]), (total[0] + total[1], total[2] + total[3]))
            ):
                sums[n, rows_of(i), tile_at(j, LANES)] = field
                ends_ref[n, rows_of(i), lanes] = force + table[LINEAR] * field
        return carry

    lax.fori_loop(tiles[0], tiles[1], tile, 0, unroll=UNROLL)


def finish_sums(table, ends_ref, sums):
    _, planes, width = ends_ref.shape
    blocks = planes // ROWS
    masks = Masks()
    zero = jnp.zeros(TILE, jnp.float32)

    def tile(j, carry):
        for n in range(2):
            at = lambda i, side: sums[n, rows_of(i), tile_at(j, (1 + side) * LANES)]
            for i in range(blocks):
                before = zero if i == 0 else at(i - 1, 0)
                after = zero if i == blocks - 1 else at(i + 1, 0)
                total = neighbours(masks, at(i, 0), before, after, at(i, -1), at(i, 1))
                ends_ref[n, rows_of(i), tile_at(j)] -= table[SCALE] * total
        return carry

    lax.fori_loop(0, width // LANES, tile, 0, unroll=UNROLL)


def clear_guards(ref):
    lead, planes, width = ref.shape
    guard = jnp.zeros((lead, planes, LANES), jnp.float32)
    ref[:, :, :LANES] = guard
    ref[:, :, width - LANES :] = guard


def lane_parts(width, parts):
    part = width // parts
    return [slice(n * part, (n + 1) * part) for n in range(parts)]


def tiles_of(lanes):
    return lanes.start // LANES, lanes.stop // LANES


def start_reads(source, target, parts, sems, offset=0):
    reads = []
    for n, lanes in enumerate(parts):
        there = slice(lanes.start + offset, lanes.stop + offset)
        reads.append(pltpu.make_async_copy(source.at[:, :, lanes], target.at[:, :, there], sems.at[n]))
        reads[-1].start()
    return reads


def sum_parts(table, enter, old_ref, old, ends_ref, sums, parts, reads):
    for lanes, read in zip(parts, reads):
        read.wait()
        sum_tiles(table, enter, old, ends_ref, sums, tiles_of(lanes))
    finish_sums(table, ends_ref, sums)


def first_sums_kernel(
    levels, step_ref, mass_ref, old_ref, ends_ref, table, planes_ref, arcs_ref, old, sums, sems
):
    parts = lane_parts(old.shape[-1], sems.shape[0])
    reads = start_reads(old_ref, old, parts, sems)
    clear_guards(sums)
    values = step_ref[0], mass_ref[0]
    fill_table(values, table, old.shape[0])
    fill_wide(values, planes_ref, arcs_ref, levels)
    sum_parts(table, None, old_ref, old, ends_ref, sums, parts, reads)


def next_sums_kernel(half_ref, table, own_ref, other_ref, old_ref, ends_ref, old, sums, sems):
    parts = lane_parts(old.shape[-1], sems.shape[0])
    reads = start_reads(old_ref, old, parts, sems)
    clear_guards(sums)
    blocks = old.shape[1] // ROWS

    def enter(i, lanes):
        return entering_tile(table, half_ref, own_ref, other_ref, i, blocks, lanes)

    sum_parts(table, enter, old_ref, old, ends_ref, sums, parts, reads)


def relax_tiles(table, masks, phi, low_ref, high_ref, stage, edges_ref, tiles):
    slices, planes, _ = stage.shape
    blocks = planes // ROWS
    half = slices // 2

    def tile(j, carry):
        lanes = tile_at(j)
        for i in range(blocks):
            at = lambda t, i, side: phi[t, rows_of(i), tile_at(j, (1 + side) * LANES)]
            force = [None] * slices
            for n in range(slices):
                t = n // 2 if n % 2 == 0 else slices - 1 - n // 2
                v = at(t, i, 0)
                before = low_ref[t : t + 1, lanes] if i == 0 else at(t, i - 1, 0)
                after = high_ref[t : t + 1, lanes] if i == blocks - 1 else at(t, i + 1, 0)
                total = neighbours(masks, v, before, after, at(t, i, -1), at(t, i, 1))
                force[t] = v * (table[LINEAR] + v * (table[SQUARE] + table[CUBE] * v)) - table[SCALE] * total
            forward, backward = [None] * slices, [None] * slices
            a, b = force[0], force[-1]
            backward[-1] = b
            r = table[DECAY]
            for t in range(1, slices):
                forward[t] = r * a
                a = force[t] + forward[t]
                s = slices - 1 - t
                b = force[s] + r * b
                backward[s] = b
            for t in range(slices):
                local = backward[t] if t == 0 else forward[t] + backward[t]
                value = table[KEEP] * at(t, i, 0) - local
                stage[t, rows_of(i), lanes] = value
                if i == 0:
                    edges_ref[0, t : t + 1, lanes] = value[:1]
                if i == blocks - 1:
                    edges_ref[1, t : t + 1, lanes] = value[ROWS - 1 :]
        return carry

    lax.fori_loop(tiles[0], tiles[1], tile, 0, unroll=min(UNROLL, tiles[1] - tiles[0]))


def relax_piece(table, enter, low_ref, high_ref, old_ref, psi_ref, edges_ref, phi, stage, old, in_sems, out_sems, tiles):
    slices, planes, width = stage.shape
    blocks = planes // ROWS
    first, last = tiles
    middle = (first + last) // 2
    bounds = [max(first - 1, 0), middle + 1, min(last + 1, width // LANES)]
    parts = [slice(a * LANES, b * LANES) for a, b in zip(bounds, bounds[1:])]
    reads = start_reads(old_ref, old if enter else phi, parts, in_sems, 0 if enter else LANES)
    clear_guards(phi)
    masks = Masks()

    def arrive(n):
        reads[n].wait()
        if not enter:
            return

        def tile(j, carry):
            lanes, inner = tile_at(j), tile_at(j, LANES)
            for i in range(blocks):
                both = enter(i, lanes)
                for k in range(slices // 2):
                    v, w = entered_pair(table, both, old, k, i, lanes)
                    phi[k, rows_of(i), inner] = v
                    phi[slices - 1 - k, rows_of(i), inner] = w
            return carry

        lax.fori_loop(bounds[n], bounds[n + 1], tile, 0, unroll=True)

    writes = []
    for n, part in enumerate(((first, middle), (middle, last))):
        arrive(n)
        relax_tiles(table, masks, phi, low_ref, high_ref, stage, edges_ref, part)
        lanes = slice(part[0] * LANES, part[1] * LANES)
        writes.append(pltpu.make_async_copy(stage.at[:, :, lanes], psi_ref.at[:, :, lanes], out_sems.at[n]))
        writes[-1].start()
    for write in writes:
        write.wait()


def first_relax_kernel(tiles, table, low_ref, high_ref, old_ref, _, psi_ref, edges_ref, phi, stage, in_sems, out_sems):
    relax_piece(
        table, None, low_ref, high_ref, old_ref, psi_ref, edges_ref, phi, stage, None, in_sems, out_sems, tiles
    )


def next_relax_kernel(
    tiles, half_ref, table, own_ref, other_ref, low_ref, high_ref, old_ref, _,
    psi_ref, edges_ref, phi, stage, old, in_sems, out_sems,
):
    blocks = old.shape[1] // ROWS

    def enter(i, lanes):
        return entering_tile(table, half_ref, own_ref, other_ref, i, blocks, lanes)

    relax_piece(
        table, enter, low_ref, high_ref, old_ref, psi_ref, edges_ref, phi, stage, old, in_sems, out_sems, tiles
    )


def last_kernel(half_ref, table, own_ref, other_ref, old_ref, out_ref, old, stage, in_sems, out_sems):
    slices, planes, width = old.shape
    blocks = planes // ROWS
    parts = lane_parts(width, in_sems.shape[0])
    reads = start_reads(old_ref, old, parts, in_sems)
    writes = []

    def tile(j, carry):
        lanes = tile_at(j)
        for i in range(blocks):
            both = entering_tile(table, half_ref, own_ref, other_ref, i, blocks, lanes)
            for k in range(slices // 2):
                v, w = entered_pair(table, both, old, k, i, lanes)
                stage[k, rows_of(i), lanes] = v
                stage[slices - 1 - k, rows_of(i), lanes] = w
        return carry

    for n, lanes in enumerate(parts):
        reads[n].wait()
        lax.fori_loop(*tiles_of(lanes), tile, 0, unroll=UNROLL)
        writes.append(pltpu.make_async_copy(stage.at[:, :, lanes], out_ref.at[:, :, lanes], out_sems.at[n]))
        writes[-1].start()
    for write in writes:
        write.wait()


VMEM = pl.BlockSpec(memory_space=pltpu.VMEM)
SMEM = pl.BlockSpec(memory_space=pltpu.SMEM)
HBM = pl.BlockSpec(memory_space=pltpu.HBM)
PARAMS = pltpu.CompilerParams(vmem_limit_bytes=24 * 2**20)


def in_hbm(array):
    return pltpu.with_memory_space_constraint(array, pltpu.HBM)


def hbm(shape):
    return pltpu.HBM(shape, jnp.float32)


def f32(shape):
    return jax.ShapeDtypeStruct(shape, jnp.float32)


def padded(lead, shape):
    return pltpu.VMEM((lead, shape[1], shape[2] + 2 * LANES), jnp.float32)


def parts_of(width):
    return 4 if width % (4 * LANES) == 0 else 1


def cost(shape, flops):
    size = shape[0] * shape[1] * shape[2]
    return pl.CostEstimate(flops=flops * size, bytes_accessed=4 * size, transcendentals=0)


def first_sums(step, mass, field, levels):
    slices, planes, width = field.shape
    assert slices % 2 == 0 and levels < ROWS
    return pl.pallas_call(
        functools.partial(first_sums_kernel, levels),
        in_specs=[SMEM] * 2 + [HBM],
        out_shape=(
            f32((2, planes, width)),
            f32((WEIGHTS + slices, *TILE)),
            f32((4, slices, width)),
            f32((ROWS, width)),
        ),
        out_specs=(VMEM,) * 4,
        scratch_shapes=[
            pltpu.VMEM(field.shape, jnp.float32),
            padded(2, field.shape),
            pltpu.SemaphoreType.DMA((parts_of(width),)),
        ],
        compiler_params=PARAMS,
        cost_estimate=cost(field.shape, 12),
    )(step, mass, in_hbm(field))


def next_sums(half, table, own, other, psi):
    _, planes, width = psi.shape
    return pl.pallas_call(
        next_sums_kernel,
        in_specs=[SMEM] + [VMEM] * 3 + [HBM],
        out_shape=f32((2, planes, width)),
        out_specs=VMEM,
        scratch_shapes=[
            pltpu.VMEM(psi.shape, jnp.float32),
            padded(2, psi.shape),
            pltpu.SemaphoreType.DMA((parts_of(width),)),
        ],
        compiler_params=PARAMS,
        cost_estimate=cost(psi.shape, 16),
    )(half, table, own, other, in_hbm(psi))


def relax(tiles, terms, table, low, high, old, psi):
    slices, planes, width = old.shape
    if terms:
        half, own, other = terms
        kernel, operands, specs = next_relax_kernel, [half, table, own, other], [SMEM] + [VMEM] * 3
    else:
        kernel, operands, specs = first_relax_kernel, [table], [VMEM]
    operands += [low, high, in_hbm(old)]
    specs += [VMEM, VMEM, HBM]
    aliases = {}
    if psi is not None:
        operands.append(in_hbm(psi))
        specs.append(HBM)
        aliases = {len(operands) - 1: 0}

    def body(*refs):
        refs = list(refs)
        if psi is None:
            refs.insert(len(operands), None)
        kernel(tiles, *refs)

    return pl.pallas_call(
        body,
        in_specs=specs,
        out_shape=(hbm(old.shape), f32((2, slices, width))),
        out_specs=(HBM, VMEM),
        input_output_aliases=aliases,
        scratch_shapes=[padded(slices, old.shape), pltpu.VMEM(old.shape, jnp.float32)]
        + ([pltpu.VMEM(old.shape, jnp.float32)] if terms else [])
        + [pltpu.SemaphoreType.DMA((2,))] * 2,
        compiler_params=PARAMS,
        cost_estimate=cost((slices, planes, (tiles[1] - tiles[0]) * LANES), 40),
    )(*operands)


def last_step(half, table, own, other, psi):
    semaphores = pltpu.SemaphoreType.DMA((parts_of(psi.shape[-1]),))
    return pl.pallas_call(
        last_kernel,
        in_specs=[SMEM] + [VMEM] * 3 + [HBM],
        out_shape=hbm(psi.shape),
        out_specs=HBM,
        scratch_shapes=[pltpu.VMEM(psi.shape, jnp.float32)] * 2 + [semaphores] * 2,
        compiler_params=PARAMS,
        cost_estimate=cost(psi.shape, 6),
    )(half, table, own, other, in_hbm(psi))


class Loop:
    def __init__(self):
        self.devices = lax.axis_size("tm")
        self.me = lax.axis_index("tm")
        self.levels = self.devices.bit_length() - 1
        assert self.devices == 1 << self.levels and self.levels > 3

    def swap(self, array, offset):
        return lax.ppermute(array, "tm", [(i, i ^ offset) for i in range(self.devices)])

    def rho(self, level):
        return self.arcs[level : level + 1]

    def is_left(self, level):
        return (self.me >> level) & 1 == 0

    def merge(self, mine, theirs, level):
        left, rho = self.is_left(level), self.rho(level)
        ours, others = jnp.where(left, rho, 1.0), jnp.where(left, 1.0, rho)
        return jnp.stack([ours * mine[0] + others * theirs[0], others * mine[1] + ours * theirs[1]])

    def down(self, mine, theirs, both, level):
        left, rho = self.is_left(level), self.rho(level)
        before = jnp.where(left, both[0], theirs[0] + rho * both[0])
        after = jnp.where(left, theirs[1] + rho * both[1], both[1])
        return jnp.stack([before, after])

    def down_other(self, mine, theirs, both, level):
        left, rho = self.is_left(level), self.rho(level)
        before = jnp.where(left, mine[0] + rho * both[0], both[0])
        after = jnp.where(left, both[1], mine[1] + rho * both[1])
        return jnp.stack([before, after])

    def solve(self, ends, arcs, works):
        self.arcs = arcs
        half = ends.shape[1] // 2
        bit = self.me & 1
        mine0 = lax.dynamic_slice_in_dim(ends, bit * half, half, 1)
        theirs0 = self.swap(lax.dynamic_slice_in_dim(ends, (1 - bit) * half, half, 1), 1)
        chip = self.merge(mine0, theirs0, 0)

        group = (self.me >> 1) & 3
        quarter = half // 4

        def part(k):
            return lax.dynamic_slice_in_dim(chip, (group ^ k) * quarter, quarter, 1)

        a0 = part(0)
        received = [self.swap(part(k), 2 * k) for k in (1, 2, 3)]
        state = works[0](chip)
        (a1, a2, a3), state = lax.optimization_barrier((received, state))
        near, far = self.merge(a0, a1, 1), self.merge(a2, a3, 1)
        arc = self.merge(near, far, 2)
        stack = []
        for level in range(3, self.levels):
            theirs = self.swap(arc, 1 << level)
            if level == 3:
                state = works[1](arc, state)
                theirs, state = lax.optimization_barrier((theirs, state))
            stack.append((arc, theirs, level))
            arc = self.merge(arc, theirs, level)
        enters = arc * self.rho(self.levels)
        for mine, theirs, level in reversed(stack):
            enters = self.down(mine, theirs, enters, level)
        enters_near = self.down(near, far, enters, 2)
        enters_far = self.down_other(near, far, enters, 2)
        p0 = self.down(a0, a1, enters_near, 1)
        p1 = self.down_other(a0, a1, enters_near, 1)
        p2 = self.down(a2, a3, enters_far, 1)
        p3 = self.down_other(a2, a3, enters_far, 1)
        received = [self.swap(p, 2 * k) for k, p in ((1, p1), (2, p2), (3, p3))]
        state = works[2](enters, state)
        received, state = lax.optimization_barrier((received, state))
        back = jnp.stack([p0] + received)
        chip_enters = jnp.concatenate(
            [lax.dynamic_index_in_dim(back, group ^ k, 0, keepdims=False) for k in range(4)], axis=1
        )
        own = self.down(mine0, theirs0, chip_enters, 0)
        other = self.swap(self.down_other(mine0, theirs0, chip_enters, 0), 1)
        return own, other, state


class Planes:
    def __init__(self, planes):
        self.planes = planes
        self.devices = lax.axis_size("space")
        self.me = lax.axis_index("space")
        self.rounds = [p for p in (0, 1) if p + 1 < self.devices]

    def row(self, parity):
        return jnp.where(self.me % 2 == parity, self.planes - 1, 0)

    def exchange(self, first, last):
        low = high = jnp.zeros_like(first)
        for parity in self.rounds:
            given = jnp.where(self.row(parity) == 0, first, last)
            pairs = range(parity, self.devices - 1, 2)
            got = lax.ppermute(given, "space", [(i, i + 1) for i in pairs] + [(i + 1, i) for i in pairs])
            low = low + jnp.where(self.row(parity) == 0, got, 0.0)
            high = high + jnp.where(self.row(parity) == 0, 0.0, got)
        return low, high


def on_device(field, step, mass):
    _, planes, width = field.shape
    loop = Loop()
    sides = Planes(planes)
    half = (loop.me & 1).astype(jnp.int32).reshape(1)
    tiles = width // LANES
    bounds = [0, 3 * tiles // 8, 5 * tiles // 8, tiles]

    def after(array, *others):
        return lax.optimization_barrier((array, *others))[0]

    old, terms = field, None
    first, last = field[:, 0], field[:, -1]
    for turn in range(ITERS):
        low, high = sides.exchange(first, last)
        if turn == 0:
            ends, table, weights, arcs = first_sums(step, mass, old, loop.levels)
        else:
            ends = next_sums(half, table, *terms[1:], old)
        row = lax.broadcasted_iota(jnp.int32, (1, planes, 1), 1)
        for place, plane in ((0, low), (planes - 1, high)):
            sums = jnp.sum(weights[2:] * plane[None], axis=1)
            ends = ends - jnp.where(row == place, sums[:, None, :], 0.0)

        def work(n, ready, state=None, old=old, terms=terms, low=low, high=high):
            psi, edges = state or (None, [])
            psi, more = relax(bounds[n : n + 2], terms, after(table, ready), low, high, old, psi)
            return psi, edges + [more[..., bounds[n] * LANES : bounds[n + 1] * LANES]]

        works = [functools.partial(work, n) for n in range(3)]
        own, other, (old, edges) = loop.solve(ends, arcs, works)
        terms = (half, own, other)
        if turn < ITERS - 1:
            edges = jnp.concatenate(edges, axis=2)
            mine = half[0] == 0
            first, last = (
                edges[n] - weights[0] * flux[0] - weights[1] * flux[1]
                for n, flux in (
                    (0, jnp.where(mine, own[:, 0], other[:, 0])),
                    (1, jnp.where(mine, other[:, -1], own[:, -1])),
                )
            )
    return last_step(half, table, own, other, old)


def solution(mesh):
    return jax.shard_map(
        on_device,
        mesh=mesh,
        in_specs=(P("tm", "space", None), P(), P()),
        out_specs=P("tm", "space", None),
        check_vma=False,
    )
```

time: 478 us -> 72.8 us (0.15); the launches traced: 473 us -> 72.5 us
  blocking collectives: 193 us -> 0 us
  waiting for transfers between devices: 155 us -> 6.83 us
  starting transfers between devices: 60.6 us -> 23.2 us
  Pallas kernels: 0 us -> 36.4 us
  local copies, waits for them, and re-layouts: 29.8 us -> 1.9 us
  other arithmetic: 21.2 us -> 2.16 us
  matrix products: 10.9 us -> 0 us
    all_to_all x2 -> x0, blocking collectives: 193 us -> none  [the longest x1 97.6 us: on_device(): lax.all_to_all(lines, 'tm', split_axis=0, concat_axis=1, tiled=True)]
    all_to_all x2 -> x0, waiting for transfers between devices: 151 us -> none  [the longest x1 77 us: on_device(): lax.all_to_all(lines, 'tm', split_axis=0, concat_axis=1, tiled=True)]
    pallas_call x0 -> x9, Pallas kernels: none -> 36.4 us  [the longest x6 25.2 us: relax(): pl.pallas_call(body, in_specs=specs, out_shape=(hbm(old.shape), f32((2, s...]
    all_to_all x2 -> x0, starting transfers between devices: 25.1 us -> none  [the longest x1 19.9 us: on_device(): lax.all_to_all(lines, 'tm', split_axis=0, concat_axis=1, tiled=True)]
    add x2 -> x6, other arithmetic: 14.7 us -> 0.26 us  [the longest x4 0.18 us: merge(): ours * mine[0] + others * theirs[0]]
    ppermute x8 -> x20, starting transfers between devices: 35.4 us -> 23.2 us  [the longest x18 19.6 us: swap(): lax.ppermute(array, 'tm', [(i, i ^ offset) for i in range(self.devices)])]
    dot_general x4 -> x0, matrix products: 10.9 us -> none  [the longest x2 8.12 us: on_device(): jnp.einsum('ts,sab->tab', operator, lax.all_to_all(force, 'tm', split_axi...]
    dot_general x2 -> x0, local copies, waits for them, and re-layouts: 8.48 us -> none  [on_device(): jnp.einsum('ts,sab->tab', operator, lax.all_to_all(force, 'tm', split_axi...]
  transfers between devices with their start and end apart: 10 -> 20, of which waited for: 6 -> 5; matrix products, arithmetic and copies ran while one was open for 2% -> 0% of each run, Pallas kernels for 0% -> 45%
where the time goes in v3:
time: 72.8 us; the launch traced here: 72.5 us
  Pallas kernels  36.4 us (50%)
  starting transfers between devices  23.2 us (32%)
  waiting for transfers between devices  6.83 us (9%)
  other arithmetic  2.16 us (3%)
  between operations  2.03 us (3%)
  local copies, waits for them, and re-layouts  1.9 us (3%)
    pallas_call x6, Pallas kernels, relax(): pl.pallas_call(body, in_specs=specs, out_shape=(hbm(old.shape), f32((2, s...  25.2 us
    ppermute x18, starting transfers between devices, swap(): lax.ppermute(array, 'tm', [(i, i ^ offset) for i in range(self.devices)])  19.6 us
    ppermute x18, waiting for transfers between devices, swap(): lax.ppermute(array, 'tm', [(i, i ^ offset) for i in range(self.devices)])  5.97 us
    pallas_call x1, Pallas kernels, next_sums(): pl.pallas_call(next_sums_kernel, in_specs=[SMEM] + [VMEM] * 3 + [HBM], ou...  4.15 us
    ppermute x2, starting transfers between devices, exchange(): lax.ppermute(given, 'space', [(i, i + 1) for i in pairs] + [(i + 1, i) fo...  3.6 us
    pallas_call x1, Pallas kernels, last_step(): pl.pallas_call(last_kernel, in_specs=[SMEM] + [VMEM] * 3 + [HBM], out_sha...  3.54 us
    pallas_call x1, Pallas kernels, first_sums(): pl.pallas_call(functools.partial(first_sums_kernel, levels), in_specs=[SM...  3.52 us
    slice x1, local copies, waits for them, and re-layouts, on_device(): first, last = (field[:, 0], field[:, -1])  1.73 us
  transfers between devices with their start and end apart: 20, of which 5 were waited for; matrix products, arithmetic and copies ran while one was open for 0% of the time, Pallas kernels for 45%

profile of v3, /device:TPU:0, one launch (start us, length us, event | category | flops | bytes accessed | tf_op | source)
XLA Modules:
  0.0 72.5 jit_solution(7264854409139905928)
XLA Ops:
  0.0 1.7 %fusion.16 = (f32[16,1,2048]{2,1,0:T(1,128)S(1)}, f32[16,1,2048]{2,1,0:T(1,128)S(1)}) fusion(f32[16,32,2048]{2,1,0:T(8,128)} %refs_3_.5), kind=kLoop, calls=%fused_computation.156 | loop fusion | bytes 524288 | tf_op jit(solution)/shard_map/slice | solution.py:574
  1.7 0.1 fusion.5
  1.8 3.0 %collective-permute-start = (f32[16,2048]{1,0:T(8,128)S(1)}, f32[16,2048]{1,0:T(8,128)S(1)}, u32[]{:S(2)}, u32[]{:S(2)}) collective-permute-start(f32[16,2048]{1,0:T(8,128)S(1)} %fusion.5), channel_id=1, source_target_pairs={{0,1},{1,0},{2,3},{3,2},{4,5},{5,4},{6,7},{7,6},{8,9},{9,8},{10,11... | collective-permute-start | bytes 393224 | tf_op jit(solution)/shard_map/ppermute | solution.py:556
  6.2 3.5 %shard_map.37 = (f32[2,32,2048]{2,1,0:T(8,128)S(1)}, f32[22,8,128]{2,1,0:T(8,128)S(1)}, f32[4,16,2048]{2,1,0:T(8,128)S(1)}, f32[8,2048]{1,0:T(8,128)S(1)}) custom-call(f32[1]{0:T(128)S(6)} %copy.22.step_ref, f32[1]{0:T(128)S(6)} %copy.23.mass_ref, f32[16,32,2048]{2,1,0:T(8,128)} %refs_3_.5), custom_call_target="tpu_custom_call" | custom-call | flops 12582912 | bytes 4194304 | tf_op jit(solution)/shard_map/pallas_call | solution.py:374
  9.7 0.1 multiply_reduce_fusion.3
  9.9 0.2 select_subtract_fusion.1
  10.0 0.1 collective-permute-start.1
  10.1 0.1 fusion.17
  10.2 1.4 %collective-permute-done.1 = f32[2,16,2048]{2,1,0:T(8,128)S(1)} collective-permute-done((f32[2,16,2048]{2,1,0:T(8,128)S(1)}, f32[2,16,2048]{2,1,0:T(8,128)S(1)}, u32[]{:S(2)}, u32[]{:S(2)}) %collective-permute-start.1) | collective-permute-done | bytes 262176 | tf_op jit(solution)/shard_map/ppermute | solution.py:467
  11.8 2.6 %collective-permute-start.4 = (f32[2,4,2048]{2,1,0:T(4,128)S(1)}, f32[2,4,2048]{2,1,0:T(4,128)S(1)}, u32[]{:S(2)}, u32[]{:S(2)}) collective-permute-start(f32[2,4,2048]{2,1,0:T(4,128)S(1)} %get-tuple-element.153), channel_id=1, source_target_pairs={{0,12},{2,14},{4,8},{6,10},{8,4},{10,6},{12,0},{14,2},{16,28},{18,... | collective-permute-start | bytes 196616 | tf_op jit(solution)/shard_map/ppermute | solution.py:467
  14.3 0.5 collective-permute-start.2
  14.9 0.4 collective-permute-start.3
  15.3 4.0 %shard_map.38 = (f32[16,32,2048]{2,1,0:T(8,128)}, f32[2,16,2048]{2,1,0:T(8,128)S(1)}) custom-call(f32[22,8,128]{2,1,0:T(8,128)S(1)} %get-tuple-element.81.refs_0_.table.refs_1_, f32[16,2048]{1,0:T(8,128)S(1)} %get-tuple-element.164.refs_1_, f32[16,2048]{1,0:T(8,128)S(1)} %get-tuple-element.163.refs_2_, f32[16,32,2048]{2,1,0:T(8,128)} %refs_3_.5), custom_call_target="tpu_custom_call" | custom-call | flops 15728640 | bytes 1572864 | tf_op jit(solution)/shard_map/pallas_call | solution.py:432
  19.4 2.7 %collective-permute-start.5 = (f32[2,4,2048]{2,1,0:T(4,128)S(1)}, f32[2,4,2048]{2,1,0:T(4,128)S(1)}, u32[]{:S(2)}, u32[]{:S(2)}) collective-permute-start(f32[2,4,2048]{2,1,0:T(4,128)S(1)} %pad_maximum_fusion.10), channel_id=1, source_target_pairs={{0,16},{2,18},{4,20},{6,22},{8,24},{10,26},{12,28},{14,30},{16,0},... | collective-permute-start | bytes 196616 | tf_op jit(solution)/shard_map/ppermute | solution.py:467
  22.1 3.3 %shard_map.39 = (f32[16,32,2048]{2,1,0:T(8,128)}, f32[2,16,2048]{2,1,0:T(8,128)S(1)}) custom-call(f32[22,8,128]{2,1,0:T(8,128)S(1)} %get-tuple-element.81.refs_0_.table.refs_1_, f32[16,2048]{1,0:T(8,128)S(1)} %get-tuple-element.164.refs_1_, f32[16,2048]{1,0:T(8,128)S(1)} %get-tuple-element.163.refs_2_, ...), custom_call_target="tpu_custom_call", output_to_operand_aliasing={{0}: (4, {})} | custom-call | flops 10485760 | bytes 1048576 | tf_op jit(solution)/shard_map/pallas_call | solution.py:432
  25.6 0.1 add_select_fusion.29
  25.7 1.6 %collective-permute-start.7 = (f32[2,4,2048]{2,1,0:T(4,128)S(1)}, f32[2,4,2048]{2,1,0:T(4,128)S(1)}, u32[]{:S(2)}, u32[]{:S(2)}) collective-permute-start(f32[2,4,2048]{2,1,0:T(4,128)S(1)} %pad_maximum_fusion.12), channel_id=1, source_target_pairs={{0,8},{2,10},{4,12},{6,14},{8,0},{10,2},{12,4},{14,6},{16,24},{18,... | collective-permute-start | bytes 196616 | tf_op jit(solution)/shard_map/ppermute | solution.py:467
  27.4 1.4 %collective-permute-start.8 = (f32[2,4,2048]{2,1,0:T(4,128)S(1)}, f32[2,4,2048]{2,1,0:T(4,128)S(1)}, u32[]{:S(2)}, u32[]{:S(2)}) collective-permute-start(f32[2,4,2048]{2,1,0:T(4,128)S(1)} %pad_maximum_fusion.13), channel_id=1, source_target_pairs={{0,12},{2,14},{4,8},{6,10},{8,4},{10,6},{12,0},{14,2},{16,28},{18,... | collective-permute-start | bytes 196616 | tf_op jit(solution)/shard_map/ppermute | solution.py:467
  28.8 0.6 collective-permute-start.6
  29.4 4.1 %shard_map.40 = (f32[16,32,2048]{2,1,0:T(8,128)}, f32[2,16,2048]{2,1,0:T(8,128)S(1)}) custom-call(f32[22,8,128]{2,1,0:T(8,128)S(1)} %get-tuple-element.81.refs_0_.table.refs_1_, f32[16,2048]{1,0:T(8,128)S(1)} %get-tuple-element.164.refs_1_, f32[16,2048]{1,0:T(8,128)S(1)} %get-tuple-element.163.refs_2_, ...), custom_call_target="tpu_custom_call", output_to_operand_aliasing={{0}: (4, {})} | custom-call | flops 15728640 | bytes 1572864 | tf_op jit(solution)/shard_map/pallas_call | solution.py:432
  33.7 0.1 pad_maximum_fusion.4
  33.7 0.1 add_select_fusion.5
  33.9 0.1 collective-permute-start.9
  34.0 1.5 %collective-permute-done.9.other_ref.refs_3_ = f32[2,16,2048]{2,1,0:T(8,128)S(1)} collective-permute-done((f32[2,16,2048]{2,1,0:T(8,128)S(1)}, f32[2,16,2048]{2,1,0:T(8,128)S(1)}, u32[]{:S(2)}, u32[]{:S(2)}) %collective-permute-start.9) | collective-permute-done | bytes 262176 | tf_op jit(solution)/shard_map/ppermute | solution.py:467
  35.6 0.6 collective-permute-start.10
  36.2 4.1 %shard_map.41 = f32[2,32,2048]{2,1,0:T(8,128)S(1)} custom-call(s32[1]{0:T(128)} %bitcast.half_ref.refs_0_, f32[22,8,128]{2,1,0:T(8,128)S(1)} %get-tuple-element.81.refs_0_.table.refs_1_, f32[2,16,2048]{2,1,0:T(8,128)S(1)} %pad_maximum_fusion.2.own_ref.refs_2_, f32[2,16,2048]{2,1,0:T(8,128)S(1)} %collective-permute-done.9.other_ref.refs_3_, ...), custom_call_target="tpu_custom_call" | custom-call | flops 16777216 | bytes 4194304 | tf_op jit(solution)/shard_map/pallas_call | solution.py:396
  40.3 0.9 %collective-permute-done.10 = f32[16,2048]{1,0:T(8,128)S(1)} collective-permute-done((f32[16,2048]{1,0:T(8,128)S(1)}, f32[16,2048]{1,0:T(8,128)S(1)}, u32[]{:S(2)}, u32[]{:S(2)}) %collective-permute-start.10) | collective-permute-done | bytes 131104 | tf_op jit(solution)/shard_map/ppermute | solution.py:556
  41.2 0.1 multiply_reduce_fusion.1
  41.3 0.1 select_subtract_fusion
  41.5 0.1 collective-permute-start.11
  41.6 1.5 %collective-permute-done.11 = f32[2,16,2048]{2,1,0:T(8,128)S(1)} collective-permute-done((f32[2,16,2048]{2,1,0:T(8,128)S(1)}, f32[2,16,2048]{2,1,0:T(8,128)S(1)}, u32[]{:S(2)}, u32[]{:S(2)}) %collective-permute-start.11) | collective-permute-done | bytes 262176 | tf_op jit(solution)/shard_map/ppermute | solution.py:467
  43.2 0.1 fusion.9
  43.2 2.6 %collective-permute-start.14 = (f32[2,4,2048]{2,1,0:T(4,128)S(1)}, f32[2,4,2048]{2,1,0:T(4,128)S(1)}, u32[]{:S(2)}, u32[]{:S(2)}) collective-permute-start(f32[2,4,2048]{2,1,0:T(4,128)S(1)} %get-tuple-element.145), channel_id=1, source_target_pairs={{0,12},{2,14},{4,8},{6,10},{8,4},{10,6},{12,0},{14,2},{16,28},{18,... | collective-permute-start | bytes 196616 | tf_op jit(solution)/shard_map/ppermute | solution.py:467
  45.8 0.5 collective-permute-start.12
  46.3 0.4 collective-permute-start.13
  46.8 4.7 %shard_map.42 = (f32[16,32,2048]{2,1,0:T(8,128)}, f32[2,16,2048]{2,1,0:T(8,128)}) custom-call(s32[1]{0:T(128)} %bitcast.half_ref.refs_0_, f32[22,8,128]{2,1,0:T(8,128)S(1)} %get-tuple-element.81.refs_0_.table.refs_1_, f32[2,16,2048]{2,1,0:T(8,128)S(1)} %pad_maximum_fusion.2.own_ref.refs_2_, f32[2,16,2048]{2,1,0:T(8,128)S(1)} %collective-permute-done.9.other_ref.refs_3_, ...), custom_call_target="tpu_custom_call" | custom-call | flops 15728640 | bytes 1572864 | tf_op jit(solution)/shard_map/pallas_call | solution.py:432
  51.6 2.2 %collective-permute-start.15 = (f32[2,4,2048]{2,1,0:T(4,128)S(1)}, f32[2,4,2048]{2,1,0:T(4,128)S(1)}, u32[]{:S(2)}, u32[]{:S(2)}) collective-permute-start(f32[2,4,2048]{2,1,0:T(4,128)S(1)} %pad_maximum_fusion.14), channel_id=1, source_target_pairs={{0,16},{2,18},{4,20},{6,22},{8,24},{10,26},{12,28},{14,30},{16,0},... | collective-permute-start | bytes 196616 | tf_op jit(solution)/shard_map/ppermute | solution.py:467
  53.8 4.1 %shard_map.43 = (f32[16,32,2048]{2,1,0:T(8,128)}, f32[2,16,2048]{2,1,0:T(8,128)}) custom-call(s32[1]{0:T(128)} %bitcast.half_ref.refs_0_, f32[22,8,128]{2,1,0:T(8,128)S(1)} %get-tuple-element.81.refs_0_.table.refs_1_, f32[2,16,2048]{2,1,0:T(8,128)S(1)} %pad_maximum_fusion.2.own_ref.refs_2_, ...), custom_call_target="tpu_custom_call", output_to_operand_aliasing={{0}: (7, {})} | custom-call | flops 10485760 | bytes 1048576 | tf_op jit(solution)/shard_map/pallas_call | solution.py:432
  58.1 0.1 add_select_fusion.15
  58.2 1.9 %collective-permute-start.17 = (f32[2,4,2048]{2,1,0:T(4,128)S(1)}, f32[2,4,2048]{2,1,0:T(4,128)S(1)}, u32[]{:S(2)}, u32[]{:S(2)}) collective-permute-start(f32[2,4,2048]{2,1,0:T(4,128)S(1)} %pad_maximum_fusion.16), channel_id=1, source_target_pairs={{0,8},{2,10},{4,12},{6,14},{8,0},{10,2},{12,4},{14,6},{16,24},{18,... | collective-permute-start | bytes 196616 | tf_op jit(solution)/shard_map/ppermute | solution.py:467
  60.1 1.0 %collective-permute-start.18 = (f32[2,4,2048]{2,1,0:T(4,128)S(1)}, f32[2,4,2048]{2,1,0:T(4,128)S(1)}, u32[]{:S(2)}, u32[]{:S(2)}) collective-permute-start(f32[2,4,2048]{2,1,0:T(4,128)S(1)} %pad_maximum_fusion.17), channel_id=1, source_target_pairs={{0,12},{2,14},{4,8},{6,10},{8,4},{10,6},{12,0},{14,2},{16,28},{18,... | collective-permute-start | bytes 196616 | tf_op jit(solution)/shard_map/ppermute | solution.py:467
  61.1 0.8 %collective-permute-start.16 = (f32[2,4,2048]{2,1,0:T(4,128)S(1)}, f32[2,4,2048]{2,1,0:T(4,128)S(1)}, u32[]{:S(2)}, u32[]{:S(2)}) collective-permute-start(f32[2,4,2048]{2,1,0:T(4,128)S(1)} %pad_maximum_fusion.15), channel_id=1, source_target_pairs={{0,4},{2,6},{4,0},{6,2},{8,12},{10,14},{12,8},{14,10},{16,20},{18,... | collective-permute-start | bytes 196616 | tf_op jit(solution)/shard_map/ppermute | solution.py:467
  61.9 4.9 %shard_map.44 = (f32[16,32,2048]{2,1,0:T(8,128)}, f32[2,16,2048]{2,1,0:T(8,128)}) custom-call(s32[1]{0:T(128)} %bitcast.half_ref.refs_0_, f32[22,8,128]{2,1,0:T(8,128)S(1)} %get-tuple-element.81.refs_0_.table.refs_1_, f32[2,16,2048]{2,1,0:T(8,128)S(1)} %pad_maximum_fusion.2.own_ref.refs_2_, ...), custom_call_target="tpu_custom_call", output_to_operand_aliasing={{0}: (7, {})} | custom-call | flops 15728640 | bytes 1572864 | tf_op jit(solution)/shard_map/pallas_call | solution.py:432
  66.9 0.1 pad_maximum_fusion.6
  67.0 0.1 pad_maximum_fusion.7
  67.2 0.1 collective-permute-start.19
  67.3 1.5 %collective-permute-done.19.other_ref = f32[2,16,2048]{2,1,0:T(8,128)S(1)} collective-permute-done((f32[2,16,2048]{2,1,0:T(8,128)S(1)}, f32[2,16,2048]{2,1,0:T(8,128)S(1)}, u32[]{:S(2)}, u32[]{:S(2)}) %collective-permute-start.19) | collective-permute-done | bytes 262176 | tf_op jit(solution)/shard_map/ppermute | solution.py:467
  68.8 3.5 %shard_map.45 = f32[16,32,2048]{2,1,0:T(8,128)} custom-call(s32[1]{0:T(128)} %bitcast.half_ref.refs_0_, f32[22,8,128]{2,1,0:T(8,128)S(1)} %get-tuple-element.81.refs_0_.table.refs_1_, f32[2,16,2048]{2,1,0:T(8,128)S(1)} %pad_maximum_fusion.8.own_ref, f32[2,16,2048]{2,1,0:T(8,128)S(1)} %collective-permute-done.19.other_ref, ...), custom_call_target="tpu_custom_call" | custom-call | flops 6291456 | bytes 4194304 | tf_op jit(solution)/shard_map/pallas_call | solution.py:448
  (59 shorter events, 1.2 us)
Async XLA Ops:
  1.8 7.9 %collective-permute-start = (f32[16,2048]{1,0:T(8,128)S(1)}, f32[16,2048]{1,0:T(8,128)S(1)}, u32[]{:S(2)}, u32[]{:S(2)}) collective-permute-start(f32[16,2048]{1,0:T(8,128)S(1)} %fusion.5), channel_id=1, source_target_pairs={{0,1},{1,0},{2,3},{3,2},{4,5},{5,4},{6,7},{7,6},{8,9},{9,8},{10,11... | collective-permute-start | bytes 393224 | tf_op jit(solution)/shard_map/ppermute | solution.py:556
  10.0 1.6 %collective-permute-start.1 = (f32[2,16,2048]{2,1,0:T(8,128)S(1)}, f32[2,16,2048]{2,1,0:T(8,128)S(1)}, u32[]{:S(2)}, u32[]{:S(2)}) collective-permute-start(f32[2,16,2048]{2,1,0:T(8,128)S(1)} %constant_dynamic-slice_fusion.1), channel_id=1, source_target_pairs={{0,2},{2,0},{4,6},{6,4},{8,10},{10,8},{12,14},{14,12},{16,18},{18,... | collective-permute-start | bytes 786440 | tf_op jit(solution)/shard_map/ppermute | solution.py:467
  11.8 7.6 %collective-permute-start.4 = (f32[2,4,2048]{2,1,0:T(4,128)S(1)}, f32[2,4,2048]{2,1,0:T(4,128)S(1)}, u32[]{:S(2)}, u32[]{:S(2)}) collective-permute-start(f32[2,4,2048]{2,1,0:T(4,128)S(1)} %get-tuple-element.153), channel_id=1, source_target_pairs={{0,12},{2,14},{4,8},{6,10},{8,4},{10,6},{12,0},{14,2},{16,28},{18,... | collective-permute-start | bytes 196616 | tf_op jit(solution)/shard_map/ppermute | solution.py:467
  14.3 5.0 %collective-permute-start.2 = (f32[2,4,2048]{2,1,0:T(4,128)S(1)}, f32[2,4,2048]{2,1,0:T(4,128)S(1)}, u32[]{:S(2)}, u32[]{:S(2)}) collective-permute-start(f32[2,4,2048]{2,1,0:T(4,128)S(1)} %get-tuple-element.154), channel_id=1, source_target_pairs={{0,4},{2,6},{4,0},{6,2},{8,12},{10,14},{12,8},{14,10},{16,20},{18,... | collective-permute-start | bytes 196616 | tf_op jit(solution)/shard_map/ppermute | solution.py:467
  14.9 4.5 %collective-permute-start.3 = (f32[2,4,2048]{2,1,0:T(4,128)S(1)}, f32[2,4,2048]{2,1,0:T(4,128)S(1)}, u32[]{:S(2)}, u32[]{:S(2)}) collective-permute-start(f32[2,4,2048]{2,1,0:T(4,128)S(1)} %get-tuple-element.155), channel_id=1, source_target_pairs={{0,8},{2,10},{4,12},{6,14},{8,0},{10,2},{12,4},{14,6},{16,24},{18,... | collective-permute-start | bytes 196616 | tf_op jit(solution)/shard_map/ppermute | solution.py:467
  19.4 6.0 %collective-permute-start.5 = (f32[2,4,2048]{2,1,0:T(4,128)S(1)}, f32[2,4,2048]{2,1,0:T(4,128)S(1)}, u32[]{:S(2)}, u32[]{:S(2)}) collective-permute-start(f32[2,4,2048]{2,1,0:T(4,128)S(1)} %pad_maximum_fusion.10), channel_id=1, source_target_pairs={{0,16},{2,18},{4,20},{6,22},{8,24},{10,26},{12,28},{14,30},{16,0},... | collective-permute-start | bytes 196616 | tf_op jit(solution)/shard_map/ppermute | solution.py:467
  25.7 7.8 %collective-permute-start.7 = (f32[2,4,2048]{2,1,0:T(4,128)S(1)}, f32[2,4,2048]{2,1,0:T(4,128)S(1)}, u32[]{:S(2)}, u32[]{:S(2)}) collective-permute-start(f32[2,4,2048]{2,1,0:T(4,128)S(1)} %pad_maximum_fusion.12), channel_id=1, source_target_pairs={{0,8},{2,10},{4,12},{6,14},{8,0},{10,2},{12,4},{14,6},{16,24},{18,... | collective-permute-start | bytes 196616 | tf_op jit(solution)/shard_map/ppermute | solution.py:467
  27.4 6.2 %collective-permute-start.8 = (f32[2,4,2048]{2,1,0:T(4,128)S(1)}, f32[2,4,2048]{2,1,0:T(4,128)S(1)}, u32[]{:S(2)}, u32[]{:S(2)}) collective-permute-start(f32[2,4,2048]{2,1,0:T(4,128)S(1)} %pad_maximum_fusion.13), channel_id=1, source_target_pairs={{0,12},{2,14},{4,8},{6,10},{8,4},{10,6},{12,0},{14,2},{16,28},{18,... | collective-permute-start | bytes 196616 | tf_op jit(solution)/shard_map/ppermute | solution.py:467
  28.8 4.7 %collective-permute-start.6 = (f32[2,4,2048]{2,1,0:T(4,128)S(1)}, f32[2,4,2048]{2,1,0:T(4,128)S(1)}, u32[]{:S(2)}, u32[]{:S(2)}) collective-permute-start(f32[2,4,2048]{2,1,0:T(4,128)S(1)} %pad_maximum_fusion.11), channel_id=1, source_target_pairs={{0,4},{2,6},{4,0},{6,2},{8,12},{10,14},{12,8},{14,10},{16,20},{18,... | collective-permute-start | bytes 196616 | tf_op jit(solution)/shard_map/ppermute | solution.py:467
  33.9 1.6 %collective-permute-start.9 = (f32[2,16,2048]{2,1,0:T(8,128)S(1)}, f32[2,16,2048]{2,1,0:T(8,128)S(1)}, u32[]{:S(2)}, u32[]{:S(2)}) collective-permute-start(f32[2,16,2048]{2,1,0:T(8,128)S(1)} %pad_maximum_fusion.5), channel_id=1, source_target_pairs={{0,2},{2,0},{4,6},{6,4},{8,10},{10,8},{12,14},{14,12},{16,18},{18,... | collective-permute-start | bytes 786440 | tf_op jit(solution)/shard_map/ppermute | solution.py:467
  35.6 5.6 %collective-permute-start.10 = (f32[16,2048]{1,0:T(8,128)S(1)}, f32[16,2048]{1,0:T(8,128)S(1)}, u32[]{:S(2)}, u32[]{:S(2)}) collective-permute-start(f32[16,2048]{1,0:T(8,128)S(1)} %fusion.2), channel_id=1, source_target_pairs={{0,1},{1,0},{2,3},{3,2},{4,5},{5,4},{6,7},{7,6},{8,9},{9,8},{10,11... | collective-permute-start | bytes 393224 | tf_op jit(solution)/shard_map/ppermute | solution.py:556
  41.5 1.6 %collective-permute-start.11 = (f32[2,16,2048]{2,1,0:T(8,128)S(1)}, f32[2,16,2048]{2,1,0:T(8,128)S(1)}, u32[]{:S(2)}, u32[]{:S(2)}) collective-permute-start(f32[2,16,2048]{2,1,0:T(8,128)S(1)} %constant_dynamic-slice_fusion), channel_id=1, source_target_pairs={{0,2},{2,0},{4,6},{6,4},{8,10},{10,8},{12,14},{14,12},{16,18},{18,... | collective-permute-start | bytes 786440 | tf_op jit(solution)/shard_map/ppermute | solution.py:467
  43.2 8.3 %collective-permute-start.14 = (f32[2,4,2048]{2,1,0:T(4,128)S(1)}, f32[2,4,2048]{2,1,0:T(4,128)S(1)}, u32[]{:S(2)}, u32[]{:S(2)}) collective-permute-start(f32[2,4,2048]{2,1,0:T(4,128)S(1)} %get-tuple-element.145), channel_id=1, source_target_pairs={{0,12},{2,14},{4,8},{6,10},{8,4},{10,6},{12,0},{14,2},{16,28},{18,... | collective-permute-start | bytes 196616 | tf_op jit(solution)/shard_map/ppermute | solution.py:467
  45.8 5.7 %collective-permute-start.12 = (f32[2,4,2048]{2,1,0:T(4,128)S(1)}, f32[2,4,2048]{2,1,0:T(4,128)S(1)}, u32[]{:S(2)}, u32[]{:S(2)}) collective-permute-start(f32[2,4,2048]{2,1,0:T(4,128)S(1)} %get-tuple-element.146), channel_id=1, source_target_pairs={{0,4},{2,6},{4,0},{6,2},{8,12},{10,14},{12,8},{14,10},{16,20},{18,... | collective-permute-start | bytes 196616 | tf_op jit(solution)/shard_map/ppermute | solution.py:467
  46.3 5.2 %collective-permute-start.13 = (f32[2,4,2048]{2,1,0:T(4,128)S(1)}, f32[2,4,2048]{2,1,0:T(4,128)S(1)}, u32[]{:S(2)}, u32[]{:S(2)}) collective-permute-start(f32[2,4,2048]{2,1,0:T(4,128)S(1)} %get-tuple-element.147), channel_id=1, source_target_pairs={{0,8},{2,10},{4,12},{6,14},{8,0},{10,2},{12,4},{14,6},{16,24},{18,... | collective-permute-start | bytes 196616 | tf_op jit(solution)/shard_map/ppermute | solution.py:467
  51.6 6.3 %collective-permute-start.15 = (f32[2,4,2048]{2,1,0:T(4,128)S(1)}, f32[2,4,2048]{2,1,0:T(4,128)S(1)}, u32[]{:S(2)}, u32[]{:S(2)}) collective-permute-start(f32[2,4,2048]{2,1,0:T(4,128)S(1)} %pad_maximum_fusion.14), channel_id=1, source_target_pairs={{0,16},{2,18},{4,20},{6,22},{8,24},{10,26},{12,28},{14,30},{16,0},... | collective-permute-start | bytes 196616 | tf_op jit(solution)/shard_map/ppermute | solution.py:467
  58.2 8.7 %collective-permute-start.17 = (f32[2,4,2048]{2,1,0:T(4,128)S(1)}, f32[2,4,2048]{2,1,0:T(4,128)S(1)}, u32[]{:S(2)}, u32[]{:S(2)}) collective-permute-start(f32[2,4,2048]{2,1,0:T(4,128)S(1)} %pad_maximum_fusion.16), channel_id=1, source_target_pairs={{0,8},{2,10},{4,12},{6,14},{8,0},{10,2},{12,4},{14,6},{16,24},{18,... | collective-permute-start | bytes 196616 | tf_op jit(solution)/shard_map/ppermute | solution.py:467
  60.1 6.8 %collective-permute-start.18 = (f32[2,4,2048]{2,1,0:T(4,128)S(1)}, f32[2,4,2048]{2,1,0:T(4,128)S(1)}, u32[]{:S(2)}, u32[]{:S(2)}) collective-permute-start(f32[2,4,2048]{2,1,0:T(4,128)S(1)} %pad_maximum_fusion.17), channel_id=1, source_target_pairs={{0,12},{2,14},{4,8},{6,10},{8,4},{10,6},{12,0},{14,2},{16,28},{18,... | collective-permute-start | bytes 196616 | tf_op jit(solution)/shard_map/ppermute | solution.py:467
  61.1 5.7 %collective-permute-start.16 = (f32[2,4,2048]{2,1,0:T(4,128)S(1)}, f32[2,4,2048]{2,1,0:T(4,128)S(1)}, u32[]{:S(2)}, u32[]{:S(2)}) collective-permute-start(f32[2,4,2048]{2,1,0:T(4,128)S(1)} %pad_maximum_fusion.15), channel_id=1, source_target_pairs={{0,4},{2,6},{4,0},{6,2},{8,12},{10,14},{12,8},{14,10},{16,20},{18,... | collective-permute-start | bytes 196616 | tf_op jit(solution)/shard_map/ppermute | solution.py:467
  67.2 1.6 %collective-permute-start.19 = (f32[2,16,2048]{2,1,0:T(8,128)S(1)}, f32[2,16,2048]{2,1,0:T(8,128)S(1)}, u32[]{:S(2)}, u32[]{:S(2)}) collective-permute-start(f32[2,16,2048]{2,1,0:T(8,128)S(1)} %pad_maximum_fusion.9), channel_id=1, source_target_pairs={{0,2},{2,0},{4,6},{6,4},{8,10},{10,8},{12,14},{14,12},{16,18},{18,... | collective-permute-start | bytes 786440 | tf_op jit(solution)/shard_map/ppermute | solution.py:467

commit v4 on v3

--- a/solution.py
+++ b/solution.py
@@ -8,12 +8,12 @@
 from jax.sharding import PartitionSpec as P
 
 NZ = 32
-ITERS = 2
 
 LANES = 128
 ROWS = 8
 TILE = (ROWS, LANES)
 UNROLL = 4
+PARTS = 3
 
 DECAY, SCALE, LINEAR, SQUARE, CUBE, KEEP, WEIGHTS = range(7)
 
@@ -104,8 +104,8 @@
     return r * (p + q), r * (p - q)
 
 
-def entered_pair(table, both, old, k, i, lanes):
-    v, w = old[k, rows_of(i), lanes], old[old.shape[0] - 1 - k, rows_of(i), lanes]
+def entered_pair(table, both, old, k, i, place):
+    v, w = old[k, rows_of(i), place], old[old.shape[0] - 1 - k, rows_of(i), place]
     if both is None:
         return v, w
     even, odd = table[WEIGHTS + 2 * k] * both[0], table[WEIGHTS + 2 * k + 1] * both[1]
@@ -163,62 +163,63 @@
     ref[:, :, width - LANES :] = guard
 
 
-def lane_parts(width, parts):
-    part = width // parts
-    return [slice(n * part, (n + 1) * part) for n in range(parts)]
-
-
-def tiles_of(lanes):
-    return lanes.start // LANES, lanes.stop // LANES
-
-
-def start_reads(source, target, parts, sems, offset=0):
+def bounds_of(width):
+    tiles = width // LANES
+    return [0, 3 * tiles // 8, 5 * tiles // 8, tiles]
+
+
+def pieces_of(width):
+    bounds = bounds_of(width)
+    return list(zip(bounds, bounds[1:]))
+
+
+def lanes_of(first, last):
+    return slice(first * LANES, last * LANES)
+
+
+def sum_parts(table, enter, source, ends_ref, old, sums, sems, prepare):
+    tiles = ends_ref.shape[-1] // LANES
+    count = sems.shape[0]
     reads = []
-    for n, lanes in enumerate(parts):
-        there = slice(lanes.start + offset, lanes.stop + offset)
-        reads.append(pltpu.make_async_copy(source.at[:, :, lanes], target.at[:, :, there], sems.at[n]))
-        reads[-1].start()
-    return reads
-
-
-def sum_parts(table, enter, old_ref, old, ends_ref, sums, parts, reads):
-    for lanes, read in zip(parts, reads):
+    for n in range(count):
+        part = n * tiles // count, (n + 1) * tiles // count
+        lanes = lanes_of(*part)
+        reads.append((part, pltpu.make_async_copy(source.at[:, :, lanes], old.at[:, :, lanes], sems.at[n])))
+        reads[-1][1].start()
+    clear_guards(sums)
+    prepare()
+    for part, read in reads:
         read.wait()
-        sum_tiles(table, enter, old, ends_ref, sums, tiles_of(lanes))
+        sum_tiles(table, enter, old, ends_ref, sums, part)
     finish_sums(table, ends_ref, sums)
 
 
 def first_sums_kernel(
     levels, step_ref, mass_ref, old_ref, ends_ref, table, planes_ref, arcs_ref, old, sums, sems
 ):
-    parts = lane_parts(old.shape[-1], sems.shape[0])
-    reads = start_reads(old_ref, old, parts, sems)
-    clear_guards(sums)
-    values = step_ref[0], mass_ref[0]
-    fill_table(values, table, old.shape[0])
-    fill_wide(values, planes_ref, arcs_ref, levels)
-    sum_parts(table, None, old_ref, old, ends_ref, sums, parts, reads)
+    def prepare():
+        values = step_ref[0], mass_ref[0]
+        fill_table(values, table, old.shape[0])
+        fill_wide(values, planes_ref, arcs_ref, levels)
+
+    sum_parts(table, None, old_ref, ends_ref, old, sums, sems, prepare)
 
 
 def next_sums_kernel(half_ref, table, own_ref, other_ref, old_ref, ends_ref, old, sums, sems):
-    parts = lane_parts(old.shape[-1], sems.shape[0])
-    reads = start_reads(old_ref, old, parts, sems)
-    clear_guards(sums)
-    blocks = old.shape[1] // ROWS
+    blocks = ends_ref.shape[1] // ROWS
 
     def enter(i, lanes):
         return entering_tile(table, half_ref, own_ref, other_ref, i, blocks, lanes)
 
-    sum_parts(table, enter, old_ref, old, ends_ref, sums, parts, reads)
-
-
-def relax_tiles(table, masks, phi, low_ref, high_ref, stage, edges_ref, tiles):
-    slices, planes, _ = stage.shape
+    sum_parts(table, enter, old_ref, ends_ref, old, sums, sems, lambda: None)
+
+
+def relax_tiles(table, masks, phi, low_ref, high_ref, psi_ref, edges_ref, tiles, start):
+    slices, planes, _ = phi.shape
     blocks = planes // ROWS
-    half = slices // 2
 
     def tile(j, carry):
-        lanes = tile_at(j)
+        lanes, place = tile_at(j), tile_at(j, -start * LANES)
         for i in range(blocks):
             at = lambda t, i, side: phi[t, rows_of(i), tile_at(j, (1 + side) * LANES)]
             force = [None] * slices
@@ -242,97 +243,102 @@
             for t in range(slices):
                 local = backward[t] if t == 0 else forward[t] + backward[t]
                 value = table[KEEP] * at(t, i, 0) - local
-                stage[t, rows_of(i), lanes] = value
+                psi_ref[t, rows_of(i), place] = value
                 if i == 0:
-                    edges_ref[0, t : t + 1, lanes] = value[:1]
+                    edges_ref[0, t : t + 1, place] = value[:1]
                 if i == blocks - 1:
-                    edges_ref[1, t : t + 1, lanes] = value[ROWS - 1 :]
+                    edges_ref[1, t : t + 1, place] = value[ROWS - 1 :]
         return carry
 
     lax.fori_loop(tiles[0], tiles[1], tile, 0, unroll=min(UNROLL, tiles[1] - tiles[0]))
 
 
-def relax_piece(table, enter, low_ref, high_ref, old_ref, psi_ref, edges_ref, phi, stage, old, in_sems, out_sems, tiles):
-    slices, planes, width = stage.shape
-    blocks = planes // ROWS
-    first, last = tiles
-    middle = (first + last) // 2
-    bounds = [max(first - 1, 0), middle + 1, min(last + 1, width // LANES)]
-    parts = [slice(a * LANES, b * LANES) for a, b in zip(bounds, bounds[1:])]
-    reads = start_reads(old_ref, old if enter else phi, parts, in_sems, 0 if enter else LANES)
+def reads_of(tiles, count, source, target, offset, sems):
+    width = source.shape[-1] // LANES
+    bounds = [max(tiles[0] - 1, 0)]
+    bounds += [tiles[0] + (tiles[1] - tiles[0]) * n // count + 1 for n in range(1, count)]
+    bounds += [min(tiles[1] + 1, width)]
+    reads = []
+    for n, part in enumerate(zip(bounds, bounds[1:])):
+        there = lanes_of(part[0] + offset, part[1] + offset)
+        reads.append(pltpu.make_async_copy(source.at[:, :, lanes_of(*part)], target.at[:, :, there], sems.at[n]))
+        reads[-1].start()
+    return bounds, reads
+
+
+def parts_of(tiles, count):
+    bounds = [tiles[0] + (tiles[1] - tiles[0]) * n // count for n in range(count + 1)]
+    return list(zip(bounds, bounds[1:]))
+
+
+def first_relax_kernel(tiles, ready, table, low_ref, high_ref, old_ref, *rest):
+    psi_ref, edges_ref, phi, stage, in_sems, out_sems = rest[-6:]
+    count = in_sems.shape[0]
+    _, reads = reads_of(tiles, count, old_ref, phi, 1, in_sems)
     clear_guards(phi)
     masks = Masks()
-
-    def arrive(n):
+    writes = []
+    for n, part in enumerate(parts_of(tiles, count)):
         reads[n].wait()
-        if not enter:
-            return
-
-        def tile(j, carry):
-            lanes, inner = tile_at(j), tile_at(j, LANES)
-            for i in range(blocks):
-                both = enter(i, lanes)
-                for k in range(slices // 2):
-                    v, w = entered_pair(table, both, old, k, i, lanes)
-                    phi[k, rows_of(i), inner] = v
-                    phi[slices - 1 - k, rows_of(i), inner] = w
-            return carry
-
-        lax.fori_loop(bounds[n], bounds[n + 1], tile, 0, unroll=True)
-
-    writes = []
-    for n, part in enumerate(((first, middle), (middle, last))):
-        arrive(n)
-        relax_tiles(table, masks, phi, low_ref, high_ref, stage, edges_ref, part)
-        lanes = slice(part[0] * LANES, part[1] * LANES)
-        writes.append(pltpu.make_async_copy(stage.at[:, :, lanes], psi_ref.at[:, :, lanes], out_sems.at[n]))
+        relax_tiles(table, masks, phi, low_ref, high_ref, stage, edges_ref, part, tiles[0])
+        here = lanes_of(part[0] - tiles[0], part[1] - tiles[0])
+        writes.append(
+            pltpu.make_async_copy(stage.at[:, :, here], psi_ref.at[:, :, lanes_of(*part)], out_sems.at[n])
+        )
         writes[-1].start()
     for write in writes:
         write.wait()
 
 
-def first_relax_kernel(tiles, table, low_ref, high_ref, old_ref, _, psi_ref, edges_ref, phi, stage, in_sems, out_sems):
-    relax_piece(
-        table, None, low_ref, high_ref, old_ref, psi_ref, edges_ref, phi, stage, None, in_sems, out_sems, tiles
-    )
-
-
 def next_relax_kernel(
-    tiles, half_ref, table, own_ref, other_ref, low_ref, high_ref, old_ref, _,
-    psi_ref, edges_ref, phi, stage, old, in_sems, out_sems,
+    tiles, ready, half_ref, table, own_ref, other_ref, low_ref, high_ref, old_ref, psi_ref, edges_ref, phi, old, sems
 ):
-    blocks = old.shape[1] // ROWS
-
-    def enter(i, lanes):
-        return entering_tile(table, half_ref, own_ref, other_ref, i, blocks, lanes)
-
-    relax_piece(
-        table, enter, low_ref, high_ref, old_ref, psi_ref, edges_ref, phi, stage, old, in_sems, out_sems, tiles
-    )
-
-
-def last_kernel(half_ref, table, own_ref, other_ref, old_ref, out_ref, old, stage, in_sems, out_sems):
-    slices, planes, width = old.shape
+    slices, planes, _ = phi.shape
     blocks = planes // ROWS
-    parts = lane_parts(width, in_sems.shape[0])
-    reads = start_reads(old_ref, old, parts, in_sems)
-    writes = []
+    count = sems.shape[0]
+    bounds, reads = reads_of(tiles, count, old_ref, old, 0, sems)
+    clear_guards(phi)
 
     def tile(j, carry):
-        lanes = tile_at(j)
+        lanes, inner = tile_at(j), tile_at(j, LANES)
         for i in range(blocks):
             both = entering_tile(table, half_ref, own_ref, other_ref, i, blocks, lanes)
             for k in range(slices // 2):
                 v, w = entered_pair(table, both, old, k, i, lanes)
-                stage[k, rows_of(i), lanes] = v
-                stage[slices - 1 - k, rows_of(i), lanes] = w
+                phi[k, rows_of(i), inner] = v
+                phi[slices - 1 - k, rows_of(i), inner] = w
         return carry
 
-    for n, lanes in enumerate(parts):
+    masks = Masks()
+    for n, part in enumerate(parts_of(tiles, count)):
         reads[n].wait()
-        lax.fori_loop(*tiles_of(lanes), tile, 0, unroll=UNROLL)
-        writes.append(pltpu.make_async_copy(stage.at[:, :, lanes], out_ref.at[:, :, lanes], out_sems.at[n]))
-        writes[-1].start()
+        lax.fori_loop(bounds[n], bounds[n + 1], tile, 0, unroll=True)
+        relax_tiles(table, masks, phi, low_ref, high_ref, psi_ref, edges_ref, part, tiles[0])
+
+
+def last_kernel(half_ref, table, own_ref, other_ref, *rest):
+    *olds, out_ref, stage, sems = rest
+    slices, planes, width = stage.shape
+    blocks = planes // ROWS
+    writes = []
+    for n, ((first, last), old) in enumerate(zip(pieces_of(width), olds)):
+        middle = (first + last) // 2
+
+        def tile(j, carry):
+            lanes = tile_at(j)
+            for i in range(blocks):
+                both = entering_tile(table, half_ref, own_ref, other_ref, i, blocks, lanes)
+                for k in range(slices // 2):
+                    v, w = entered_pair(table, both, old, k, i, tile_at(j, -first * LANES))
+                    stage[k, rows_of(i), lanes] = v
+                    stage[slices - 1 - k, rows_of(i), lanes] = w
+            return carry
+
+        for k, part in enumerate(((first, middle), (middle, last))):
+            lax.fori_loop(*part, tile, 0, unroll=True)
+            lanes = lanes_of(*part)
+            writes.append(pltpu.make_async_copy(stage.at[:, :, lanes], out_ref.at[:, :, lanes], sems.at[2 * n + k]))
+            writes[-1].start()
     for write in writes:
         write.wait()
 
@@ -359,13 +365,21 @@
     return pltpu.VMEM((lead, shape[1], shape[2] + 2 * LANES), jnp.float32)
 
 
-def parts_of(width):
-    return 4 if width % (4 * LANES) == 0 else 1
-
-
 def cost(shape, flops):
     size = shape[0] * shape[1] * shape[2]
     return pl.CostEstimate(flops=flops * size, bytes_accessed=4 * size, transcendentals=0)
+
+
+def vmem(shape):
+    return pltpu.VMEM(shape, jnp.float32)
+
+
+def in_vmem(array):
+    return pltpu.with_memory_space_constraint(array, pltpu.VMEM)
+
+
+def piece_shape(shape, piece):
+    return shape[0], shape[1], (piece[1] - piece[0]) * LANES
 
 
 def first_sums(step, mass, field, levels):
@@ -384,76 +398,75 @@
         scratch_shapes=[
             pltpu.VMEM(field.shape, jnp.float32),
             padded(2, field.shape),
-            pltpu.SemaphoreType.DMA((parts_of(width),)),
+            pltpu.SemaphoreType.DMA((4,)),
         ],
         compiler_params=PARAMS,
         cost_estimate=cost(field.shape, 12),
     )(step, mass, in_hbm(field))
 
 
-def next_sums(half, table, own, other, psi):
-    _, planes, width = psi.shape
+def next_sums(half, table, own, other, old):
+    _, planes, width = old.shape
     return pl.pallas_call(
         next_sums_kernel,
         in_specs=[SMEM] + [VMEM] * 3 + [HBM],
         out_shape=f32((2, planes, width)),
         out_specs=VMEM,
         scratch_shapes=[
-            pltpu.VMEM(psi.shape, jnp.float32),
-            padded(2, psi.shape),
-            pltpu.SemaphoreType.DMA((parts_of(width),)),
+            pltpu.VMEM(old.shape, jnp.float32),
+            padded(2, old.shape),
+            pltpu.SemaphoreType.DMA((4,)),
         ],
         compiler_params=PARAMS,
-        cost_estimate=cost(psi.shape, 16),
-    )(half, table, own, other, in_hbm(psi))
-
-
-def relax(tiles, terms, table, low, high, old, psi):
+        cost_estimate=cost(old.shape, 16),
+    )(half, table, own, other, in_hbm(old))
+
+
+def first_relax(tiles, ready, table, low, high, old, psi):
     slices, planes, width = old.shape
-    if terms:
-        half, own, other = terms
-        kernel, operands, specs = next_relax_kernel, [half, table, own, other], [SMEM] + [VMEM] * 3
-    else:
-        kernel, operands, specs = first_relax_kernel, [table], [VMEM]
-    operands += [low, high, in_hbm(old)]
-    specs += [VMEM, VMEM, HBM]
-    aliases = {}
-    if psi is not None:
-        operands.append(in_hbm(psi))
-        specs.append(HBM)
-        aliases = {len(operands) - 1: 0}
-
-    def body(*refs):
-        refs = list(refs)
-        if psi is None:
-            refs.insert(len(operands), None)
-        kernel(tiles, *refs)
-
+    piece = piece_shape(old.shape, tiles)
+    operands = [ready, table, low, high, in_hbm(old)] + ([] if psi is None else [in_hbm(psi)])
+    semaphores = pltpu.SemaphoreType.DMA((PARTS,))
     return pl.pallas_call(
-        body,
-        in_specs=specs,
-        out_shape=(hbm(old.shape), f32((2, slices, width))),
+        functools.partial(first_relax_kernel, tiles),
+        in_specs=[VMEM] * 4 + [HBM] * (len(operands) - 4),
+        out_shape=(hbm(old.shape), f32((2, slices, piece[-1]))),
         out_specs=(HBM, VMEM),
-        input_output_aliases=aliases,
-        scratch_shapes=[padded(slices, old.shape), pltpu.VMEM(old.shape, jnp.float32)]
-        + ([pltpu.VMEM(old.shape, jnp.float32)] if terms else [])
-        + [pltpu.SemaphoreType.DMA((2,))] * 2,
+        input_output_aliases={} if psi is None else {5: 0},
+        scratch_shapes=[padded(slices, old.shape), pltpu.VMEM(piece, jnp.float32), semaphores, semaphores],
         compiler_params=PARAMS,
-        cost_estimate=cost((slices, planes, (tiles[1] - tiles[0]) * LANES), 40),
+        cost_estimate=cost(piece, 40),
     )(*operands)
 
 
-def last_step(half, table, own, other, psi):
-    semaphores = pltpu.SemaphoreType.DMA((parts_of(psi.shape[-1]),))
+def next_relax(tiles, ready, half, own, other, table, low, high, old):
+    slices, planes, width = old.shape
+    piece = piece_shape(old.shape, tiles)
+    return pl.pallas_call(
+        functools.partial(next_relax_kernel, tiles),
+        in_specs=[VMEM, SMEM] + [VMEM] * 5 + [HBM],
+        out_shape=(vmem(piece), f32((2, slices, piece[-1]))),
+        out_specs=(VMEM, VMEM),
+        scratch_shapes=[
+            padded(slices, old.shape),
+            pltpu.VMEM(old.shape, jnp.float32),
+            pltpu.SemaphoreType.DMA((PARTS,)),
+        ],
+        compiler_params=PARAMS,
+        cost_estimate=cost(piece, 40),
+    )(ready, half, table, own, other, low, high, in_hbm(old))
+
+
+def last_step(shape, half, table, own, other, olds):
     return pl.pallas_call(
         last_kernel,
-        in_specs=[SMEM] + [VMEM] * 3 + [HBM],
-        out_shape=hbm(psi.shape),
+        in_specs=[SMEM] + [VMEM] * (3 + len(olds)),
+        out_shape=hbm(shape),
         out_specs=HBM,
-        scratch_shapes=[pltpu.VMEM(psi.shape, jnp.float32)] * 2 + [semaphores] * 2,
+        scratch_shapes=[pltpu.VMEM(shape, jnp.float32), pltpu.SemaphoreType.DMA((2 * len(olds),))],
         compiler_params=PARAMS,
-        cost_estimate=cost(psi.shape, 6),
-    )(half, table, own, other, in_hbm(psi))
+        cost_estimate=cost(shape, 6),
+    )(half, table, own, other, *map(in_vmem, olds))
 
 
 class Loop:
@@ -560,48 +573,44 @@
 
 
 def on_device(field, step, mass):
-    _, planes, width = field.shape
+    shape = _, planes, width = field.shape
     loop = Loop()
     sides = Planes(planes)
     half = (loop.me & 1).astype(jnp.int32).reshape(1)
-    tiles = width // LANES
-    bounds = [0, 3 * tiles // 8, 5 * tiles // 8, tiles]
-
-    def after(array, *others):
-        return lax.optimization_barrier((array, *others))[0]
-
-    old, terms = field, None
-    first, last = field[:, 0], field[:, -1]
-    for turn in range(ITERS):
-        low, high = sides.exchange(first, last)
-        if turn == 0:
-            ends, table, weights, arcs = first_sums(step, mass, old, loop.levels)
-        else:
-            ends = next_sums(half, table, *terms[1:], old)
+
+    pieces = pieces_of(width)
+
+    def edge_sums(ends, low, high):
         row = lax.broadcasted_iota(jnp.int32, (1, planes, 1), 1)
         for place, plane in ((0, low), (planes - 1, high)):
             sums = jnp.sum(weights[2:] * plane[None], axis=1)
             ends = ends - jnp.where(row == place, sums[:, None, :], 0.0)
-
-        def work(n, ready, state=None, old=old, terms=terms, low=low, high=high):
-            psi, edges = state or (None, [])
-            psi, more = relax(bounds[n : n + 2], terms, after(table, ready), low, high, old, psi)
-            return psi, edges + [more[..., bounds[n] * LANES : bounds[n + 1] * LANES]]
-
-        works = [functools.partial(work, n) for n in range(3)]
-        own, other, (old, edges) = loop.solve(ends, arcs, works)
-        terms = (half, own, other)
-        if turn < ITERS - 1:
-            edges = jnp.concatenate(edges, axis=2)
-            mine = half[0] == 0
-            first, last = (
-                edges[n] - weights[0] * flux[0] - weights[1] * flux[1]
-                for n, flux in (
-                    (0, jnp.where(mine, own[:, 0], other[:, 0])),
-                    (1, jnp.where(mine, other[:, -1], own[:, -1])),
-                )
-            )
-    return last_step(half, table, own, other, old)
+        return ends
+
+    low, high = sides.exchange(field[:, 0], field[:, -1])
+    ends, table, weights, arcs = first_sums(step, mass, field, loop.levels)
+
+    def first_work(tiles, ready, state=(None, ())):
+        psi, edge = first_relax(tiles, ready, table, low, high, field, state[0])
+        return psi, (*state[1], edge)
+
+    works = [functools.partial(first_work, tiles) for tiles in pieces]
+    own, other, (psi, edges) = loop.solve(edge_sums(ends, low, high), arcs, works)
+
+    edges = jnp.concatenate(edges, axis=2)
+    mine = half[0] == 0
+    fluxes = jnp.where(mine, own[:, 0], other[:, 0]), jnp.where(mine, other[:, -1], own[:, -1])
+    low, high = sides.exchange(
+        *(edge - weights[0] * flux[0] - weights[1] * flux[1] for edge, flux in zip(edges, fluxes))
+    )
+    ends = next_sums(half, table, own, other, psi)
+
+    def next_work(tiles, ready, state=(), own=own, other=other):
+        return *state, next_relax(tiles, ready, half, own, other, table, low, high, psi)[0]
+
+    works = [functools.partial(next_work, tiles) for tiles in pieces]
+    own, other, olds = loop.solve(edge_sums(ends, low, high), arcs, works)
+    return last_step(shape, half, table, own, other, olds)
 
 
 def solution(mesh):

time: 72.8 us -> 68.6 us (0.942)
  Pallas kernels: 36.4 us -> 31.9 us
    pallas_call x7, Pallas kernels: 28.7 us -> 24.2 us  [the longest x3 11.3 us: first_relax(): pl.pallas_call(functools.partial(first_relax_kernel, tiles), in_specs=[VM...]
    slice x4 -> x1, local copies, waits for them, and re-layouts: 1.75 us -> 1.73 us  [on_device(): low, high = sides.exchange(field[:, 0], field[:, -1])]
  transfers between devices with their start and end apart: 20 -> 20, of which waited for: 5 -> 5; matrix products, arithmetic and copies ran while one was open for 0% -> 0% of each run, Pallas kernels for 45% -> 43%
where the time goes in v4:
time: 68.6 us; the launch traced here: 68.3 us
  Pallas kernels  31.9 us (47%)
  starting transfers between devices  23.4 us (34%)
  waiting for transfers between devices  6.86 us (10%)
  other arithmetic  2.22 us (3%)
  between operations  2.02 us (3%)
  local copies, waits for them, and re-layouts  1.87 us (3%)
    ppermute x18, starting transfers between devices, swap(): lax.ppermute(array, 'tm', [(i, i ^ offset) for i in range(self.devices)])  19.8 us
    pallas_call x3, Pallas kernels, first_relax(): pl.pallas_call(functools.partial(first_relax_kernel, tiles), in_specs=[VM...  11.3 us
    pallas_call x3, Pallas kernels, next_relax(): pl.pallas_call(functools.partial(next_relax_kernel, tiles), in_specs=[VME...  10.7 us
    ppermute x18, waiting for transfers between devices, swap(): lax.ppermute(array, 'tm', [(i, i ^ offset) for i in range(self.devices)])  6.01 us
    pallas_call x1, Pallas kernels, next_sums(): pl.pallas_call(next_sums_kernel, in_specs=[SMEM] + [VMEM] * 3 + [HBM], ou...  4.15 us
    ppermute x2, starting transfers between devices, exchange(): lax.ppermute(given, 'space', [(i, i + 1) for i in pairs] + [(i + 1, i) fo...  3.6 us
    pallas_call x1, Pallas kernels, first_sums(): pl.pallas_call(functools.partial(first_sums_kernel, levels), in_specs=[SM...  3.52 us
    pallas_call x1, Pallas kernels, last_step(): pl.pallas_call(last_kernel, in_specs=[SMEM] + [VMEM] * (3 + len(olds)), o...  2.18 us
  transfers between devices with their start and end apart: 20, of which 5 were waited for; matrix products, arithmetic and copies ran while one was open for 0% of the time, Pallas kernels for 43%

profile of v4, /device:TPU:0, one launch (start us, length us, event | category | flops | bytes accessed | tf_op | source)
XLA Modules:
  0.0 68.3 jit_solution(4334458114287934829)
XLA Ops:
  0.0 1.7 %fusion.16 = (f32[16,1,2048]{2,1,0:T(1,128)S(1)}, f32[16,1,2048]{2,1,0:T(1,128)S(1)}) fusion(f32[16,32,2048]{2,1,0:T(8,128)} %old_ref.7), kind=kLoop, calls=%fused_computation.158 | loop fusion | bytes 524288 | tf_op jit(solution)/shard_map/slice | solution.py:590
  1.7 0.1 fusion.5
  1.8 3.0 %collective-permute-start = (f32[16,2048]{1,0:T(8,128)S(1)}, f32[16,2048]{1,0:T(8,128)S(1)}, u32[]{:S(2)}, u32[]{:S(2)}) collective-permute-start(f32[16,2048]{1,0:T(8,128)S(1)} %fusion.5), channel_id=1, source_target_pairs={{0,1},{1,0},{2,3},{3,2},{4,5},{5,4},{6,7},{7,6},{8,9},{9,8},{10,11... | collective-permute-start | bytes 393224 | tf_op jit(solution)/shard_map/ppermute | solution.py:569
  6.2 3.5 %shard_map.37 = (f32[2,32,2048]{2,1,0:T(8,128)S(1)}, f32[22,8,128]{2,1,0:T(8,128)S(1)}, f32[4,16,2048]{2,1,0:T(8,128)S(1)}, f32[8,2048]{1,0:T(8,128)S(1)}) custom-call(f32[1]{0:T(128)S(6)} %copy.18.step_ref, f32[1]{0:T(128)S(6)} %copy.19.mass_ref, f32[16,32,2048]{2,1,0:T(8,128)} %old_ref.7), custom_call_target="tpu_custom_call" | custom-call | flops 12582912 | bytes 4194304 | tf_op jit(solution)/shard_map/pallas_call | solution.py:388
  9.7 0.1 multiply_reduce_fusion.3
  9.9 0.1 select_subtract_fusion.1
  10.0 0.1 collective-permute-start.1
  10.1 0.1 fusion.17
  10.2 1.4 %collective-permute-done.1 = f32[2,16,2048]{2,1,0:T(8,128)S(1)} collective-permute-done((f32[2,16,2048]{2,1,0:T(8,128)S(1)}, f32[2,16,2048]{2,1,0:T(8,128)S(1)}, u32[]{:S(2)}, u32[]{:S(2)}) %collective-permute-start.1) | collective-permute-done | bytes 262176 | tf_op jit(solution)/shard_map/ppermute | solution.py:480
  11.7 0.1 fusion.13
  11.8 2.6 %collective-permute-start.4 = (f32[2,4,2048]{2,1,0:T(4,128)S(1)}, f32[2,4,2048]{2,1,0:T(4,128)S(1)}, u32[]{:S(2)}, u32[]{:S(2)}) collective-permute-start(f32[2,4,2048]{2,1,0:T(4,128)S(1)} %get-tuple-element.151), channel_id=1, source_target_pairs={{0,12},{2,14},{4,8},{6,10},{8,4},{10,6},{12,0},{14,2},{16,28},{18,... | collective-permute-start | bytes 196616 | tf_op jit(solution)/shard_map/ppermute | solution.py:480
  14.3 0.5 collective-permute-start.2
  14.9 0.4 collective-permute-start.3
  15.3 3.9 %shard_map.38 = (f32[16,32,2048]{2,1,0:T(8,128)}, f32[2,16,768]{2,1,0:T(8,128)S(1)}) custom-call(f32[2,16,2048]{2,1,0:T(8,128)S(1)} %pad_maximum_fusion.ready, f32[22,8,128]{2,1,0:T(8,128)S(1)} %get-tuple-element.47.table, f32[16,2048]{1,0:T(8,128)S(1)} %get-tuple-element.162.low_ref, f32[16,2048]{1,0:T(8,128)S(1)} %get-tuple-element.161.high_ref, ...), custom_call_target="tpu_custom_call" | custom-call | flops 15728640 | bytes 1572864 | tf_op jit(solution)/shard_map/pallas_call | solution.py:430
  19.4 2.7 %collective-permute-start.5 = (f32[2,4,2048]{2,1,0:T(4,128)S(1)}, f32[2,4,2048]{2,1,0:T(4,128)S(1)}, u32[]{:S(2)}, u32[]{:S(2)}) collective-permute-start(f32[2,4,2048]{2,1,0:T(4,128)S(1)} %pad_maximum_fusion.10.ready), channel_id=1, source_target_pairs={{0,16},{2,18},{4,20},{6,22},{8,24},{10,26},{12,28},{14,30},{16,0},... | collective-permute-start | bytes 196616 | tf_op jit(solution)/shard_map/ppermute | solution.py:480
  22.0 3.4 %shard_map.39 = (f32[16,32,2048]{2,1,0:T(8,128)}, f32[2,16,512]{2,1,0:T(8,128)S(1)}) custom-call(f32[2,4,2048]{2,1,0:T(4,128)S(1)} %pad_maximum_fusion.10.ready, f32[22,8,128]{2,1,0:T(8,128)S(1)} %get-tuple-element.47.table, f32[16,2048]{1,0:T(8,128)S(1)} %get-tuple-element.162.low_ref, ...), custom_call_target="tpu_custom_call", output_to_operand_aliasing={{0}: (5, {})} | custom-call | flops 10485760 | bytes 1048576 | tf_op jit(solution)/shard_map/pallas_call | solution.py:430
  25.6 0.1 add_select_fusion.29
  25.7 1.6 %collective-permute-start.7 = (f32[2,4,2048]{2,1,0:T(4,128)S(1)}, f32[2,4,2048]{2,1,0:T(4,128)S(1)}, u32[]{:S(2)}, u32[]{:S(2)}) collective-permute-start(f32[2,4,2048]{2,1,0:T(4,128)S(1)} %pad_maximum_fusion.12), channel_id=1, source_target_pairs={{0,8},{2,10},{4,12},{6,14},{8,0},{10,2},{12,4},{14,6},{16,24},{18,... | collective-permute-start | bytes 196616 | tf_op jit(solution)/shard_map/ppermute | solution.py:480
  27.3 1.4 %collective-permute-start.8 = (f32[2,4,2048]{2,1,0:T(4,128)S(1)}, f32[2,4,2048]{2,1,0:T(4,128)S(1)}, u32[]{:S(2)}, u32[]{:S(2)}) collective-permute-start(f32[2,4,2048]{2,1,0:T(4,128)S(1)} %pad_maximum_fusion.13), channel_id=1, source_target_pairs={{0,12},{2,14},{4,8},{6,10},{8,4},{10,6},{12,0},{14,2},{16,28},{18,... | collective-permute-start | bytes 196616 | tf_op jit(solution)/shard_map/ppermute | solution.py:480
  28.8 0.6 collective-permute-start.6
  29.4 4.0 %shard_map.40 = (f32[16,32,2048]{2,1,0:T(8,128)}, f32[2,16,768]{2,1,0:T(8,128)S(1)}) custom-call(f32[2,4,2048]{2,1,0:T(4,128)S(1)} %pad_maximum_fusion.14.ready, f32[22,8,128]{2,1,0:T(8,128)S(1)} %get-tuple-element.47.table, f32[16,2048]{1,0:T(8,128)S(1)} %get-tuple-element.162.low_ref, ...), custom_call_target="tpu_custom_call", output_to_operand_aliasing={{0}: (5, {})} | custom-call | flops 15728640 | bytes 1572864 | tf_op jit(solution)/shard_map/pallas_call | solution.py:430
  33.5 0.1 pad_maximum_fusion.3
  33.6 0.1 pad_maximum_fusion.4
  33.7 0.1 collective-permute-start.9
  33.9 1.5 %collective-permute-done.9.other_ref = f32[2,16,2048]{2,1,0:T(8,128)S(1)} collective-permute-done((f32[2,16,2048]{2,1,0:T(8,128)S(1)}, f32[2,16,2048]{2,1,0:T(8,128)S(1)}, u32[]{:S(2)}, u32[]{:S(2)}) %collective-permute-start.9) | collective-permute-done | bytes 262176 | tf_op jit(solution)/shard_map/ppermute | solution.py:480
  35.5 0.6 collective-permute-start.10
  36.1 4.2 %shard_map.41 = f32[2,32,2048]{2,1,0:T(8,128)S(1)} custom-call(s32[1]{0:T(128)} %bitcast.half_ref, f32[22,8,128]{2,1,0:T(8,128)S(1)} %get-tuple-element.47.table, f32[2,16,2048]{2,1,0:T(8,128)S(1)} %pad_maximum_fusion.2.own_ref, f32[2,16,2048]{2,1,0:T(8,128)S(1)} %collective-permute-done.9.other_ref, f32[16,32,2048]{2,1,0:T(8,128)} %get-tuple-element.69.old_ref), custom_call_target="tpu_custom_call" | custom-call | flops 16777216 | bytes 4194304 | tf_op jit(solution)/shard_map/pallas_call | solution.py:410
  40.2 0.8 %collective-permute-done.10 = f32[16,2048]{1,0:T(8,128)S(1)} collective-permute-done((f32[16,2048]{1,0:T(8,128)S(1)}, f32[16,2048]{1,0:T(8,128)S(1)}, u32[]{:S(2)}, u32[]{:S(2)}) %collective-permute-start.10) | collective-permute-done | bytes 131104 | tf_op jit(solution)/shard_map/ppermute | solution.py:569
  41.1 0.1 multiply_reduce_fusion.1
  41.2 0.1 select_subtract_fusion
  41.4 0.1 collective-permute-start.11
  41.5 1.5 %collective-permute-done.11 = f32[2,16,2048]{2,1,0:T(8,128)S(1)} collective-permute-done((f32[2,16,2048]{2,1,0:T(8,128)S(1)}, f32[2,16,2048]{2,1,0:T(8,128)S(1)}, u32[]{:S(2)}, u32[]{:S(2)}) %collective-permute-start.11) | collective-permute-done | bytes 262176 | tf_op jit(solution)/shard_map/ppermute | solution.py:480
  43.1 2.6 %collective-permute-start.14 = (f32[2,4,2048]{2,1,0:T(4,128)S(1)}, f32[2,4,2048]{2,1,0:T(4,128)S(1)}, u32[]{:S(2)}, u32[]{:S(2)}) collective-permute-start(f32[2,4,2048]{2,1,0:T(4,128)S(1)} %get-tuple-element.143), channel_id=1, source_target_pairs={{0,12},{2,14},{4,8},{6,10},{8,4},{10,6},{12,0},{14,2},{16,28},{18,... | collective-permute-start | bytes 196616 | tf_op jit(solution)/shard_map/ppermute | solution.py:480
  45.7 0.5 collective-permute-start.12
  46.2 0.4 collective-permute-start.13
  46.7 3.7 %shard_map.42 = (f32[16,32,768]{2,1,0:T(8,128)S(1)}, f32[2,16,768]{2,1,0:T(8,128)}) custom-call(f32[2,16,2048]{2,1,0:T(8,128)S(1)} %pad_maximum_fusion.1.ready, s32[1]{0:T(128)} %bitcast.half_ref, f32[22,8,128]{2,1,0:T(8,128)S(1)} %get-tuple-element.47.table, f32[2,16,2048]{2,1,0:T(8,128)S(1)} %pad_maximum_fusion.2.own_ref, ...), custom_call_target="tpu_custom_call" | custom-call | flops 15728640 | bytes 1572864 | tf_op jit(solution)/shard_map/pallas_call | solution.py:445
  50.6 2.4 %collective-permute-start.15 = (f32[2,4,2048]{2,1,0:T(4,128)S(1)}, f32[2,4,2048]{2,1,0:T(4,128)S(1)}, u32[]{:S(2)}, u32[]{:S(2)}) collective-permute-start(f32[2,4,2048]{2,1,0:T(4,128)S(1)} %pad_maximum_fusion.15.ready), channel_id=1, source_target_pairs={{0,16},{2,18},{4,20},{6,22},{8,24},{10,26},{12,28},{14,30},{16,0},... | collective-permute-start | bytes 196616 | tf_op jit(solution)/shard_map/ppermute | solution.py:480
  53.0 3.2 %shard_map.43 = (f32[16,32,512]{2,1,0:T(8,128)S(1)}, f32[2,16,512]{2,1,0:T(8,128)}) custom-call(f32[2,4,2048]{2,1,0:T(4,128)S(1)} %pad_maximum_fusion.15.ready, s32[1]{0:T(128)} %bitcast.half_ref, f32[22,8,128]{2,1,0:T(8,128)S(1)} %get-tuple-element.47.table, f32[2,16,2048]{2,1,0:T(8,128)S(1)} %pad_maximum_fusion.2.own_ref, ...), custom_call_target="tpu_custom_call" | custom-call | flops 10485760 | bytes 1048576 | tf_op jit(solution)/shard_map/pallas_call | solution.py:445
  56.3 0.1 add_select_fusion.15
  56.5 1.6 %collective-permute-start.17 = (f32[2,4,2048]{2,1,0:T(4,128)S(1)}, f32[2,4,2048]{2,1,0:T(4,128)S(1)}, u32[]{:S(2)}, u32[]{:S(2)}) collective-permute-start(f32[2,4,2048]{2,1,0:T(4,128)S(1)} %pad_maximum_fusion.17), channel_id=1, source_target_pairs={{0,8},{2,10},{4,12},{6,14},{8,0},{10,2},{12,4},{14,6},{16,24},{18,... | collective-permute-start | bytes 196616 | tf_op jit(solution)/shard_map/ppermute | solution.py:480
  58.1 1.5 %collective-permute-start.18 = (f32[2,4,2048]{2,1,0:T(4,128)S(1)}, f32[2,4,2048]{2,1,0:T(4,128)S(1)}, u32[]{:S(2)}, u32[]{:S(2)}) collective-permute-start(f32[2,4,2048]{2,1,0:T(4,128)S(1)} %pad_maximum_fusion.18), channel_id=1, source_target_pairs={{0,12},{2,14},{4,8},{6,10},{8,4},{10,6},{12,0},{14,2},{16,28},{18,... | collective-permute-start | bytes 196616 | tf_op jit(solution)/shard_map/ppermute | solution.py:480
  59.6 0.6 collective-permute-start.16
  60.2 3.8 %shard_map.44 = (f32[16,32,768]{2,1,0:T(8,128)S(1)}, f32[2,16,768]{2,1,0:T(8,128)}) custom-call(f32[2,4,2048]{2,1,0:T(4,128)S(1)} %pad_maximum_fusion.19.ready, s32[1]{0:T(128)} %bitcast.half_ref, f32[22,8,128]{2,1,0:T(8,128)S(1)} %get-tuple-element.47.table, f32[2,16,2048]{2,1,0:T(8,128)S(1)} %pad_maximum_fusion.2.own_ref, ...), custom_call_target="tpu_custom_call" | custom-call | flops 15728640 | bytes 1572864 | tf_op jit(solution)/shard_map/pallas_call | solution.py:445
  64.1 0.1 pad_maximum_fusion.6
  64.2 0.1 pad_maximum_fusion.7
  64.3 0.1 collective-permute-start.19
  64.4 1.5 %collective-permute-done.19.other_ref = f32[2,16,2048]{2,1,0:T(8,128)S(1)} collective-permute-done((f32[2,16,2048]{2,1,0:T(8,128)S(1)}, f32[2,16,2048]{2,1,0:T(8,128)S(1)}, u32[]{:S(2)}, u32[]{:S(2)}) %collective-permute-start.19) | collective-permute-done | bytes 262176 | tf_op jit(solution)/shard_map/ppermute | solution.py:480
  65.9 2.2 %shard_map.45 = f32[16,32,2048]{2,1,0:T(8,128)} custom-call(s32[1]{0:T(128)} %bitcast.half_ref, f32[22,8,128]{2,1,0:T(8,128)S(1)} %get-tuple-element.47.table, f32[2,16,2048]{2,1,0:T(8,128)S(1)} %pad_maximum_fusion.8.own_ref, f32[2,16,2048]{2,1,0:T(8,128)S(1)} %collective-permute-done.19.other_ref, f32[16,32,768]{2,1,0:T(8,128)S(1)} %get-tuple-element.86.rest_0_, ...), custom_call_target="tpu_custom_call" | custom-call | flops 6291456 | bytes 4194304 | tf_op jit(solution)/shard_map/pallas_call | solution.py:461
  (60 shorter events, 1.3 us)
Async XLA Ops:
  1.8 7.9 %collective-permute-start = (f32[16,2048]{1,0:T(8,128)S(1)}, f32[16,2048]{1,0:T(8,128)S(1)}, u32[]{:S(2)}, u32[]{:S(2)}) collective-permute-start(f32[16,2048]{1,0:T(8,128)S(1)} %fusion.5), channel_id=1, source_target_pairs={{0,1},{1,0},{2,3},{3,2},{4,5},{5,4},{6,7},{7,6},{8,9},{9,8},{10,11... | collective-permute-start | bytes 393224 | tf_op jit(solution)/shard_map/ppermute | solution.py:569
  10.0 1.6 %collective-permute-start.1 = (f32[2,16,2048]{2,1,0:T(8,128)S(1)}, f32[2,16,2048]{2,1,0:T(8,128)S(1)}, u32[]{:S(2)}, u32[]{:S(2)}) collective-permute-start(f32[2,16,2048]{2,1,0:T(8,128)S(1)} %constant_dynamic-slice_fusion.1), channel_id=1, source_target_pairs={{0,2},{2,0},{4,6},{6,4},{8,10},{10,8},{12,14},{14,12},{16,18},{18,... | collective-permute-start | bytes 786440 | tf_op jit(solution)/shard_map/ppermute | solution.py:480
  11.8 7.5 %collective-permute-start.4 = (f32[2,4,2048]{2,1,0:T(4,128)S(1)}, f32[2,4,2048]{2,1,0:T(4,128)S(1)}, u32[]{:S(2)}, u32[]{:S(2)}) collective-permute-start(f32[2,4,2048]{2,1,0:T(4,128)S(1)} %get-tuple-element.151), channel_id=1, source_target_pairs={{0,12},{2,14},{4,8},{6,10},{8,4},{10,6},{12,0},{14,2},{16,28},{18,... | collective-permute-start | bytes 196616 | tf_op jit(solution)/shard_map/ppermute | solution.py:480
  14.3 4.9 %collective-permute-start.2 = (f32[2,4,2048]{2,1,0:T(4,128)S(1)}, f32[2,4,2048]{2,1,0:T(4,128)S(1)}, u32[]{:S(2)}, u32[]{:S(2)}) collective-permute-start(f32[2,4,2048]{2,1,0:T(4,128)S(1)} %get-tuple-element.153), channel_id=1, source_target_pairs={{0,4},{2,6},{4,0},{6,2},{8,12},{10,14},{12,8},{14,10},{16,20},{18,... | collective-permute-start | bytes 196616 | tf_op jit(solution)/shard_map/ppermute | solution.py:480
  14.9 4.4 %collective-permute-start.3 = (f32[2,4,2048]{2,1,0:T(4,128)S(1)}, f32[2,4,2048]{2,1,0:T(4,128)S(1)}, u32[]{:S(2)}, u32[]{:S(2)}) collective-permute-start(f32[2,4,2048]{2,1,0:T(4,128)S(1)} %get-tuple-element.154), channel_id=1, source_target_pairs={{0,8},{2,10},{4,12},{6,14},{8,0},{10,2},{12,4},{14,6},{16,24},{18,... | collective-permute-start | bytes 196616 | tf_op jit(solution)/shard_map/ppermute | solution.py:480
  19.4 6.0 %collective-permute-start.5 = (f32[2,4,2048]{2,1,0:T(4,128)S(1)}, f32[2,4,2048]{2,1,0:T(4,128)S(1)}, u32[]{:S(2)}, u32[]{:S(2)}) collective-permute-start(f32[2,4,2048]{2,1,0:T(4,128)S(1)} %pad_maximum_fusion.10.ready), channel_id=1, source_target_pairs={{0,16},{2,18},{4,20},{6,22},{8,24},{10,26},{12,28},{14,30},{16,0},... | collective-permute-start | bytes 196616 | tf_op jit(solution)/shard_map/ppermute | solution.py:480
  25.7 7.8 %collective-permute-start.7 = (f32[2,4,2048]{2,1,0:T(4,128)S(1)}, f32[2,4,2048]{2,1,0:T(4,128)S(1)}, u32[]{:S(2)}, u32[]{:S(2)}) collective-permute-start(f32[2,4,2048]{2,1,0:T(4,128)S(1)} %pad_maximum_fusion.12), channel_id=1, source_target_pairs={{0,8},{2,10},{4,12},{6,14},{8,0},{10,2},{12,4},{14,6},{16,24},{18,... | collective-permute-start | bytes 196616 | tf_op jit(solution)/shard_map/ppermute | solution.py:480
  27.3 6.1 %collective-permute-start.8 = (f32[2,4,2048]{2,1,0:T(4,128)S(1)}, f32[2,4,2048]{2,1,0:T(4,128)S(1)}, u32[]{:S(2)}, u32[]{:S(2)}) collective-permute-start(f32[2,4,2048]{2,1,0:T(4,128)S(1)} %pad_maximum_fusion.13), channel_id=1, source_target_pairs={{0,12},{2,14},{4,8},{6,10},{8,4},{10,6},{12,0},{14,2},{16,28},{18,... | collective-permute-start | bytes 196616 | tf_op jit(solution)/shard_map/ppermute | solution.py:480
  28.8 4.7 %collective-permute-start.6 = (f32[2,4,2048]{2,1,0:T(4,128)S(1)}, f32[2,4,2048]{2,1,0:T(4,128)S(1)}, u32[]{:S(2)}, u32[]{:S(2)}) collective-permute-start(f32[2,4,2048]{2,1,0:T(4,128)S(1)} %pad_maximum_fusion.11), channel_id=1, source_target_pairs={{0,4},{2,6},{4,0},{6,2},{8,12},{10,14},{12,8},{14,10},{16,20},{18,... | collective-permute-start | bytes 196616 | tf_op jit(solution)/shard_map/ppermute | solution.py:480
  33.7 1.6 %collective-permute-start.9 = (f32[2,16,2048]{2,1,0:T(8,128)S(1)}, f32[2,16,2048]{2,1,0:T(8,128)S(1)}, u32[]{:S(2)}, u32[]{:S(2)}) collective-permute-start(f32[2,16,2048]{2,1,0:T(8,128)S(1)} %pad_maximum_fusion.5), channel_id=1, source_target_pairs={{0,2},{2,0},{4,6},{6,4},{8,10},{10,8},{12,14},{14,12},{16,18},{18,... | collective-permute-start | bytes 786440 | tf_op jit(solution)/shard_map/ppermute | solution.py:480
  35.5 5.6 %collective-permute-start.10 = (f32[16,2048]{1,0:T(8,128)S(1)}, f32[16,2048]{1,0:T(8,128)S(1)}, u32[]{:S(2)}, u32[]{:S(2)}) collective-permute-start(f32[16,2048]{1,0:T(8,128)S(1)} %fusion.2), channel_id=1, source_target_pairs={{0,1},{1,0},{2,3},{3,2},{4,5},{5,4},{6,7},{7,6},{8,9},{9,8},{10,11... | collective-permute-start | bytes 393224 | tf_op jit(solution)/shard_map/ppermute | solution.py:569
  41.4 1.6 %collective-permute-start.11 = (f32[2,16,2048]{2,1,0:T(8,128)S(1)}, f32[2,16,2048]{2,1,0:T(8,128)S(1)}, u32[]{:S(2)}, u32[]{:S(2)}) collective-permute-start(f32[2,16,2048]{2,1,0:T(8,128)S(1)} %constant_dynamic-slice_fusion), channel_id=1, source_target_pairs={{0,2},{2,0},{4,6},{6,4},{8,10},{10,8},{12,14},{14,12},{16,18},{18,... | collective-permute-start | bytes 786440 | tf_op jit(solution)/shard_map/ppermute | solution.py:480
  43.1 7.3 %collective-permute-start.14 = (f32[2,4,2048]{2,1,0:T(4,128)S(1)}, f32[2,4,2048]{2,1,0:T(4,128)S(1)}, u32[]{:S(2)}, u32[]{:S(2)}) collective-permute-start(f32[2,4,2048]{2,1,0:T(4,128)S(1)} %get-tuple-element.143), channel_id=1, source_target_pairs={{0,12},{2,14},{4,8},{6,10},{8,4},{10,6},{12,0},{14,2},{16,28},{18,... | collective-permute-start | bytes 196616 | tf_op jit(solution)/shard_map/ppermute | solution.py:480
  45.7 4.8 %collective-permute-start.12 = (f32[2,4,2048]{2,1,0:T(4,128)S(1)}, f32[2,4,2048]{2,1,0:T(4,128)S(1)}, u32[]{:S(2)}, u32[]{:S(2)}) collective-permute-start(f32[2,4,2048]{2,1,0:T(4,128)S(1)} %get-tuple-element.145), channel_id=1, source_target_pairs={{0,4},{2,6},{4,0},{6,2},{8,12},{10,14},{12,8},{14,10},{16,20},{18,... | collective-permute-start | bytes 196616 | tf_op jit(solution)/shard_map/ppermute | solution.py:480
  46.2 4.3 %collective-permute-start.13 = (f32[2,4,2048]{2,1,0:T(4,128)S(1)}, f32[2,4,2048]{2,1,0:T(4,128)S(1)}, u32[]{:S(2)}, u32[]{:S(2)}) collective-permute-start(f32[2,4,2048]{2,1,0:T(4,128)S(1)} %get-tuple-element.146), channel_id=1, source_target_pairs={{0,8},{2,10},{4,12},{6,14},{8,0},{10,2},{12,4},{14,6},{16,24},{18,... | collective-permute-start | bytes 196616 | tf_op jit(solution)/shard_map/ppermute | solution.py:480
  50.6 5.6 %collective-permute-start.15 = (f32[2,4,2048]{2,1,0:T(4,128)S(1)}, f32[2,4,2048]{2,1,0:T(4,128)S(1)}, u32[]{:S(2)}, u32[]{:S(2)}) collective-permute-start(f32[2,4,2048]{2,1,0:T(4,128)S(1)} %pad_maximum_fusion.15.ready), channel_id=1, source_target_pairs={{0,16},{2,18},{4,20},{6,22},{8,24},{10,26},{12,28},{14,30},{16,0},... | collective-permute-start | bytes 196616 | tf_op jit(solution)/shard_map/ppermute | solution.py:480
  56.5 7.6 %collective-permute-start.17 = (f32[2,4,2048]{2,1,0:T(4,128)S(1)}, f32[2,4,2048]{2,1,0:T(4,128)S(1)}, u32[]{:S(2)}, u32[]{:S(2)}) collective-permute-start(f32[2,4,2048]{2,1,0:T(4,128)S(1)} %pad_maximum_fusion.17), channel_id=1, source_target_pairs={{0,8},{2,10},{4,12},{6,14},{8,0},{10,2},{12,4},{14,6},{16,24},{18,... | collective-permute-start | bytes 196616 | tf_op jit(solution)/shard_map/ppermute | solution.py:480
  58.1 5.9 %collective-permute-start.18 = (f32[2,4,2048]{2,1,0:T(4,128)S(1)}, f32[2,4,2048]{2,1,0:T(4,128)S(1)}, u32[]{:S(2)}, u32[]{:S(2)}) collective-permute-start(f32[2,4,2048]{2,1,0:T(4,128)S(1)} %pad_maximum_fusion.18), channel_id=1, source_target_pairs={{0,12},{2,14},{4,8},{6,10},{8,4},{10,6},{12,0},{14,2},{16,28},{18,... | collective-permute-start | bytes 196616 | tf_op jit(solution)/shard_map/ppermute | solution.py:480
  59.6 4.5 %collective-permute-start.16 = (f32[2,4,2048]{2,1,0:T(4,128)S(1)}, f32[2,4,2048]{2,1,0:T(4,128)S(1)}, u32[]{:S(2)}, u32[]{:S(2)}) collective-permute-start(f32[2,4,2048]{2,1,0:T(4,128)S(1)} %pad_maximum_fusion.16), channel_id=1, source_target_pairs={{0,4},{2,6},{4,0},{6,2},{8,12},{10,14},{12,8},{14,10},{16,20},{18,... | collective-permute-start | bytes 196616 | tf_op jit(solution)/shard_map/ppermute | solution.py:480
  64.3 1.6 %collective-permute-start.19 = (f32[2,16,2048]{2,1,0:T(8,128)S(1)}, f32[2,16,2048]{2,1,0:T(8,128)S(1)}, u32[]{:S(2)}, u32[]{:S(2)}) collective-permute-start(f32[2,16,2048]{2,1,0:T(8,128)S(1)} %pad_maximum_fusion.9), channel_id=1, source_target_pairs={{0,2},{2,0},{4,6},{6,4},{8,10},{10,8},{12,14},{14,12},{16,18},{18,... | collective-permute-start | bytes 786440 | tf_op jit(solution)/shard_map/ppermute | solution.py:480

commit v5 on v4

--- a/solution.py
+++ b/solution.py
@@ -14,6 +14,7 @@
 TILE = (ROWS, LANES)
 UNROLL = 4
 PARTS = 3
+READS = 8
 
 DECAY, SCALE, LINEAR, SQUARE, CUBE, KEEP, WEIGHTS = range(7)
 
@@ -37,7 +38,7 @@
         table[WEIGHTS + 2 * k + 1] = 0.5 * (powers[k] - powers[slices - 1 - k])
 
 
-def fill_wide(scalars, planes_ref, arcs_ref, levels):
+def fill_wide(scalars, planes_ref, arcs_ref, green_ref, levels):
     _, slices, width = planes_ref.shape
 
     def rate_of(shape):
@@ -52,6 +53,7 @@
     start, end = jnp.exp(-rate * t), jnp.exp(-rate * (slices - 1 - t))
     r = jnp.exp(-rate)
     values = (r * start, r * end, scale * end, scale * start)
+    green_ref[...] = scale * jnp.exp(-rate * jnp.abs(t - lax.broadcasted_iota(jnp.int32, shape, 1).astype(jnp.float32)))
     row = lax.broadcasted_iota(jnp.int32, TILE, 0)
     rate = rate_of(TILE)
     arcs = jnp.zeros(TILE, jnp.float32)
@@ -134,13 +136,11 @@
                 ends_ref[n, rows_of(i), lanes] = force + table[LINEAR] * field
         return carry
 
-    lax.fori_loop(tiles[0], tiles[1], tile, 0, unroll=UNROLL)
-
-
-def finish_sums(table, ends_ref, sums):
-    _, planes, width = ends_ref.shape
-    blocks = planes // ROWS
-    masks = Masks()
+    lax.fori_loop(tiles[0], tiles[1], tile, 0, unroll=True)
+
+
+def finish_sums(table, masks, ends_ref, sums, tiles):
+    blocks = ends_ref.shape[1] // ROWS
     zero = jnp.zeros(TILE, jnp.float32)
 
     def tile(j, carry):
@@ -153,7 +153,7 @@
                 ends_ref[n, rows_of(i), tile_at(j)] -= table[SCALE] * total
         return carry
 
-    lax.fori_loop(0, width // LANES, tile, 0, unroll=UNROLL)
+    lax.fori_loop(*tiles, tile, 0, unroll=True)
 
 
 def clear_guards(ref):
@@ -165,7 +165,7 @@
 
 def bounds_of(width):
     tiles = width // LANES
-    return [0, 3 * tiles // 8, 5 * tiles // 8, tiles]
+    return [0, 7 * tiles // 16, 11 * tiles // 16, tiles]
 
 
 def pieces_of(width):
@@ -188,19 +188,21 @@
         reads[-1][1].start()
     clear_guards(sums)
     prepare()
+    masks = Masks()
     for part, read in reads:
         read.wait()
         sum_tiles(table, enter, old, ends_ref, sums, part)
-    finish_sums(table, ends_ref, sums)
+        last = part[1] == tiles
+        finish_sums(table, masks, ends_ref, sums, (max(part[0] - 1, 0), part[1] if last else part[1] - 1))
 
 
 def first_sums_kernel(
-    levels, step_ref, mass_ref, old_ref, ends_ref, table, planes_ref, arcs_ref, old, sums, sems
+    levels, step_ref, mass_ref, old_ref, ends_ref, table, planes_ref, arcs_ref, green_ref, old, sums, sems
 ):
     def prepare():
         values = step_ref[0], mass_ref[0]
         fill_table(values, table, old.shape[0])
-        fill_wide(values, planes_ref, arcs_ref, levels)
+        fill_wide(values, planes_ref, arcs_ref, green_ref, levels)
 
     sum_parts(table, None, old_ref, ends_ref, old, sums, sems, prepare)
 
@@ -217,6 +219,7 @@
 def relax_tiles(table, masks, phi, low_ref, high_ref, psi_ref, edges_ref, tiles, start):
     slices, planes, _ = phi.shape
     blocks = planes // ROWS
+    zero = jnp.zeros(TILE, jnp.float32)
 
     def tile(j, carry):
         lanes, place = tile_at(j), tile_at(j, -start * LANES)
@@ -226,8 +229,8 @@
             for n in range(slices):
                 t = n // 2 if n % 2 == 0 else slices - 1 - n // 2
                 v = at(t, i, 0)
-                before = low_ref[t : t + 1, lanes] if i == 0 else at(t, i - 1, 0)
-                after = high_ref[t : t + 1, lanes] if i == blocks - 1 else at(t, i + 1, 0)
+                before = (zero if low_ref is None else low_ref[t : t + 1, lanes]) if i == 0 else at(t, i - 1, 0)
+                after = (zero if high_ref is None else high_ref[t : t + 1, lanes]) if i == blocks - 1 else at(t, i + 1, 0)
                 total = neighbours(masks, v, before, after, at(t, i, -1), at(t, i, 1))
                 force[t] = v * (table[LINEAR] + v * (table[SQUARE] + table[CUBE] * v)) - table[SCALE] * total
             forward, backward = [None] * slices, [None] * slices
@@ -244,9 +247,9 @@
                 local = backward[t] if t == 0 else forward[t] + backward[t]
                 value = table[KEEP] * at(t, i, 0) - local
                 psi_ref[t, rows_of(i), place] = value
-                if i == 0:
+                if edges_ref is not None and i == 0:
                     edges_ref[0, t : t + 1, place] = value[:1]
-                if i == blocks - 1:
+                if edges_ref is not None and i == blocks - 1:
                     edges_ref[1, t : t + 1, place] = value[ROWS - 1 :]
         return carry
 
@@ -291,7 +294,7 @@
 
 
 def next_relax_kernel(
-    tiles, ready, half_ref, table, own_ref, other_ref, low_ref, high_ref, old_ref, psi_ref, edges_ref, phi, old, sems
+    tiles, ready, half_ref, table, own_ref, other_ref, old_ref, psi_ref, phi, old, sems
 ):
     slices, planes, _ = phi.shape
     blocks = planes // ROWS
@@ -313,32 +316,46 @@
     for n, part in enumerate(parts_of(tiles, count)):
         reads[n].wait()
         lax.fori_loop(bounds[n], bounds[n + 1], tile, 0, unroll=True)
-        relax_tiles(table, masks, phi, low_ref, high_ref, psi_ref, edges_ref, part, tiles[0])
-
-
-def last_kernel(half_ref, table, own_ref, other_ref, *rest):
-    *olds, out_ref, stage, sems = rest
-    slices, planes, width = stage.shape
+        relax_tiles(table, masks, phi, None, None, psi_ref, None, part, tiles[0])
+
+
+def last_kernel(mine, pieces, half_ref, table, low_ref, high_ref, enters_ref, *rest):
+    olds, (out_ref, stage, sems) = rest[: len(pieces)], rest[-3:]
+    slices, planes, _ = stage.shape
     blocks = planes // ROWS
+    base = half_ref[0] * planes if mine else (1 - half_ref[0]) * planes
+    r = table[DECAY]
+    row = lax.broadcasted_iota(jnp.int32, TILE, 0) + base
     writes = []
-    for n, ((first, last), old) in enumerate(zip(pieces_of(width), olds)):
-        middle = (first + last) // 2
+    for n, ((first, last), old) in enumerate(zip(pieces, olds)):
 
         def tile(j, carry):
-            lanes = tile_at(j)
+            lanes, place = tile_at(j), tile_at(j, -first * LANES)
+
+            def edge(t, i):
+                value = 0.0
+                if i == 0:
+                    value += jnp.where(row == 0, low_ref[t : t + 1, lanes], 0.0)
+                if i == blocks - 1:
+                    value += jnp.where(row + ROWS * i == 2 * planes - 1, high_ref[t : t + 1, lanes], 0.0)
+                return value
+
             for i in range(blocks):
-                both = entering_tile(table, half_ref, own_ref, other_ref, i, blocks, lanes)
+                rows = pl.ds(pl.multiple_of(base + ROWS * i, ROWS), ROWS)
+                p, q = enters_ref[0, rows_of(i), lanes], enters_ref[1, rows_of(i), lanes]
+                even, odd = r * (p + q), r * (p - q)
                 for k in range(slices // 2):
-                    v, w = entered_pair(table, both, old, k, i, tile_at(j, -first * LANES))
-                    stage[k, rows_of(i), lanes] = v
-                    stage[slices - 1 - k, rows_of(i), lanes] = w
+                    x, y = table[WEIGHTS + 2 * k] * even, table[WEIGHTS + 2 * k + 1] * odd
+                    stage[k, rows_of(i), lanes] = old[k, rows, place] - (x + y) + edge(k, i)
+                    t = slices - 1 - k
+                    stage[t, rows_of(i), lanes] = old[t, rows, place] - (x - y) + edge(t, i)
             return carry
 
-        for k, part in enumerate(((first, middle), (middle, last))):
-            lax.fori_loop(*part, tile, 0, unroll=True)
-            lanes = lanes_of(*part)
-            writes.append(pltpu.make_async_copy(stage.at[:, :, lanes], out_ref.at[:, :, lanes], sems.at[2 * n + k]))
-            writes[-1].start()
+        lax.fori_loop(first, last, tile, 0, unroll=UNROLL)
+        lanes = lanes_of(first, last)
+        there = out_ref.at[:, pl.ds(pl.multiple_of(base, ROWS), planes), lanes]
+        writes.append(pltpu.make_async_copy(stage.at[:, :, lanes], there, sems.at[n]))
+        writes[-1].start()
     for write in writes:
         write.wait()
 
@@ -384,7 +401,7 @@
 
 def first_sums(step, mass, field, levels):
     slices, planes, width = field.shape
-    assert slices % 2 == 0 and levels < ROWS
+    assert slices % 2 == 0 and slices <= LANES and levels < ROWS
     return pl.pallas_call(
         functools.partial(first_sums_kernel, levels),
         in_specs=[SMEM] * 2 + [HBM],
@@ -393,12 +410,13 @@
             f32((WEIGHTS + slices, *TILE)),
             f32((4, slices, width)),
             f32((ROWS, width)),
+            f32((slices, LANES)),
         ),
-        out_specs=(VMEM,) * 4,
+        out_specs=(VMEM,) * 5,
         scratch_shapes=[
             pltpu.VMEM(field.shape, jnp.float32),
             padded(2, field.shape),
-            pltpu.SemaphoreType.DMA((4,)),
+            pltpu.SemaphoreType.DMA((READS,)),
         ],
         compiler_params=PARAMS,
         cost_estimate=cost(field.shape, 12),
@@ -415,7 +433,7 @@
         scratch_shapes=[
             pltpu.VMEM(old.shape, jnp.float32),
             padded(2, old.shape),
-            pltpu.SemaphoreType.DMA((4,)),
+            pltpu.SemaphoreType.DMA((READS,)),
         ],
         compiler_params=PARAMS,
         cost_estimate=cost(old.shape, 16),
@@ -439,14 +457,14 @@
     )(*operands)
 
 
-def next_relax(tiles, ready, half, own, other, table, low, high, old):
+def next_relax(tiles, ready, half, own, other, table, old):
     slices, planes, width = old.shape
     piece = piece_shape(old.shape, tiles)
     return pl.pallas_call(
         functools.partial(next_relax_kernel, tiles),
-        in_specs=[VMEM, SMEM] + [VMEM] * 5 + [HBM],
-        out_shape=(vmem(piece), f32((2, slices, piece[-1]))),
-        out_specs=(VMEM, VMEM),
+        in_specs=[VMEM, SMEM] + [VMEM] * 3 + [HBM],
+        out_shape=vmem(piece),
+        out_specs=VMEM,
         scratch_shapes=[
             padded(slices, old.shape),
             pltpu.VMEM(old.shape, jnp.float32),
@@ -454,19 +472,26 @@
         ],
         compiler_params=PARAMS,
         cost_estimate=cost(piece, 40),
-    )(ready, half, table, own, other, low, high, in_hbm(old))
-
-
-def last_step(shape, half, table, own, other, olds):
+    )(ready, half, table, own, other, in_hbm(old))
+
+
+def last_step(shape, mine, half, table, low, high, enters, olds, out):
+    slices, planes, width = shape
+    pieces = pieces_of(width)
+    operands = [half, table, low, high, enters, *map(in_vmem, olds)] + ([] if out is None else [in_hbm(out)])
     return pl.pallas_call(
-        last_kernel,
-        in_specs=[SMEM] + [VMEM] * (3 + len(olds)),
+        functools.partial(last_kernel, mine, pieces),
+        in_specs=[SMEM] + [VMEM] * (4 + len(olds)) + ([] if out is None else [HBM]),
         out_shape=hbm(shape),
         out_specs=HBM,
-        scratch_shapes=[pltpu.VMEM(shape, jnp.float32), pltpu.SemaphoreType.DMA((2 * len(olds),))],
+        input_output_aliases={} if out is None else {len(operands) - 1: 0},
+        scratch_shapes=[
+            pltpu.VMEM((slices, planes // 2, width), jnp.float32),
+            pltpu.SemaphoreType.DMA((len(pieces),)),
+        ],
         compiler_params=PARAMS,
-        cost_estimate=cost(shape, 6),
-    )(half, table, own, other, *map(in_vmem, olds))
+        cost_estimate=cost((slices, planes // 2, width), 6),
+    )(*operands)
 
 
 class Loop:
@@ -561,14 +586,14 @@
     def row(self, parity):
         return jnp.where(self.me % 2 == parity, self.planes - 1, 0)
 
-    def exchange(self, first, last):
-        low = high = jnp.zeros_like(first)
+    def exchange(self, plane):
+        low = high = 0.0
         for parity in self.rounds:
-            given = jnp.where(self.row(parity) == 0, first, last)
+            row = self.row(parity)
             pairs = range(parity, self.devices - 1, 2)
-            got = lax.ppermute(given, "space", [(i, i + 1) for i in pairs] + [(i + 1, i) for i in pairs])
-            low = low + jnp.where(self.row(parity) == 0, got, 0.0)
-            high = high + jnp.where(self.row(parity) == 0, 0.0, got)
+            got = lax.ppermute(plane(row), "space", [(i, i + 1) for i in pairs] + [(i + 1, i) for i in pairs])
+            low = low + jnp.where(row == 0, got, 0.0)
+            high = high + jnp.where(row == 0, 0.0, got)
         return low, high
 
 
@@ -580,37 +605,43 @@
 
     pieces = pieces_of(width)
 
-    def edge_sums(ends, low, high):
+    def sums_of(plane):
+        return jnp.sum(weights[2:] * plane[None], axis=1)
+
+    def with_edges(ends, first, last):
         row = lax.broadcasted_iota(jnp.int32, (1, planes, 1), 1)
-        for place, plane in ((0, low), (planes - 1, high)):
-            sums = jnp.sum(weights[2:] * plane[None], axis=1)
+        for place, sums in ((0, first), (planes - 1, last)):
             ends = ends - jnp.where(row == place, sums[:, None, :], 0.0)
         return ends
 
-    low, high = sides.exchange(field[:, 0], field[:, -1])
-    ends, table, weights, arcs = first_sums(step, mass, field, loop.levels)
+    low, high = sides.exchange(lambda row: lax.dynamic_index_in_dim(field, row, 1, keepdims=False))
+    ends, table, weights, arcs, green = first_sums(step, mass, field, loop.levels)
 
     def first_work(tiles, ready, state=(None, ())):
         psi, edge = first_relax(tiles, ready, table, low, high, field, state[0])
         return psi, (*state[1], edge)
 
     works = [functools.partial(first_work, tiles) for tiles in pieces]
-    own, other, (psi, edges) = loop.solve(edge_sums(ends, low, high), arcs, works)
+    own, other, (psi, edges) = loop.solve(with_edges(ends, sums_of(low), sums_of(high)), arcs, works)
 
     edges = jnp.concatenate(edges, axis=2)
     mine = half[0] == 0
     fluxes = jnp.where(mine, own[:, 0], other[:, 0]), jnp.where(mine, other[:, -1], own[:, -1])
-    low, high = sides.exchange(
-        *(edge - weights[0] * flux[0] - weights[1] * flux[1] for edge, flux in zip(edges, fluxes))
-    )
-    ends = next_sums(half, table, own, other, psi)
+    first, last = (edge - weights[0] * flux[0] - weights[1] * flux[1] for edge, flux in zip(edges, fluxes))
+    halo = lambda row: jnp.where(row == 0, first, last)
+    sums = sides.exchange(lambda row: sums_of(halo(row)))
+    ends = with_edges(next_sums(half, table, own, other, psi), *sums)
+    ends, first, last = lax.optimization_barrier((ends, first, last))
+    low, high = sides.exchange(halo)
 
     def next_work(tiles, ready, state=(), own=own, other=other):
-        return *state, next_relax(tiles, ready, half, own, other, table, low, high, psi)[0]
+        return *state, next_relax(tiles, ready, half, own, other, table, psi)
 
     works = [functools.partial(next_work, tiles) for tiles in pieces]
-    own, other, olds = loop.solve(edge_sums(ends, low, high), arcs, works)
-    return last_step(shape, half, table, own, other, olds)
+    own, other, olds = loop.solve(ends, arcs, works)
+    low, high = (jnp.dot(green[:, : field.shape[0]], plane, precision=lax.Precision.HIGHEST) for plane in (low, high))
+    out = last_step(shape, True, half, table, low, high, own, olds, None)
+    return last_step(shape, False, half, table, low, high, other, olds, out)
 
 
 def solution(mesh):

time: 68.6 us -> 65.6 us (0.956)
  Pallas kernels: 31.9 us -> 29.4 us
  waiting for transfers between devices: 6.86 us -> 4.58 us
  starting transfers between devices: 23.4 us -> 25 us
    pallas_call x3, Pallas kernels: 10.7 us -> 8.79 us  [next_relax(): pl.pallas_call(functools.partial(next_relax_kernel, tiles), in_specs=[VME...]
    slice x1 -> x0, local copies, waits for them, and re-layouts: 1.73 us -> none  [on_device(): low, high = sides.exchange(field[:, 0], field[:, -1])]
    ppermute x2 -> x3, starting transfers between devices: 3.6 us -> 5.19 us  [exchange(): lax.ppermute(plane(row), 'space', [(i, i + 1) for i in pairs] + [(i + 1,...]
    ppermute x18, waiting for transfers between devices: 6.01 us -> 4.57 us  [swap(): lax.ppermute(array, 'tm', [(i, i ^ offset) for i in range(self.devices)])]
    dynamic_slice x0 -> x1, local copies, waits for them, and re-layouts: none -> 1.32 us  [on_device(): lax.dynamic_index_in_dim(field, row, 1, keepdims=False)]
    pallas_call x1 -> x2, Pallas kernels: 2.18 us -> 3.11 us  [last_step(): pl.pallas_call(functools.partial(last_kernel, mine, pieces), in_specs=[SM...]
    ppermute x2 -> x3, waiting for transfers between devices: 0.85 us -> 0.01 us  [exchange(): lax.ppermute(plane(row), 'space', [(i, i + 1) for i in pairs] + [(i + 1,...]
    pallas_call x1, Pallas kernels: 4.15 us -> 3.37 us  [next_sums(): pl.pallas_call(next_sums_kernel, in_specs=[SMEM] + [VMEM] * 3 + [HBM], ou...]
  transfers between devices with their start and end apart: 20 -> 21, of which waited for: 5 -> 6; matrix products, arithmetic and copies ran while one was open for 0% -> 2% of each run, Pallas kernels for 43% -> 43%
where the time goes in v5:
time: 65.6 us; the launch traced here: 65.3 us
  Pallas kernels  29.4 us (45%)
  starting transfers between devices  25 us (38%)
  waiting for transfers between devices  4.58 us (7%)
  other arithmetic  2.19 us (3%)
  between operations  2.04 us (3%)
  local copies, waits for them, and re-layouts  1.51 us (2%)
    ppermute x18, starting transfers between devices, swap(): lax.ppermute(array, 'tm', [(i, i ^ offset) for i in range(self.devices)])  19.8 us
    pallas_call x3, Pallas kernels, first_relax(): pl.pallas_call(functools.partial(first_relax_kernel, tiles), in_specs=[VM...  11.2 us
    pallas_call x3, Pallas kernels, next_relax(): pl.pallas_call(functools.partial(next_relax_kernel, tiles), in_specs=[VME...  8.79 us
    ppermute x3, starting transfers between devices, exchange(): lax.ppermute(plane(row), 'space', [(i, i + 1) for i in pairs] + [(i + 1,...  5.19 us
    ppermute x18, waiting for transfers between devices, swap(): lax.ppermute(array, 'tm', [(i, i ^ offset) for i in range(self.devices)])  4.57 us
    pallas_call x1, Pallas kernels, next_sums(): pl.pallas_call(next_sums_kernel, in_specs=[SMEM] + [VMEM] * 3 + [HBM], ou...  3.37 us
    pallas_call x2, Pallas kernels, last_step(): pl.pallas_call(functools.partial(last_kernel, mine, pieces), in_specs=[SM...  3.11 us
    pallas_call x1, Pallas kernels, first_sums(): pl.pallas_call(functools.partial(first_sums_kernel, levels), in_specs=[SM...  2.92 us
  transfers between devices with their start and end apart: 21, of which 6 were waited for; matrix products, arithmetic and copies ran while one was open for 2% of the time, Pallas kernels for 43%

profile of v5, /device:TPU:0, one launch (start us, length us, event | category | flops | bytes accessed | tf_op | source)
XLA Modules:
  0.0 65.3 jit_solution(8908623538635101152)
XLA Ops:
  0.0 1.3 %constant_dynamic-slice_fusion.2 = f32[16,1,2048]{2,1,0:T(1,128)S(1)} fusion(f32[16,32,2048]{2,1,0:T(8,128)} %old_ref.7, s32[]{:T(128)S(6)} %select_n.421), kind=kLoop, calls=%fused_computation.161 | loop fusion | bytes 262148 | tf_op jit(solution)/shard_map/jit(dynamic_index_in_dim)/dynamic_slice | solution.py:617
  1.4 3.0 %collective-permute-start = (f32[16,2048]{1,0:T(8,128)S(1)}, f32[16,2048]{1,0:T(8,128)S(1)}, u32[]{:S(2)}, u32[]{:S(2)}) collective-permute-start(f32[16,2048]{1,0:T(8,128)S(1)} %bitcast.79), channel_id=1, source_target_pairs={{0,1},{1,0},{2,3},{3,2},{4,5},{5,4},{6,7},{7,6},{8,9},{9,8},{10,11... | collective-permute-start | bytes 393224 | tf_op jit(solution)/shard_map/ppermute | solution.py:594
  5.7 2.9 %shard_map.37 = (f32[2,32,2048]{2,1,0:T(8,128)S(1)}, f32[22,8,128]{2,1,0:T(8,128)S(1)}, f32[4,16,2048]{2,1,0:T(8,128)S(1)}, f32[8,2048]{1,0:T(8,128)S(1)}, f32[16,128]{1,0:T(8,128)S(1)}) custom-call(f32[1]{0:T(128)S(6)} %copy.16.step_ref, f32[1]{0:T(128)S(6)} %copy.17.mass_ref, f32[16,32,2048]{2,1,0:T(8,128)} %old_ref.7), custom_call_target="tpu_custom_call" | custom-call | flops 12582912 | bytes 4194304 | tf_op jit(solution)/shard_map/pallas_call | solution.py:405
  8.7 0.1 multiply_reduce_fusion.2
  8.8 0.1 select_subtract_fusion.1
  9.0 0.1 collective-permute-start.1
  9.1 1.4 %collective-permute-done.1 = f32[2,16,2048]{2,1,0:T(8,128)S(1)} collective-permute-done((f32[2,16,2048]{2,1,0:T(8,128)S(1)}, f32[2,16,2048]{2,1,0:T(8,128)S(1)}, u32[]{:S(2)}, u32[]{:S(2)}) %collective-permute-start.1) | collective-permute-done | bytes 262176 | tf_op jit(solution)/shard_map/ppermute | solution.py:505
  10.6 0.1 fusion.14
  10.7 2.6 %collective-permute-start.4 = (f32[2,4,2048]{2,1,0:T(4,128)S(1)}, f32[2,4,2048]{2,1,0:T(4,128)S(1)}, u32[]{:S(2)}, u32[]{:S(2)}) collective-permute-start(f32[2,4,2048]{2,1,0:T(4,128)S(1)} %get-tuple-element.151), channel_id=1, source_target_pairs={{0,12},{2,14},{4,8},{6,10},{8,4},{10,6},{12,0},{14,2},{16,28},{18,... | collective-permute-start | bytes 196616 | tf_op jit(solution)/shard_map/ppermute | solution.py:505
  13.3 0.5 collective-permute-start.2
  13.8 0.4 collective-permute-start.3
  14.3 4.3 %shard_map.38 = (f32[16,32,2048]{2,1,0:T(8,128)}, f32[2,16,896]{2,1,0:T(8,128)S(1)}) custom-call(f32[2,16,2048]{2,1,0:T(8,128)S(1)} %pad_maximum_fusion.ready, f32[22,8,128]{2,1,0:T(8,128)S(1)} %get-tuple-element.48.table, f32[16,2048]{1,0:T(8,128)S(1)} %get-tuple-element.160.low_ref, f32[16,2048]{1,0:T(8,128)S(1)} %get-tuple-element.159.high_ref, ...), custom_call_target="tpu_custom_call" | custom-call | flops 18350080 | bytes 1835008 | tf_op jit(solution)/shard_map/pallas_call | solution.py:448
  18.7 2.7 %collective-permute-start.5 = (f32[2,4,2048]{2,1,0:T(4,128)S(1)}, f32[2,4,2048]{2,1,0:T(4,128)S(1)}, u32[]{:S(2)}, u32[]{:S(2)}) collective-permute-start(f32[2,4,2048]{2,1,0:T(4,128)S(1)} %pad_maximum_fusion.10.ready), channel_id=1, source_target_pairs={{0,16},{2,18},{4,20},{6,22},{8,24},{10,26},{12,28},{14,30},{16,0},... | collective-permute-start | bytes 196616 | tf_op jit(solution)/shard_map/ppermute | solution.py:505
  21.3 3.4 %shard_map.39 = (f32[16,32,2048]{2,1,0:T(8,128)}, f32[2,16,512]{2,1,0:T(8,128)S(1)}) custom-call(f32[2,4,2048]{2,1,0:T(4,128)S(1)} %pad_maximum_fusion.10.ready, f32[22,8,128]{2,1,0:T(8,128)S(1)} %get-tuple-element.48.table, f32[16,2048]{1,0:T(8,128)S(1)} %get-tuple-element.160.low_ref, ...), custom_call_target="tpu_custom_call", output_to_operand_aliasing={{0}: (5, {})} | custom-call | flops 10485760 | bytes 1048576 | tf_op jit(solution)/shard_map/pallas_call | solution.py:448
  24.9 0.1 add_select_fusion.29
  25.0 1.6 %collective-permute-start.7 = (f32[2,4,2048]{2,1,0:T(4,128)S(1)}, f32[2,4,2048]{2,1,0:T(4,128)S(1)}, u32[]{:S(2)}, u32[]{:S(2)}) collective-permute-start(f32[2,4,2048]{2,1,0:T(4,128)S(1)} %pad_maximum_fusion.12), channel_id=1, source_target_pairs={{0,8},{2,10},{4,12},{6,14},{8,0},{10,2},{12,4},{14,6},{16,24},{18,... | collective-permute-start | bytes 196616 | tf_op jit(solution)/shard_map/ppermute | solution.py:505
  26.6 1.4 %collective-permute-start.8 = (f32[2,4,2048]{2,1,0:T(4,128)S(1)}, f32[2,4,2048]{2,1,0:T(4,128)S(1)}, u32[]{:S(2)}, u32[]{:S(2)}) collective-permute-start(f32[2,4,2048]{2,1,0:T(4,128)S(1)} %pad_maximum_fusion.13), channel_id=1, source_target_pairs={{0,12},{2,14},{4,8},{6,10},{8,4},{10,6},{12,0},{14,2},{16,28},{18,... | collective-permute-start | bytes 196616 | tf_op jit(solution)/shard_map/ppermute | solution.py:505
  28.1 0.6 collective-permute-start.6
  28.7 3.6 %shard_map.40 = (f32[16,32,2048]{2,1,0:T(8,128)}, f32[2,16,640]{2,1,0:T(8,128)S(1)}) custom-call(f32[2,4,2048]{2,1,0:T(4,128)S(1)} %pad_maximum_fusion.14.ready, f32[22,8,128]{2,1,0:T(8,128)S(1)} %get-tuple-element.48.table, f32[16,2048]{1,0:T(8,128)S(1)} %get-tuple-element.160.low_ref, ...), custom_call_target="tpu_custom_call", output_to_operand_aliasing={{0}: (5, {})} | custom-call | flops 13107200 | bytes 1310720 | tf_op jit(solution)/shard_map/pallas_call | solution.py:448
  32.4 0.2 collective-permute-done.6
  32.8 0.1 add_select_fusion.5
  32.9 0.1 collective-permute-start.9
  33.0 1.5 %collective-permute-done.9.other_ref = f32[2,16,2048]{2,1,0:T(8,128)S(1)} collective-permute-done((f32[2,16,2048]{2,1,0:T(8,128)S(1)}, f32[2,16,2048]{2,1,0:T(8,128)S(1)}, u32[]{:S(2)}, u32[]{:S(2)}) %collective-permute-start.9) | collective-permute-done | bytes 262176 | tf_op jit(solution)/shard_map/ppermute | solution.py:505
  34.6 0.1 multiply_reduce_fusion
  34.7 1.0 %collective-permute-start.10 = (f32[2,2048]{1,0:T(2,128)S(1)}, f32[2,2048]{1,0:T(2,128)S(1)}, u32[]{:S(2)}, u32[]{:S(2)}) collective-permute-start(f32[2,2048]{1,0:T(2,128)S(1)} %multiply_reduce_fusion), channel_id=1, source_target_pairs={{0,1},{1,0},{2,3},{3,2},{4,5},{5,4},{6,7},{7,6},{8,9},{9,8},{10,11... | collective-permute-start | bytes 49160 | tf_op jit(solution)/shard_map/ppermute | solution.py:594
  35.7 3.4 %shard_map.41 = f32[2,32,2048]{2,1,0:T(8,128)S(1)} custom-call(s32[1]{0:T(128)} %bitcast.half_ref, f32[22,8,128]{2,1,0:T(8,128)S(1)} %get-tuple-element.48.table, f32[2,16,2048]{2,1,0:T(8,128)S(1)} %pad_maximum_fusion.2.own_ref, f32[2,16,2048]{2,1,0:T(8,128)S(1)} %collective-permute-done.9.other_ref, f32[16,32,2048]{2,1,0:T(8,128)} %get-tuple-element.71.old_ref), custom_call_target="tpu_custom_call" | custom-call | flops 16777216 | bytes 4194304 | tf_op jit(solution)/shard_map/pallas_call | solution.py:428
  39.2 0.1 select_subtract_fusion
  39.3 0.1 collective-permute-start.12
  39.4 1.1 %collective-permute-start.11 = (f32[16,2048]{1,0:T(8,128)S(1)}, f32[16,2048]{1,0:T(8,128)S(1)}, u32[]{:S(2)}, u32[]{:S(2)}) collective-permute-start(f32[16,2048]{1,0:T(8,128)S(1)} %broadcast_select_fusion.2), channel_id=1, source_target_pairs={{0,1},{1,0},{2,3},{3,2},{4,5},{5,4},{6,7},{7,6},{8,9},{9,8},{10,11... | collective-permute-start | bytes 393224 | tf_op jit(solution)/shard_map/ppermute | solution.py:594
  40.6 0.4 collective-permute-done.12
  41.1 2.4 %collective-permute-start.15 = (f32[2,4,2048]{2,1,0:T(4,128)S(1)}, f32[2,4,2048]{2,1,0:T(4,128)S(1)}, u32[]{:S(2)}, u32[]{:S(2)}) collective-permute-start(f32[2,4,2048]{2,1,0:T(4,128)S(1)} %get-tuple-element.143), channel_id=1, source_target_pairs={{0,12},{2,14},{4,8},{6,10},{8,4},{10,6},{12,0},{14,2},{16,28},{18,... | collective-permute-start | bytes 196616 | tf_op jit(solution)/shard_map/ppermute | solution.py:505
  43.4 0.6 collective-permute-start.13
  44.0 0.6 collective-permute-start.14
  44.6 3.4 %shard_map.42.rest_0_ = f32[16,32,896]{2,1,0:T(8,128)S(1)} custom-call(f32[2,16,2048]{2,1,0:T(8,128)S(1)} %pad_maximum_fusion.1.ready, s32[1]{0:T(128)} %bitcast.half_ref, f32[22,8,128]{2,1,0:T(8,128)S(1)} %get-tuple-element.48.table, f32[2,16,2048]{2,1,0:T(8,128)S(1)} %pad_maximum_fusion.2.own_ref, f32[2,16,2048]{2,1,0:T(8,128)S(1)} %collective-permute-done.9.other_ref, ...), custom_call_target="tpu_custom_call" | custom-call | flops 18350080 | bytes 1835008 | tf_op jit(solution)/shard_map/pallas_call | solution.py:463
  48.0 0.2 collective-permute-done.14
  48.4 2.4 %collective-permute-start.16 = (f32[2,4,2048]{2,1,0:T(4,128)S(1)}, f32[2,4,2048]{2,1,0:T(4,128)S(1)}, u32[]{:S(2)}, u32[]{:S(2)}) collective-permute-start(f32[2,4,2048]{2,1,0:T(4,128)S(1)} %pad_maximum_fusion.15.ready), channel_id=1, source_target_pairs={{0,16},{2,18},{4,20},{6,22},{8,24},{10,26},{12,28},{14,30},{16,0},... | collective-permute-start | bytes 196616 | tf_op jit(solution)/shard_map/ppermute | solution.py:505
  50.8 0.2 fusion.3.high_ref
  51.1 2.6 %shard_map.43.rest_1_ = f32[16,32,512]{2,1,0:T(8,128)S(1)} custom-call(f32[2,4,2048]{2,1,0:T(4,128)S(1)} %pad_maximum_fusion.15.ready, s32[1]{0:T(128)} %bitcast.half_ref, f32[22,8,128]{2,1,0:T(8,128)S(1)} %get-tuple-element.48.table, f32[2,16,2048]{2,1,0:T(8,128)S(1)} %pad_maximum_fusion.2.own_ref, f32[2,16,2048]{2,1,0:T(8,128)S(1)} %collective-permute-done.9.other_ref, ...), custom_call_target="tpu_custom_call" | custom-call | flops 10485760 | bytes 1048576 | tf_op jit(solution)/shard_map/pallas_call | solution.py:463
  53.8 0.1 add_select_fusion.15
  53.9 1.3 %collective-permute-start.18 = (f32[2,4,2048]{2,1,0:T(4,128)S(1)}, f32[2,4,2048]{2,1,0:T(4,128)S(1)}, u32[]{:S(2)}, u32[]{:S(2)}) collective-permute-start(f32[2,4,2048]{2,1,0:T(4,128)S(1)} %pad_maximum_fusion.17), channel_id=1, source_target_pairs={{0,8},{2,10},{4,12},{6,14},{8,0},{10,2},{12,4},{14,6},{16,24},{18,... | collective-permute-start | bytes 196616 | tf_op jit(solution)/shard_map/ppermute | solution.py:505
  55.2 1.8 %collective-permute-start.19 = (f32[2,4,2048]{2,1,0:T(4,128)S(1)}, f32[2,4,2048]{2,1,0:T(4,128)S(1)}, u32[]{:S(2)}, u32[]{:S(2)}) collective-permute-start(f32[2,4,2048]{2,1,0:T(4,128)S(1)} %pad_maximum_fusion.18), channel_id=1, source_target_pairs={{0,12},{2,14},{4,8},{6,10},{8,4},{10,6},{12,0},{14,2},{16,28},{18,... | collective-permute-start | bytes 196616 | tf_op jit(solution)/shard_map/ppermute | solution.py:505
  57.0 0.6 collective-permute-start.17
  57.7 2.8 %shard_map.44.rest_2_ = f32[16,32,640]{2,1,0:T(8,128)S(1)} custom-call(f32[2,4,2048]{2,1,0:T(4,128)S(1)} %pad_maximum_fusion.19.ready, s32[1]{0:T(128)} %bitcast.half_ref, f32[22,8,128]{2,1,0:T(8,128)S(1)} %get-tuple-element.48.table, f32[2,16,2048]{2,1,0:T(8,128)S(1)} %pad_maximum_fusion.2.own_ref, f32[2,16,2048]{2,1,0:T(8,128)S(1)} %collective-permute-done.9.other_ref, ...), custom_call_target="tpu_custom_call" | custom-call | flops 13107200 | bytes 1310720 | tf_op jit(solution)/shard_map/pallas_call | solution.py:463
  60.5 0.8 %collective-permute-done.17 = f32[2,4,2048]{2,1,0:T(4,128)S(1)} collective-permute-done((f32[2,4,2048]{2,1,0:T(4,128)S(1)}, f32[2,4,2048]{2,1,0:T(4,128)S(1)}, u32[]{:S(2)}, u32[]{:S(2)}) %collective-permute-start.17) | collective-permute-done | bytes 65568 | tf_op jit(solution)/shard_map/ppermute | solution.py:505
  61.6 0.1 collective-permute-start.20
  61.7 0.3 fusion.5.low_ref
  62.0 1.6 %shard_map.45.rest_3_ = f32[16,32,2048]{2,1,0:T(8,128)} custom-call(s32[1]{0:T(128)} %bitcast.half_ref, f32[22,8,128]{2,1,0:T(8,128)S(1)} %get-tuple-element.48.table, f32[16,2048]{1,0:T(8,128)S(1)} %fusion.5.low_ref, f32[16,2048]{1,0:T(8,128)S(1)} %fusion.3.high_ref, f32[2,16,2048]{2,1,0:T(8,128)S(1)} %pad_maximum_fusion.9.enters_ref, ...), custom_call_target="tpu_custom_call" | custom-call | flops 3145728 | bytes 2097152 | tf_op jit(solution)/shard_map/pallas_call | solution.py:482
  63.6 1.6 %shard_map.46 = f32[16,32,2048]{2,1,0:T(8,128)} custom-call(s32[1]{0:T(128)} %bitcast.half_ref, f32[22,8,128]{2,1,0:T(8,128)S(1)} %get-tuple-element.48.table, f32[16,2048]{1,0:T(8,128)S(1)} %fusion.5.low_ref, f32[16,2048]{1,0:T(8,128)S(1)} %fusion.3.high_ref, f32[2,16,2048]{2,1,0:T(8,128)S(1)} %collective-permute-done.20.enters_ref, ...), custom_call_target="tpu_custom_call", output_to_operand_aliasing={{}: (8, {})} | custom-call | flops 3145728 | bytes 2097152 | tf_op jit(solution)/shard_map/pallas_call | solution.py:482
  (67 shorter events, 1.6 us)
Async XLA Ops:
  1.4 7.3 %collective-permute-start = (f32[16,2048]{1,0:T(8,128)S(1)}, f32[16,2048]{1,0:T(8,128)S(1)}, u32[]{:S(2)}, u32[]{:S(2)}) collective-permute-start(f32[16,2048]{1,0:T(8,128)S(1)} %bitcast.79), channel_id=1, source_target_pairs={{0,1},{1,0},{2,3},{3,2},{4,5},{5,4},{6,7},{7,6},{8,9},{9,8},{10,11... | collective-permute-start | bytes 393224 | tf_op jit(solution)/shard_map/ppermute | solution.py:594
  9.0 1.6 %collective-permute-start.1 = (f32[2,16,2048]{2,1,0:T(8,128)S(1)}, f32[2,16,2048]{2,1,0:T(8,128)S(1)}, u32[]{:S(2)}, u32[]{:S(2)}) collective-permute-start(f32[2,16,2048]{2,1,0:T(8,128)S(1)} %constant_dynamic-slice_fusion.1), channel_id=1, source_target_pairs={{0,2},{2,0},{4,6},{6,4},{8,10},{10,8},{12,14},{14,12},{16,18},{18,... | collective-permute-start | bytes 786440 | tf_op jit(solution)/shard_map/ppermute | solution.py:505
  10.7 7.8 %collective-permute-start.4 = (f32[2,4,2048]{2,1,0:T(4,128)S(1)}, f32[2,4,2048]{2,1,0:T(4,128)S(1)}, u32[]{:S(2)}, u32[]{:S(2)}) collective-permute-start(f32[2,4,2048]{2,1,0:T(4,128)S(1)} %get-tuple-element.151), channel_id=1, source_target_pairs={{0,12},{2,14},{4,8},{6,10},{8,4},{10,6},{12,0},{14,2},{16,28},{18,... | collective-permute-start | bytes 196616 | tf_op jit(solution)/shard_map/ppermute | solution.py:505
  13.3 5.3 %collective-permute-start.2 = (f32[2,4,2048]{2,1,0:T(4,128)S(1)}, f32[2,4,2048]{2,1,0:T(4,128)S(1)}, u32[]{:S(2)}, u32[]{:S(2)}) collective-permute-start(f32[2,4,2048]{2,1,0:T(4,128)S(1)} %get-tuple-element.153), channel_id=1, source_target_pairs={{0,4},{2,6},{4,0},{6,2},{8,12},{10,14},{12,8},{14,10},{16,20},{18,... | collective-permute-start | bytes 196616 | tf_op jit(solution)/shard_map/ppermute | solution.py:505
  13.8 4.8 %collective-permute-start.3 = (f32[2,4,2048]{2,1,0:T(4,128)S(1)}, f32[2,4,2048]{2,1,0:T(4,128)S(1)}, u32[]{:S(2)}, u32[]{:S(2)}) collective-permute-start(f32[2,4,2048]{2,1,0:T(4,128)S(1)} %get-tuple-element.154), channel_id=1, source_target_pairs={{0,8},{2,10},{4,12},{6,14},{8,0},{10,2},{12,4},{14,6},{16,24},{18,... | collective-permute-start | bytes 196616 | tf_op jit(solution)/shard_map/ppermute | solution.py:505
  18.7 6.0 %collective-permute-start.5 = (f32[2,4,2048]{2,1,0:T(4,128)S(1)}, f32[2,4,2048]{2,1,0:T(4,128)S(1)}, u32[]{:S(2)}, u32[]{:S(2)}) collective-permute-start(f32[2,4,2048]{2,1,0:T(4,128)S(1)} %pad_maximum_fusion.10.ready), channel_id=1, source_target_pairs={{0,16},{2,18},{4,20},{6,22},{8,24},{10,26},{12,28},{14,30},{16,0},... | collective-permute-start | bytes 196616 | tf_op jit(solution)/shard_map/ppermute | solution.py:505
  25.0 7.4 %collective-permute-start.7 = (f32[2,4,2048]{2,1,0:T(4,128)S(1)}, f32[2,4,2048]{2,1,0:T(4,128)S(1)}, u32[]{:S(2)}, u32[]{:S(2)}) collective-permute-start(f32[2,4,2048]{2,1,0:T(4,128)S(1)} %pad_maximum_fusion.12), channel_id=1, source_target_pairs={{0,8},{2,10},{4,12},{6,14},{8,0},{10,2},{12,4},{14,6},{16,24},{18,... | collective-permute-start | bytes 196616 | tf_op jit(solution)/shard_map/ppermute | solution.py:505
  26.6 5.7 %collective-permute-start.8 = (f32[2,4,2048]{2,1,0:T(4,128)S(1)}, f32[2,4,2048]{2,1,0:T(4,128)S(1)}, u32[]{:S(2)}, u32[]{:S(2)}) collective-permute-start(f32[2,4,2048]{2,1,0:T(4,128)S(1)} %pad_maximum_fusion.13), channel_id=1, source_target_pairs={{0,12},{2,14},{4,8},{6,10},{8,4},{10,6},{12,0},{14,2},{16,28},{18,... | collective-permute-start | bytes 196616 | tf_op jit(solution)/shard_map/ppermute | solution.py:505
  28.1 4.5 %collective-permute-start.6 = (f32[2,4,2048]{2,1,0:T(4,128)S(1)}, f32[2,4,2048]{2,1,0:T(4,128)S(1)}, u32[]{:S(2)}, u32[]{:S(2)}) collective-permute-start(f32[2,4,2048]{2,1,0:T(4,128)S(1)} %pad_maximum_fusion.11), channel_id=1, source_target_pairs={{0,4},{2,6},{4,0},{6,2},{8,12},{10,14},{12,8},{14,10},{16,20},{18,... | collective-permute-start | bytes 196616 | tf_op jit(solution)/shard_map/ppermute | solution.py:505
  32.9 1.6 %collective-permute-start.9 = (f32[2,16,2048]{2,1,0:T(8,128)S(1)}, f32[2,16,2048]{2,1,0:T(8,128)S(1)}, u32[]{:S(2)}, u32[]{:S(2)}) collective-permute-start(f32[2,16,2048]{2,1,0:T(8,128)S(1)} %pad_maximum_fusion.5), channel_id=1, source_target_pairs={{0,2},{2,0},{4,6},{6,4},{8,10},{10,8},{12,14},{14,12},{16,18},{18,... | collective-permute-start | bytes 786440 | tf_op jit(solution)/shard_map/ppermute | solution.py:505
  34.7 4.5 %collective-permute-start.10 = (f32[2,2048]{1,0:T(2,128)S(1)}, f32[2,2048]{1,0:T(2,128)S(1)}, u32[]{:S(2)}, u32[]{:S(2)}) collective-permute-start(f32[2,2048]{1,0:T(2,128)S(1)} %multiply_reduce_fusion), channel_id=1, source_target_pairs={{0,1},{1,0},{2,3},{3,2},{4,5},{5,4},{6,7},{7,6},{8,9},{9,8},{10,11... | collective-permute-start | bytes 49160 | tf_op jit(solution)/shard_map/ppermute | solution.py:594
  39.3 1.6 %collective-permute-start.12 = (f32[2,16,2048]{2,1,0:T(8,128)S(1)}, f32[2,16,2048]{2,1,0:T(8,128)S(1)}, u32[]{:S(2)}, u32[]{:S(2)}) collective-permute-start(f32[2,16,2048]{2,1,0:T(8,128)S(1)} %constant_dynamic-slice_fusion), channel_id=1, source_target_pairs={{0,2},{2,0},{4,6},{6,4},{8,10},{10,8},{12,14},{14,12},{16,18},{18,... | collective-permute-start | bytes 786440 | tf_op jit(solution)/shard_map/ppermute | solution.py:505
  39.4 11.4 %collective-permute-start.11 = (f32[16,2048]{1,0:T(8,128)S(1)}, f32[16,2048]{1,0:T(8,128)S(1)}, u32[]{:S(2)}, u32[]{:S(2)}) collective-permute-start(f32[16,2048]{1,0:T(8,128)S(1)} %broadcast_select_fusion.2), channel_id=1, source_target_pairs={{0,1},{1,0},{2,3},{3,2},{4,5},{5,4},{6,7},{7,6},{8,9},{9,8},{10,11... | collective-permute-start | bytes 393224 | tf_op jit(solution)/shard_map/ppermute | solution.py:594
  41.1 7.0 %collective-permute-start.15 = (f32[2,4,2048]{2,1,0:T(4,128)S(1)}, f32[2,4,2048]{2,1,0:T(4,128)S(1)}, u32[]{:S(2)}, u32[]{:S(2)}) collective-permute-start(f32[2,4,2048]{2,1,0:T(4,128)S(1)} %get-tuple-element.143), channel_id=1, source_target_pairs={{0,12},{2,14},{4,8},{6,10},{8,4},{10,6},{12,0},{14,2},{16,28},{18,... | collective-permute-start | bytes 196616 | tf_op jit(solution)/shard_map/ppermute | solution.py:505
  43.4 4.6 %collective-permute-start.13 = (f32[2,4,2048]{2,1,0:T(4,128)S(1)}, f32[2,4,2048]{2,1,0:T(4,128)S(1)}, u32[]{:S(2)}, u32[]{:S(2)}) collective-permute-start(f32[2,4,2048]{2,1,0:T(4,128)S(1)} %get-tuple-element.145), channel_id=1, source_target_pairs={{0,4},{2,6},{4,0},{6,2},{8,12},{10,14},{12,8},{14,10},{16,20},{18,... | collective-permute-start | bytes 196616 | tf_op jit(solution)/shard_map/ppermute | solution.py:505
  44.0 4.3 %collective-permute-start.14 = (f32[2,4,2048]{2,1,0:T(4,128)S(1)}, f32[2,4,2048]{2,1,0:T(4,128)S(1)}, u32[]{:S(2)}, u32[]{:S(2)}) collective-permute-start(f32[2,4,2048]{2,1,0:T(4,128)S(1)} %get-tuple-element.146), channel_id=1, source_target_pairs={{0,8},{2,10},{4,12},{6,14},{8,0},{10,2},{12,4},{14,6},{16,24},{18,... | collective-permute-start | bytes 196616 | tf_op jit(solution)/shard_map/ppermute | solution.py:505
  48.4 5.3 %collective-permute-start.16 = (f32[2,4,2048]{2,1,0:T(4,128)S(1)}, f32[2,4,2048]{2,1,0:T(4,128)S(1)}, u32[]{:S(2)}, u32[]{:S(2)}) collective-permute-start(f32[2,4,2048]{2,1,0:T(4,128)S(1)} %pad_maximum_fusion.15.ready), channel_id=1, source_target_pairs={{0,16},{2,18},{4,20},{6,22},{8,24},{10,26},{12,28},{14,30},{16,0},... | collective-permute-start | bytes 196616 | tf_op jit(solution)/shard_map/ppermute | solution.py:505
  53.9 6.6 %collective-permute-start.18 = (f32[2,4,2048]{2,1,0:T(4,128)S(1)}, f32[2,4,2048]{2,1,0:T(4,128)S(1)}, u32[]{:S(2)}, u32[]{:S(2)}) collective-permute-start(f32[2,4,2048]{2,1,0:T(4,128)S(1)} %pad_maximum_fusion.17), channel_id=1, source_target_pairs={{0,8},{2,10},{4,12},{6,14},{8,0},{10,2},{12,4},{14,6},{16,24},{18,... | collective-permute-start | bytes 196616 | tf_op jit(solution)/shard_map/ppermute | solution.py:505
  55.2 5.3 %collective-permute-start.19 = (f32[2,4,2048]{2,1,0:T(4,128)S(1)}, f32[2,4,2048]{2,1,0:T(4,128)S(1)}, u32[]{:S(2)}, u32[]{:S(2)}) collective-permute-start(f32[2,4,2048]{2,1,0:T(4,128)S(1)} %pad_maximum_fusion.18), channel_id=1, source_target_pairs={{0,12},{2,14},{4,8},{6,10},{8,4},{10,6},{12,0},{14,2},{16,28},{18,... | collective-permute-start | bytes 196616 | tf_op jit(solution)/shard_map/ppermute | solution.py:505
  57.0 4.3 %collective-permute-start.17 = (f32[2,4,2048]{2,1,0:T(4,128)S(1)}, f32[2,4,2048]{2,1,0:T(4,128)S(1)}, u32[]{:S(2)}, u32[]{:S(2)}) collective-permute-start(f32[2,4,2048]{2,1,0:T(4,128)S(1)} %pad_maximum_fusion.16), channel_id=1, source_target_pairs={{0,4},{2,6},{4,0},{6,2},{8,12},{10,14},{12,8},{14,10},{16,20},{18,... | collective-permute-start | bytes 196616 | tf_op jit(solution)/shard_map/ppermute | solution.py:505
  61.6 1.9 %collective-permute-start.20 = (f32[2,16,2048]{2,1,0:T(8,128)S(1)}, f32[2,16,2048]{2,1,0:T(8,128)S(1)}, u32[]{:S(2)}, u32[]{:S(2)}) collective-permute-start(f32[2,16,2048]{2,1,0:T(8,128)S(1)} %pad_maximum_fusion.8), channel_id=1, source_target_pairs={{0,2},{2,0},{4,6},{6,4},{8,10},{10,8},{12,14},{14,12},{16,18},{18,... | collective-permute-start | bytes 786440 | tf_op jit(solution)/shard_map/ppermute | solution.py:505

commit v6 on v5

--- a/solution.py
+++ b/solution.py
@@ -319,6 +319,10 @@
         relax_tiles(table, masks, phi, None, None, psi_ref, None, part, tiles[0])
 
 
+def chunks_of(first, last):
+    return [(a, min(a + 2, last)) for a in range(first, last, 2)]
+
+
 def last_kernel(mine, pieces, half_ref, table, low_ref, high_ref, enters_ref, *rest):
     olds, (out_ref, stage, sems) = rest[: len(pieces)], rest[-3:]
     slices, planes, _ = stage.shape
@@ -327,7 +331,7 @@
     r = table[DECAY]
     row = lax.broadcasted_iota(jnp.int32, TILE, 0) + base
     writes = []
-    for n, ((first, last), old) in enumerate(zip(pieces, olds)):
+    for (first, last), old in zip(pieces, olds):
 
         def tile(j, carry):
             lanes, place = tile_at(j), tile_at(j, -first * LANES)
@@ -351,11 +355,12 @@
                     stage[t, rows_of(i), lanes] = old[t, rows, place] - (x - y) + edge(t, i)
             return carry
 
-        lax.fori_loop(first, last, tile, 0, unroll=UNROLL)
-        lanes = lanes_of(first, last)
-        there = out_ref.at[:, pl.ds(pl.multiple_of(base, ROWS), planes), lanes]
-        writes.append(pltpu.make_async_copy(stage.at[:, :, lanes], there, sems.at[n]))
-        writes[-1].start()
+        for part in chunks_of(first, last):
+            lax.fori_loop(*part, tile, 0, unroll=True)
+            lanes = lanes_of(*part)
+            there = out_ref.at[:, pl.ds(pl.multiple_of(base, ROWS), planes), lanes]
+            writes.append(pltpu.make_async_copy(stage.at[:, :, lanes], there, sems.at[len(writes)]))
+            writes[-1].start()
     for write in writes:
         write.wait()
 
@@ -487,7 +492,7 @@
         input_output_aliases={} if out is None else {len(operands) - 1: 0},
         scratch_shapes=[
             pltpu.VMEM((slices, planes // 2, width), jnp.float32),
-            pltpu.SemaphoreType.DMA((len(pieces),)),
+            pltpu.SemaphoreType.DMA((sum(len(chunks_of(*piece)) for piece in pieces),)),
         ],
         compiler_params=PARAMS,
         cost_estimate=cost((slices, planes // 2, width), 6),

time: 65.6 us -> 65.4 us (level)
  no operation moved by 1% of the time
where the time goes in v6:
time: 65.4 us; the launch traced here: 65 us
  Pallas kernels  29.2 us (45%)
  starting transfers between devices  25 us (38%)
  waiting for transfers between devices  4.58 us (7%)
  other arithmetic  2.19 us (3%)
  between operations  2.04 us (3%)
  local copies, waits for them, and re-layouts  1.51 us (2%)
    ppermute x18, starting transfers between devices, swap(): lax.ppermute(array, 'tm', [(i, i ^ offset) for i in range(self.devices)])  19.8 us
    pallas_call x3, Pallas kernels, first_relax(): pl.pallas_call(functools.partial(first_relax_kernel, tiles), in_specs=[VM...  11.2 us
    pallas_call x3, Pallas kernels, next_relax(): pl.pallas_call(functools.partial(next_relax_kernel, tiles), in_specs=[VME...  8.79 us
    ppermute x3, starting transfers between devices, exchange(): lax.ppermute(plane(row), 'space', [(i, i + 1) for i in pairs] + [(i + 1,...  5.19 us
    ppermute x18, waiting for transfers between devices, swap(): lax.ppermute(array, 'tm', [(i, i ^ offset) for i in range(self.devices)])  4.57 us
    pallas_call x1, Pallas kernels, next_sums(): pl.pallas_call(next_sums_kernel, in_specs=[SMEM] + [VMEM] * 3 + [HBM], ou...  3.37 us
    pallas_call x1, Pallas kernels, first_sums(): pl.pallas_call(functools.partial(first_sums_kernel, levels), in_specs=[SM...  2.92 us
    pallas_call x2, Pallas kernels, last_step(): pl.pallas_call(functools.partial(last_kernel, mine, pieces), in_specs=[SM...  2.88 us
  transfers between devices with their start and end apart: 21, of which 6 were waited for; matrix products, arithmetic and copies ran while one was open for 2% of the time, Pallas kernels for 43%

profile of v6, /device:TPU:0, one launch (start us, length us, event | category | flops | bytes accessed | tf_op | source)
XLA Modules:
  0.0 65.0 jit_solution(163140475190388992)
XLA Ops:
  0.0 1.3 %constant_dynamic-slice_fusion.2 = f32[16,1,2048]{2,1,0:T(1,128)S(1)} fusion(f32[16,32,2048]{2,1,0:T(8,128)} %old_ref.7, s32[]{:T(128)S(6)} %select_n.421), kind=kLoop, calls=%fused_computation.161 | loop fusion | bytes 262148 | tf_op jit(solution)/shard_map/jit(dynamic_index_in_dim)/dynamic_slice | solution.py:622
  1.4 3.0 %collective-permute-start = (f32[16,2048]{1,0:T(8,128)S(1)}, f32[16,2048]{1,0:T(8,128)S(1)}, u32[]{:S(2)}, u32[]{:S(2)}) collective-permute-start(f32[16,2048]{1,0:T(8,128)S(1)} %bitcast.79), channel_id=1, source_target_pairs={{0,1},{1,0},{2,3},{3,2},{4,5},{5,4},{6,7},{7,6},{8,9},{9,8},{10,11... | collective-permute-start | bytes 393224 | tf_op jit(solution)/shard_map/ppermute | solution.py:599
  5.7 2.9 %shard_map.37 = (f32[2,32,2048]{2,1,0:T(8,128)S(1)}, f32[22,8,128]{2,1,0:T(8,128)S(1)}, f32[4,16,2048]{2,1,0:T(8,128)S(1)}, f32[8,2048]{1,0:T(8,128)S(1)}, f32[16,128]{1,0:T(8,128)S(1)}) custom-call(f32[1]{0:T(128)S(6)} %copy.16.step_ref, f32[1]{0:T(128)S(6)} %copy.17.mass_ref, f32[16,32,2048]{2,1,0:T(8,128)} %old_ref.7), custom_call_target="tpu_custom_call" | custom-call | flops 12582912 | bytes 4194304 | tf_op jit(solution)/shard_map/pallas_call | solution.py:410
  8.7 0.1 multiply_reduce_fusion.2
  8.8 0.1 select_subtract_fusion.1
  9.0 0.1 collective-permute-start.1
  9.1 1.4 %collective-permute-done.1 = f32[2,16,2048]{2,1,0:T(8,128)S(1)} collective-permute-done((f32[2,16,2048]{2,1,0:T(8,128)S(1)}, f32[2,16,2048]{2,1,0:T(8,128)S(1)}, u32[]{:S(2)}, u32[]{:S(2)}) %collective-permute-start.1) | collective-permute-done | bytes 262176 | tf_op jit(solution)/shard_map/ppermute | solution.py:510
  10.6 0.1 fusion.14
  10.7 2.6 %collective-permute-start.4 = (f32[2,4,2048]{2,1,0:T(4,128)S(1)}, f32[2,4,2048]{2,1,0:T(4,128)S(1)}, u32[]{:S(2)}, u32[]{:S(2)}) collective-permute-start(f32[2,4,2048]{2,1,0:T(4,128)S(1)} %get-tuple-element.151), channel_id=1, source_target_pairs={{0,12},{2,14},{4,8},{6,10},{8,4},{10,6},{12,0},{14,2},{16,28},{18,... | collective-permute-start | bytes 196616 | tf_op jit(solution)/shard_map/ppermute | solution.py:510
  13.3 0.5 collective-permute-start.2
  13.8 0.4 collective-permute-start.3
  14.3 4.3 %shard_map.38 = (f32[16,32,2048]{2,1,0:T(8,128)}, f32[2,16,896]{2,1,0:T(8,128)S(1)}) custom-call(f32[2,16,2048]{2,1,0:T(8,128)S(1)} %pad_maximum_fusion.ready, f32[22,8,128]{2,1,0:T(8,128)S(1)} %get-tuple-element.48.table, f32[16,2048]{1,0:T(8,128)S(1)} %get-tuple-element.160.low_ref, f32[16,2048]{1,0:T(8,128)S(1)} %get-tuple-element.159.high_ref, ...), custom_call_target="tpu_custom_call" | custom-call | flops 18350080 | bytes 1835008 | tf_op jit(solution)/shard_map/pallas_call | solution.py:453
  18.7 2.7 %collective-permute-start.5 = (f32[2,4,2048]{2,1,0:T(4,128)S(1)}, f32[2,4,2048]{2,1,0:T(4,128)S(1)}, u32[]{:S(2)}, u32[]{:S(2)}) collective-permute-start(f32[2,4,2048]{2,1,0:T(4,128)S(1)} %pad_maximum_fusion.10.ready), channel_id=1, source_target_pairs={{0,16},{2,18},{4,20},{6,22},{8,24},{10,26},{12,28},{14,30},{16,0},... | collective-permute-start | bytes 196616 | tf_op jit(solution)/shard_map/ppermute | solution.py:510
  21.3 3.4 %shard_map.39 = (f32[16,32,2048]{2,1,0:T(8,128)}, f32[2,16,512]{2,1,0:T(8,128)S(1)}) custom-call(f32[2,4,2048]{2,1,0:T(4,128)S(1)} %pad_maximum_fusion.10.ready, f32[22,8,128]{2,1,0:T(8,128)S(1)} %get-tuple-element.48.table, f32[16,2048]{1,0:T(8,128)S(1)} %get-tuple-element.160.low_ref, ...), custom_call_target="tpu_custom_call", output_to_operand_aliasing={{0}: (5, {})} | custom-call | flops 10485760 | bytes 1048576 | tf_op jit(solution)/shard_map/pallas_call | solution.py:453
  24.9 0.1 add_select_fusion.29
  25.0 1.6 %collective-permute-start.7 = (f32[2,4,2048]{2,1,0:T(4,128)S(1)}, f32[2,4,2048]{2,1,0:T(4,128)S(1)}, u32[]{:S(2)}, u32[]{:S(2)}) collective-permute-start(f32[2,4,2048]{2,1,0:T(4,128)S(1)} %pad_maximum_fusion.12), channel_id=1, source_target_pairs={{0,8},{2,10},{4,12},{6,14},{8,0},{10,2},{12,4},{14,6},{16,24},{18,... | collective-permute-start | bytes 196616 | tf_op jit(solution)/shard_map/ppermute | solution.py:510
  26.6 1.4 %collective-permute-start.8 = (f32[2,4,2048]{2,1,0:T(4,128)S(1)}, f32[2,4,2048]{2,1,0:T(4,128)S(1)}, u32[]{:S(2)}, u32[]{:S(2)}) collective-permute-start(f32[2,4,2048]{2,1,0:T(4,128)S(1)} %pad_maximum_fusion.13), channel_id=1, source_target_pairs={{0,12},{2,14},{4,8},{6,10},{8,4},{10,6},{12,0},{14,2},{16,28},{18,... | collective-permute-start | bytes 196616 | tf_op jit(solution)/shard_map/ppermute | solution.py:510
  28.1 0.6 collective-permute-start.6
  28.7 3.6 %shard_map.40 = (f32[16,32,2048]{2,1,0:T(8,128)}, f32[2,16,640]{2,1,0:T(8,128)S(1)}) custom-call(f32[2,4,2048]{2,1,0:T(4,128)S(1)} %pad_maximum_fusion.14.ready, f32[22,8,128]{2,1,0:T(8,128)S(1)} %get-tuple-element.48.table, f32[16,2048]{1,0:T(8,128)S(1)} %get-tuple-element.160.low_ref, ...), custom_call_target="tpu_custom_call", output_to_operand_aliasing={{0}: (5, {})} | custom-call | flops 13107200 | bytes 1310720 | tf_op jit(solution)/shard_map/pallas_call | solution.py:453
  32.4 0.2 collective-permute-done.6
  32.8 0.1 add_select_fusion.5
  32.9 0.1 collective-permute-start.9
  33.0 1.5 %collective-permute-done.9.other_ref = f32[2,16,2048]{2,1,0:T(8,128)S(1)} collective-permute-done((f32[2,16,2048]{2,1,0:T(8,128)S(1)}, f32[2,16,2048]{2,1,0:T(8,128)S(1)}, u32[]{:S(2)}, u32[]{:S(2)}) %collective-permute-start.9) | collective-permute-done | bytes 262176 | tf_op jit(solution)/shard_map/ppermute | solution.py:510
  34.6 0.1 multiply_reduce_fusion
  34.7 1.0 %collective-permute-start.10 = (f32[2,2048]{1,0:T(2,128)S(1)}, f32[2,2048]{1,0:T(2,128)S(1)}, u32[]{:S(2)}, u32[]{:S(2)}) collective-permute-start(f32[2,2048]{1,0:T(2,128)S(1)} %multiply_reduce_fusion), channel_id=1, source_target_pairs={{0,1},{1,0},{2,3},{3,2},{4,5},{5,4},{6,7},{7,6},{8,9},{9,8},{10,11... | collective-permute-start | bytes 49160 | tf_op jit(solution)/shard_map/ppermute | solution.py:599
  35.7 3.4 %shard_map.41 = f32[2,32,2048]{2,1,0:T(8,128)S(1)} custom-call(s32[1]{0:T(128)} %bitcast.half_ref, f32[22,8,128]{2,1,0:T(8,128)S(1)} %get-tuple-element.48.table, f32[2,16,2048]{2,1,0:T(8,128)S(1)} %pad_maximum_fusion.2.own_ref, f32[2,16,2048]{2,1,0:T(8,128)S(1)} %collective-permute-done.9.other_ref, f32[16,32,2048]{2,1,0:T(8,128)} %get-tuple-element.71.old_ref), custom_call_target="tpu_custom_call" | custom-call | flops 16777216 | bytes 4194304 | tf_op jit(solution)/shard_map/pallas_call | solution.py:433
  39.2 0.1 select_subtract_fusion
  39.3 0.1 collective-permute-start.12
  39.4 1.1 %collective-permute-start.11 = (f32[16,2048]{1,0:T(8,128)S(1)}, f32[16,2048]{1,0:T(8,128)S(1)}, u32[]{:S(2)}, u32[]{:S(2)}) collective-permute-start(f32[16,2048]{1,0:T(8,128)S(1)} %broadcast_select_fusion.2), channel_id=1, source_target_pairs={{0,1},{1,0},{2,3},{3,2},{4,5},{5,4},{6,7},{7,6},{8,9},{9,8},{10,11... | collective-permute-start | bytes 393224 | tf_op jit(solution)/shard_map/ppermute | solution.py:599
  40.6 0.4 collective-permute-done.12
  41.1 2.4 %collective-permute-start.15 = (f32[2,4,2048]{2,1,0:T(4,128)S(1)}, f32[2,4,2048]{2,1,0:T(4,128)S(1)}, u32[]{:S(2)}, u32[]{:S(2)}) collective-permute-start(f32[2,4,2048]{2,1,0:T(4,128)S(1)} %get-tuple-element.143), channel_id=1, source_target_pairs={{0,12},{2,14},{4,8},{6,10},{8,4},{10,6},{12,0},{14,2},{16,28},{18,... | collective-permute-start | bytes 196616 | tf_op jit(solution)/shard_map/ppermute | solution.py:510
  43.4 0.6 collective-permute-start.13
  44.0 0.6 collective-permute-start.14
  44.6 3.4 %shard_map.42.rest_0_ = f32[16,32,896]{2,1,0:T(8,128)S(1)} custom-call(f32[2,16,2048]{2,1,0:T(8,128)S(1)} %pad_maximum_fusion.1.ready, s32[1]{0:T(128)} %bitcast.half_ref, f32[22,8,128]{2,1,0:T(8,128)S(1)} %get-tuple-element.48.table, f32[2,16,2048]{2,1,0:T(8,128)S(1)} %pad_maximum_fusion.2.own_ref, f32[2,16,2048]{2,1,0:T(8,128)S(1)} %collective-permute-done.9.other_ref, ...), custom_call_target="tpu_custom_call" | custom-call | flops 18350080 | bytes 1835008 | tf_op jit(solution)/shard_map/pallas_call | solution.py:468
  48.0 0.2 collective-permute-done.14
  48.4 2.4 %collective-permute-start.16 = (f32[2,4,2048]{2,1,0:T(4,128)S(1)}, f32[2,4,2048]{2,1,0:T(4,128)S(1)}, u32[]{:S(2)}, u32[]{:S(2)}) collective-permute-start(f32[2,4,2048]{2,1,0:T(4,128)S(1)} %pad_maximum_fusion.15.ready), channel_id=1, source_target_pairs={{0,16},{2,18},{4,20},{6,22},{8,24},{10,26},{12,28},{14,30},{16,0},... | collective-permute-start | bytes 196616 | tf_op jit(solution)/shard_map/ppermute | solution.py:510
  50.8 0.2 fusion.3.high_ref
  51.1 2.6 %shard_map.43.rest_1_ = f32[16,32,512]{2,1,0:T(8,128)S(1)} custom-call(f32[2,4,2048]{2,1,0:T(4,128)S(1)} %pad_maximum_fusion.15.ready, s32[1]{0:T(128)} %bitcast.half_ref, f32[22,8,128]{2,1,0:T(8,128)S(1)} %get-tuple-element.48.table, f32[2,16,2048]{2,1,0:T(8,128)S(1)} %pad_maximum_fusion.2.own_ref, f32[2,16,2048]{2,1,0:T(8,128)S(1)} %collective-permute-done.9.other_ref, ...), custom_call_target="tpu_custom_call" | custom-call | flops 10485760 | bytes 1048576 | tf_op jit(solution)/shard_map/pallas_call | solution.py:468
  53.8 0.1 add_select_fusion.15
  53.9 1.3 %collective-permute-start.18 = (f32[2,4,2048]{2,1,0:T(4,128)S(1)}, f32[2,4,2048]{2,1,0:T(4,128)S(1)}, u32[]{:S(2)}, u32[]{:S(2)}) collective-permute-start(f32[2,4,2048]{2,1,0:T(4,128)S(1)} %pad_maximum_fusion.17), channel_id=1, source_target_pairs={{0,8},{2,10},{4,12},{6,14},{8,0},{10,2},{12,4},{14,6},{16,24},{18,... | collective-permute-start | bytes 196616 | tf_op jit(solution)/shard_map/ppermute | solution.py:510
  55.2 1.8 %collective-permute-start.19 = (f32[2,4,2048]{2,1,0:T(4,128)S(1)}, f32[2,4,2048]{2,1,0:T(4,128)S(1)}, u32[]{:S(2)}, u32[]{:S(2)}) collective-permute-start(f32[2,4,2048]{2,1,0:T(4,128)S(1)} %pad_maximum_fusion.18), channel_id=1, source_target_pairs={{0,12},{2,14},{4,8},{6,10},{8,4},{10,6},{12,0},{14,2},{16,28},{18,... | collective-permute-start | bytes 196616 | tf_op jit(solution)/shard_map/ppermute | solution.py:510
  57.0 0.6 collective-permute-start.17
  57.7 2.8 %shard_map.44.rest_2_ = f32[16,32,640]{2,1,0:T(8,128)S(1)} custom-call(f32[2,4,2048]{2,1,0:T(4,128)S(1)} %pad_maximum_fusion.19.ready, s32[1]{0:T(128)} %bitcast.half_ref, f32[22,8,128]{2,1,0:T(8,128)S(1)} %get-tuple-element.48.table, f32[2,16,2048]{2,1,0:T(8,128)S(1)} %pad_maximum_fusion.2.own_ref, f32[2,16,2048]{2,1,0:T(8,128)S(1)} %collective-permute-done.9.other_ref, ...), custom_call_target="tpu_custom_call" | custom-call | flops 13107200 | bytes 1310720 | tf_op jit(solution)/shard_map/pallas_call | solution.py:468
  60.5 0.8 %collective-permute-done.17 = f32[2,4,2048]{2,1,0:T(4,128)S(1)} collective-permute-done((f32[2,4,2048]{2,1,0:T(4,128)S(1)}, f32[2,4,2048]{2,1,0:T(4,128)S(1)}, u32[]{:S(2)}, u32[]{:S(2)}) %collective-permute-start.17) | collective-permute-done | bytes 65568 | tf_op jit(solution)/shard_map/ppermute | solution.py:510
  61.6 0.1 collective-permute-start.20
  61.7 0.3 fusion.5.low_ref
  62.0 1.4 %shard_map.45.rest_3_ = f32[16,32,2048]{2,1,0:T(8,128)} custom-call(s32[1]{0:T(128)} %bitcast.half_ref, f32[22,8,128]{2,1,0:T(8,128)S(1)} %get-tuple-element.48.table, f32[16,2048]{1,0:T(8,128)S(1)} %fusion.5.low_ref, f32[16,2048]{1,0:T(8,128)S(1)} %fusion.3.high_ref, f32[2,16,2048]{2,1,0:T(8,128)S(1)} %pad_maximum_fusion.9.enters_ref, ...), custom_call_target="tpu_custom_call" | custom-call | flops 3145728 | bytes 2097152 | tf_op jit(solution)/shard_map/pallas_call | solution.py:487
  63.4 1.4 %shard_map.46 = f32[16,32,2048]{2,1,0:T(8,128)} custom-call(s32[1]{0:T(128)} %bitcast.half_ref, f32[22,8,128]{2,1,0:T(8,128)S(1)} %get-tuple-element.48.table, f32[16,2048]{1,0:T(8,128)S(1)} %fusion.5.low_ref, f32[16,2048]{1,0:T(8,128)S(1)} %fusion.3.high_ref, f32[2,16,2048]{2,1,0:T(8,128)S(1)} %collective-permute-done.20.enters_ref, ...), custom_call_target="tpu_custom_call", output_to_operand_aliasing={{}: (8, {})} | custom-call | flops 3145728 | bytes 2097152 | tf_op jit(solution)/shard_map/pallas_call | solution.py:487
  (67 shorter events, 1.6 us)
Async XLA Ops:
  1.4 7.3 %collective-permute-start = (f32[16,2048]{1,0:T(8,128)S(1)}, f32[16,2048]{1,0:T(8,128)S(1)}, u32[]{:S(2)}, u32[]{:S(2)}) collective-permute-start(f32[16,2048]{1,0:T(8,128)S(1)} %bitcast.79), channel_id=1, source_target_pairs={{0,1},{1,0},{2,3},{3,2},{4,5},{5,4},{6,7},{7,6},{8,9},{9,8},{10,11... | collective-permute-start | bytes 393224 | tf_op jit(solution)/shard_map/ppermute | solution.py:599
  9.0 1.6 %collective-permute-start.1 = (f32[2,16,2048]{2,1,0:T(8,128)S(1)}, f32[2,16,2048]{2,1,0:T(8,128)S(1)}, u32[]{:S(2)}, u32[]{:S(2)}) collective-permute-start(f32[2,16,2048]{2,1,0:T(8,128)S(1)} %constant_dynamic-slice_fusion.1), channel_id=1, source_target_pairs={{0,2},{2,0},{4,6},{6,4},{8,10},{10,8},{12,14},{14,12},{16,18},{18,... | collective-permute-start | bytes 786440 | tf_op jit(solution)/shard_map/ppermute | solution.py:510
  10.7 7.8 %collective-permute-start.4 = (f32[2,4,2048]{2,1,0:T(4,128)S(1)}, f32[2,4,2048]{2,1,0:T(4,128)S(1)}, u32[]{:S(2)}, u32[]{:S(2)}) collective-permute-start(f32[2,4,2048]{2,1,0:T(4,128)S(1)} %get-tuple-element.151), channel_id=1, source_target_pairs={{0,12},{2,14},{4,8},{6,10},{8,4},{10,6},{12,0},{14,2},{16,28},{18,... | collective-permute-start | bytes 196616 | tf_op jit(solution)/shard_map/ppermute | solution.py:510
  13.3 5.3 %collective-permute-start.2 = (f32[2,4,2048]{2,1,0:T(4,128)S(1)}, f32[2,4,2048]{2,1,0:T(4,128)S(1)}, u32[]{:S(2)}, u32[]{:S(2)}) collective-permute-start(f32[2,4,2048]{2,1,0:T(4,128)S(1)} %get-tuple-element.153), channel_id=1, source_target_pairs={{0,4},{2,6},{4,0},{6,2},{8,12},{10,14},{12,8},{14,10},{16,20},{18,... | collective-permute-start | bytes 196616 | tf_op jit(solution)/shard_map/ppermute | solution.py:510
  13.8 4.8 %collective-permute-start.3 = (f32[2,4,2048]{2,1,0:T(4,128)S(1)}, f32[2,4,2048]{2,1,0:T(4,128)S(1)}, u32[]{:S(2)}, u32[]{:S(2)}) collective-permute-start(f32[2,4,2048]{2,1,0:T(4,128)S(1)} %get-tuple-element.154), channel_id=1, source_target_pairs={{0,8},{2,10},{4,12},{6,14},{8,0},{10,2},{12,4},{14,6},{16,24},{18,... | collective-permute-start | bytes 196616 | tf_op jit(solution)/shard_map/ppermute | solution.py:510
  18.7 6.0 %collective-permute-start.5 = (f32[2,4,2048]{2,1,0:T(4,128)S(1)}, f32[2,4,2048]{2,1,0:T(4,128)S(1)}, u32[]{:S(2)}, u32[]{:S(2)}) collective-permute-start(f32[2,4,2048]{2,1,0:T(4,128)S(1)} %pad_maximum_fusion.10.ready), channel_id=1, source_target_pairs={{0,16},{2,18},{4,20},{6,22},{8,24},{10,26},{12,28},{14,30},{16,0},... | collective-permute-start | bytes 196616 | tf_op jit(solution)/shard_map/ppermute | solution.py:510
  25.0 7.4 %collective-permute-start.7 = (f32[2,4,2048]{2,1,0:T(4,128)S(1)}, f32[2,4,2048]{2,1,0:T(4,128)S(1)}, u32[]{:S(2)}, u32[]{:S(2)}) collective-permute-start(f32[2,4,2048]{2,1,0:T(4,128)S(1)} %pad_maximum_fusion.12), channel_id=1, source_target_pairs={{0,8},{2,10},{4,12},{6,14},{8,0},{10,2},{12,4},{14,6},{16,24},{18,... | collective-permute-start | bytes 196616 | tf_op jit(solution)/shard_map/ppermute | solution.py:510
  26.6 5.7 %collective-permute-start.8 = (f32[2,4,2048]{2,1,0:T(4,128)S(1)}, f32[2,4,2048]{2,1,0:T(4,128)S(1)}, u32[]{:S(2)}, u32[]{:S(2)}) collective-permute-start(f32[2,4,2048]{2,1,0:T(4,128)S(1)} %pad_maximum_fusion.13), channel_id=1, source_target_pairs={{0,12},{2,14},{4,8},{6,10},{8,4},{10,6},{12,0},{14,2},{16,28},{18,... | collective-permute-start | bytes 196616 | tf_op jit(solution)/shard_map/ppermute | solution.py:510
  28.1 4.5 %collective-permute-start.6 = (f32[2,4,2048]{2,1,0:T(4,128)S(1)}, f32[2,4,2048]{2,1,0:T(4,128)S(1)}, u32[]{:S(2)}, u32[]{:S(2)}) collective-permute-start(f32[2,4,2048]{2,1,0:T(4,128)S(1)} %pad_maximum_fusion.11), channel_id=1, source_target_pairs={{0,4},{2,6},{4,0},{6,2},{8,12},{10,14},{12,8},{14,10},{16,20},{18,... | collective-permute-start | bytes 196616 | tf_op jit(solution)/shard_map/ppermute | solution.py:510
  32.9 1.6 %collective-permute-start.9 = (f32[2,16,2048]{2,1,0:T(8,128)S(1)}, f32[2,16,2048]{2,1,0:T(8,128)S(1)}, u32[]{:S(2)}, u32[]{:S(2)}) collective-permute-start(f32[2,16,2048]{2,1,0:T(8,128)S(1)} %pad_maximum_fusion.5), channel_id=1, source_target_pairs={{0,2},{2,0},{4,6},{6,4},{8,10},{10,8},{12,14},{14,12},{16,18},{18,... | collective-permute-start | bytes 786440 | tf_op jit(solution)/shard_map/ppermute | solution.py:510
  34.7 4.5 %collective-permute-start.10 = (f32[2,2048]{1,0:T(2,128)S(1)}, f32[2,2048]{1,0:T(2,128)S(1)}, u32[]{:S(2)}, u32[]{:S(2)}) collective-permute-start(f32[2,2048]{1,0:T(2,128)S(1)} %multiply_reduce_fusion), channel_id=1, source_target_pairs={{0,1},{1,0},{2,3},{3,2},{4,5},{5,4},{6,7},{7,6},{8,9},{9,8},{10,11... | collective-permute-start | bytes 49160 | tf_op jit(solution)/shard_map/ppermute | solution.py:599
  39.3 1.6 %collective-permute-start.12 = (f32[2,16,2048]{2,1,0:T(8,128)S(1)}, f32[2,16,2048]{2,1,0:T(8,128)S(1)}, u32[]{:S(2)}, u32[]{:S(2)}) collective-permute-start(f32[2,16,2048]{2,1,0:T(8,128)S(1)} %constant_dynamic-slice_fusion), channel_id=1, source_target_pairs={{0,2},{2,0},{4,6},{6,4},{8,10},{10,8},{12,14},{14,12},{16,18},{18,... | collective-permute-start | bytes 786440 | tf_op jit(solution)/shard_map/ppermute | solution.py:510
  39.4 11.4 %collective-permute-start.11 = (f32[16,2048]{1,0:T(8,128)S(1)}, f32[16,2048]{1,0:T(8,128)S(1)}, u32[]{:S(2)}, u32[]{:S(2)}) collective-permute-start(f32[16,2048]{1,0:T(8,128)S(1)} %broadcast_select_fusion.2), channel_id=1, source_target_pairs={{0,1},{1,0},{2,3},{3,2},{4,5},{5,4},{6,7},{7,6},{8,9},{9,8},{10,11... | collective-permute-start | bytes 393224 | tf_op jit(solution)/shard_map/ppermute | solution.py:599
  41.1 7.0 %collective-permute-start.15 = (f32[2,4,2048]{2,1,0:T(4,128)S(1)}, f32[2,4,2048]{2,1,0:T(4,128)S(1)}, u32[]{:S(2)}, u32[]{:S(2)}) collective-permute-start(f32[2,4,2048]{2,1,0:T(4,128)S(1)} %get-tuple-element.143), channel_id=1, source_target_pairs={{0,12},{2,14},{4,8},{6,10},{8,4},{10,6},{12,0},{14,2},{16,28},{18,... | collective-permute-start | bytes 196616 | tf_op jit(solution)/shard_map/ppermute | solution.py:510
  43.4 4.6 %collective-permute-start.13 = (f32[2,4,2048]{2,1,0:T(4,128)S(1)}, f32[2,4,2048]{2,1,0:T(4,128)S(1)}, u32[]{:S(2)}, u32[]{:S(2)}) collective-permute-start(f32[2,4,2048]{2,1,0:T(4,128)S(1)} %get-tuple-element.145), channel_id=1, source_target_pairs={{0,4},{2,6},{4,0},{6,2},{8,12},{10,14},{12,8},{14,10},{16,20},{18,... | collective-permute-start | bytes 196616 | tf_op jit(solution)/shard_map/ppermute | solution.py:510
  44.0 4.3 %collective-permute-start.14 = (f32[2,4,2048]{2,1,0:T(4,128)S(1)}, f32[2,4,2048]{2,1,0:T(4,128)S(1)}, u32[]{:S(2)}, u32[]{:S(2)}) collective-permute-start(f32[2,4,2048]{2,1,0:T(4,128)S(1)} %get-tuple-element.146), channel_id=1, source_target_pairs={{0,8},{2,10},{4,12},{6,14},{8,0},{10,2},{12,4},{14,6},{16,24},{18,... | collective-permute-start | bytes 196616 | tf_op jit(solution)/shard_map/ppermute | solution.py:510
  48.4 5.3 %collective-permute-start.16 = (f32[2,4,2048]{2,1,0:T(4,128)S(1)}, f32[2,4,2048]{2,1,0:T(4,128)S(1)}, u32[]{:S(2)}, u32[]{:S(2)}) collective-permute-start(f32[2,4,2048]{2,1,0:T(4,128)S(1)} %pad_maximum_fusion.15.ready), channel_id=1, source_target_pairs={{0,16},{2,18},{4,20},{6,22},{8,24},{10,26},{12,28},{14,30},{16,0},... | collective-permute-start | bytes 196616 | tf_op jit(solution)/shard_map/ppermute | solution.py:510
  53.9 6.6 %collective-permute-start.18 = (f32[2,4,2048]{2,1,0:T(4,128)S(1)}, f32[2,4,2048]{2,1,0:T(4,128)S(1)}, u32[]{:S(2)}, u32[]{:S(2)}) collective-permute-start(f32[2,4,2048]{2,1,0:T(4,128)S(1)} %pad_maximum_fusion.17), channel_id=1, source_target_pairs={{0,8},{2,10},{4,12},{6,14},{8,0},{10,2},{12,4},{14,6},{16,24},{18,... | collective-permute-start | bytes 196616 | tf_op jit(solution)/shard_map/ppermute | solution.py:510
  55.2 5.3 %collective-permute-start.19 = (f32[2,4,2048]{2,1,0:T(4,128)S(1)}, f32[2,4,2048]{2,1,0:T(4,128)S(1)}, u32[]{:S(2)}, u32[]{:S(2)}) collective-permute-start(f32[2,4,2048]{2,1,0:T(4,128)S(1)} %pad_maximum_fusion.18), channel_id=1, source_target_pairs={{0,12},{2,14},{4,8},{6,10},{8,4},{10,6},{12,0},{14,2},{16,28},{18,... | collective-permute-start | bytes 196616 | tf_op jit(solution)/shard_map/ppermute | solution.py:510
  57.0 4.3 %collective-permute-start.17 = (f32[2,4,2048]{2,1,0:T(4,128)S(1)}, f32[2,4,2048]{2,1,0:T(4,128)S(1)}, u32[]{:S(2)}, u32[]{:S(2)}) collective-permute-start(f32[2,4,2048]{2,1,0:T(4,128)S(1)} %pad_maximum_fusion.16), channel_id=1, source_target_pairs={{0,4},{2,6},{4,0},{6,2},{8,12},{10,14},{12,8},{14,10},{16,20},{18,... | collective-permute-start | bytes 196616 | tf_op jit(solution)/shard_map/ppermute | solution.py:510
  61.6 1.8 %collective-permute-start.20 = (f32[2,16,2048]{2,1,0:T(8,128)S(1)}, f32[2,16,2048]{2,1,0:T(8,128)S(1)}, u32[]{:S(2)}, u32[]{:S(2)}) collective-permute-start(f32[2,16,2048]{2,1,0:T(8,128)S(1)} %pad_maximum_fusion.8), channel_id=1, source_target_pairs={{0,2},{2,0},{4,6},{6,4},{8,10},{10,8},{12,14},{14,12},{16,18},{18,... | collective-permute-start | bytes 786440 | tf_op jit(solution)/shard_map/ppermute | solution.py:510
